TPU v7x, 32 devices: a whole 2x2x4 slice. The times are simulated.
32 devices in a mesh: tgt: 4 (over y, x), src: 8 (over z, core).
Axes of the slice: x: 2, y: 2, z: 4, core: 2. Of those that a mesh axis runs over, the one named last changes fastest.
Arguments:
- positions: float32 [3, 8192], P(None, ('tgt', 'src')), may hold values from -6 to 6
- forces: float32 [3, 8192], P(None, ('tgt', 'src')), may hold values from -6 to 6
- neighbours: int32 [12, 8192], P(None, ('tgt', 'src')), may hold values from 0 to 255
- patch_owner: int32 [8192, 1], P(('tgt', 'src')), may hold values from 0 to 31; in each aligned block of 256 rows (0 to 255, 256 to 511, ...) at most 40 rows name the same one
- rest_length: float32 [6, 40960], P(None, ('tgt', 'src')), may hold values from 1 to 4
- moduli: float32 [2, 40960], P(None, ('tgt', 'src')), may hold values from 0.1 to 1
- rest_bend: float32 [3, 40960], P(None, ('tgt', 'src')), may hold values from -3 to 3
Outputs:
- final_positions: float32 [3, 8192], P(None, ('tgt', 'src'))
- final_velocity: float32 [3, 8192], P(None, ('tgt', 'src'))
Inputs may be any that keep to these rules, and one draw needn't show every extreme that they name: patch_owner[n, 0] is a flattened device index, tgt slowest; within the 256 nodes of one device no owner is named more than 40 times, and some device names some owner exactly 40 times. `neighbours`: indices into the node's own block of 256 nodes.
All inputs are finite; a program needn't handle non-finite values.
Results may differ from a plain program's by a relative error of at most 0.0003.
Values sent between devices are 32-bit elements; how exact they have to be, the bound alone decides.
No kernel may reach another device: no remote copies, remote signals or barrier semaphores. Data moves between devices by JAX's collectives and lax.ppermute only.
A program may use at most 64 MiB of HBM per device.

v0:
```python
import math

import jax
import jax.numpy as jnp
from jax import lax
from jax.sharding import PartitionSpec as P

STEPS = 3


blob_square = 0.0025
time_step = 0.5


def pick_block(length, wanted):
    return wanted if length % wanted == 0 else length


def stokes_block(target_pos, source_pos, source_force):
    delta = target_pos[:, :, None] - source_pos[:, None, :]
    radius_sq = jnp.sum(delta * delta, axis=0)
    shifted = radius_sq + blob_square
    inverse = 1.0 / (shifted * jnp.sqrt(shifted))
    along = jnp.sum(delta * source_force[:, None, :], axis=0)
    direct = (radius_sq + 2.0 * blob_square) * inverse
    tensor = along * inverse
    return jnp.sum(direct[None] * source_force[:, None, :] + tensor[None] * delta, axis=2)


def stokes_sum(target_pos, source_pos, source_force):
    count_target = target_pos.shape[1]
    count_source = source_pos.shape[1]
    target_rows = pick_block(count_target, 512)
    source_rows = pick_block(count_source, 2048)
    targets = target_pos.reshape(3, count_target // target_rows, target_rows).transpose(1, 0, 2)
    sources = source_pos.reshape(3, count_source // source_rows, source_rows).transpose(1, 0, 2)
    weights = source_force.reshape(3, count_source // source_rows, source_rows).transpose(1, 0, 2)

    def per_target(target_block):

        def add_block(running, blocks):
            return (running + stokes_block(target_block, blocks[0], blocks[1]), None)

        total, _ = lax.scan(add_block, jnp.zeros((3, target_rows), jnp.float32), (sources, weights))
        return total

    result = lax.map(per_target, targets)
    return result.transpose(1, 0, 2).reshape(3, count_target)


def cycle_weights():
    return jnp.concatenate(
        [jnp.full((6,), 2.0 / 9.0, jnp.float32), jnp.full((6,), -1.0 / 18.0, jnp.float32)]
    )


def membrane_force(edges, rest_length, moduli, rest_bend):
    nearest = edges[:, :6, :]
    stretch = jnp.sum(nearest * nearest, axis=0) / (rest_length * rest_length)
    tension = (stretch - 1.0) / (stretch + 1.0)
    surface = moduli[0] * jnp.sum((tension / rest_length)[None] * nearest, axis=1)
    bending = jnp.sum(cycle_weights()[None, :, None] * edges, axis=1) - rest_bend
    return surface + moduli[1] * bending


def evaluate(current, load):
    targets = lax.all_gather(current, "src", axis=1, tiled=True)
    partial_sum = stokes_sum(
        targets,
        lax.all_gather(current, "tgt", axis=1, tiled=True),
        lax.all_gather(load, "tgt", axis=1, tiled=True),
    )
    return lax.psum_scatter(partial_sum, "src", scatter_dimension=1, tiled=True)


def body(positions, forces, neighbours, patch_owner, rest_length, moduli, rest_bend):
    devices = lax.axis_size("tgt") * lax.axis_size("src")
    local_nodes = positions.shape[1]
    capacity = rest_length.shape[1] // devices
    owners = patch_owner[:, 0]
    onehot = (owners[:, None] == jnp.arange(devices, dtype=jnp.int32)[None, :]).astype(jnp.int32)
    before = jnp.cumsum(onehot, axis=0) - onehot
    place = owners * capacity + jnp.sum(before * onehot, axis=1)
    scale = 1.0 / math.sqrt(local_nodes * devices)
    fetched = (
        lax.all_to_all(
            rest_length.reshape(6, devices, capacity),
            ("tgt", "src"),
            split_axis=1,
            concat_axis=1,
            tiled=True,
        ),
        lax.all_to_all(
            moduli.reshape(2, devices, capacity),
            ("tgt", "src"),
            split_axis=1,
            concat_axis=1,
            tiled=True,
        ),
        lax.all_to_all(
            rest_bend.reshape(3, devices, capacity),
            ("tgt", "src"),
            split_axis=1,
            concat_axis=1,
            tiled=True,
        ),
    )
    node_length = fetched[0].reshape(6, devices * capacity)[:, place]
    node_moduli = fetched[1].reshape(2, devices * capacity)[:, place]
    node_bend = fetched[2].reshape(3, devices * capacity)[:, place]
    current = positions
    load = forces
    for update in range(STEPS):
        velocity = evaluate(current, load) * scale
        current = current + time_step * velocity
        edges = current[:, neighbours] - current[:, None, :]
        load = membrane_force(edges, node_length, node_moduli, node_bend)
    velocity = evaluate(current, load) * scale
    return (current, velocity)


def solution(mesh):
    placed = (
        P(None, ("tgt", "src")),
        P(None, ("tgt", "src")),
        P(None, ("tgt", "src")),
        P(("tgt", "src"), None),
        P(None, ("tgt", "src")),
        P(None, ("tgt", "src")),
        P(None, ("tgt", "src")),
    )
    return jax.shard_map(
        body,
        mesh=mesh,
        in_specs=placed,
        out_specs=(P(None, ("tgt", "src")), P(None, ("tgt", "src"))),
        check_vma=False,
    )
```

profile of v0, /device:TPU:1, one launch (start us, length us, event | category | flops | bytes accessed | tf_op | source)
XLA Modules:
  0.0 371.6 jit_solution(3022078826127090702)
XLA Ops:
  7.2 15.7 %all_gather.36 = f32[3,2048]{1,0:T(4,128)S(1)} all-gather(f32[3,256]{1,0:T(4,128)} %param.15), channel_id=1, replica_groups=mesh['tgt'=4,'src'=8] {'src'}, dimensions={1}, use_global_device_ids=true | all-gather | bytes 27648 | tf_op jit(solution)/shard_map/all_gather | solution.py:67
  22.9 6.5 %all_gather.37 = f32[3,1024]{1,0:T(4,128)S(1)} all-gather(f32[3,256]{1,0:T(4,128)} %param.15), channel_id=1, replica_groups=mesh['tgt'=4,'src'=8] {'tgt'}, dimensions={1}, use_global_device_ids=true | all-gather | bytes 15360 | tf_op jit(solution)/shard_map/all_gather | solution.py:70
  29.4 5.7 %all_gather.38 = f32[3,1024]{1,0:T(4,128)S(1)} all-gather(f32[3,256]{1,0:T(4,128)} %param.16), channel_id=1, replica_groups=mesh['tgt'=4,'src'=8] {'tgt'}, dimensions={1}, use_global_device_ids=true | all-gather | bytes 15360 | tf_op jit(solution)/shard_map/all_gather | solution.py:71
  35.1 15.0 %while.36 = (s32[]{:T(128)}, f32[4,3,512]{2,1,0:T(4,128)S(1)}, f32[4,3,512]{2,1,0:T(4,128)S(1)}, f32[1,3,1024]{2,1,0:T(4,128)S(1)}, f32[1,3,1024]{2,1,0:T(4,128)S(1)}, /*index=5*/s32[]{:T(128)}) while((s32[]{:T(128)}, f32[4,3,512]{2,1,0:T(4,128)S(1)}, f32[4,3,512]{2,1,0:T(4,128)S(1)}, f32[1,3,1024]{2,1,0:T(4,128)S(1)}, ...), condition=%wide.region_4.5_spmd, body=%wide.region_0.4_spmd.sunk | while | flops 17824256 | bytes 16873548 | solution.py:47
  35.1 1.1 fusion.45
  37.3 1.6 fusion.46
  38.9 1.1 fusion.45
  41.0 1.6 fusion.46
  42.7 1.1 fusion.45
  44.8 1.6 fusion.46
  46.4 1.1 fusion.45
  48.5 1.6 fusion.46
  50.2 1.4 copy.154
  52.3 8.6 %all-to-all-start = ((f32[2,32,40]{2,0,1:T(2,128)}), f32[2,32,40]{2,0,1:T(2,128)S(1)}, u32[]{:S(2)}, u32[]{:S(2)}) async-start(f32[2,32,40]{2,0,1:T(2,128)} %copy.157), calls=%async_computation.1 | async-start | bytes 65536 | tf_op jit(solution)/shard_map/all_to_all | solution.py:93
  63.8 4.3 %all-to-all-done = f32[2,32,40]{2,0,1:T(2,128)S(1)} async-done(((f32[2,32,40]{2,0,1:T(2,128)}), f32[2,32,40]{2,0,1:T(2,128)S(1)}, u32[]{:S(2)}, u32[]{:S(2)}) %all-to-all-start) | async-done | bytes 10272 | tf_op jit(solution)/shard_map/all_to_all | solution.py:93
  68.1 2.5 all-to-all-start.2
  71.9 7.0 %all-to-all-done.2 = f32[3,32,40]{2,0,1:T(4,128)S(1)} async-done(((f32[3,32,40]{2,0,1:T(4,128)}), f32[3,32,40]{2,0,1:T(4,128)S(1)}, u32[]{:S(2)}, u32[]{:S(2)}) %all-to-all-start.2) | async-done | bytes 15392 | tf_op jit(solution)/shard_map/all_to_all | solution.py:100
  78.8 2.4 all-to-all-start.1
  82.4 3.1 reduce-scatter.7.cloned.1.call-done
  86.4 8.1 %gather_fusion.1 = f32[3072,3]{1,0:T(8,128)S(1)} fusion(f32[3,256]{0,1:T(8,128)S(1)} %multiply_add_fusion.2, s32[3072]{0:T(1024)S(1)} %broadcast_clamp_fusion), kind=kCustom, calls=%fused_computation.1 | custom fusion | bytes 86016 | tf_op jit(solution)/shard_map/gather | solution.py:116
  95.1 20.3 %all_gather.39 = f32[3,2048]{0,1:T(8,128)S(1)} all-gather(f32[3,256]{0,1:T(8,128)S(1)} %multiply_add_fusion.2), channel_id=1, replica_groups=mesh['tgt'=4,'src'=8] {'src'}, dimensions={1}, use_global_device_ids=true | all-gather | bytes 27648 | tf_op jit(solution)/shard_map/all_gather | solution.py:67
  115.8 9.2 %all_gather.40 = f32[3,1024]{0,1:T(8,128)S(1)} all-gather(f32[3,256]{0,1:T(8,128)S(1)} %multiply_add_fusion.2), channel_id=1, replica_groups=mesh['tgt'=4,'src'=8] {'tgt'}, dimensions={1}, use_global_device_ids=true | all-gather | bytes 15360 | tf_op jit(solution)/shard_map/all_gather | solution.py:70
  128.1 5.9 %all_gather.41 = f32[3,1024]{1,0:T(4,128)S(1)} all-gather(f32[3,256]{1,0:T(4,128)S(1)} %fusion.34), channel_id=1, replica_groups=mesh['tgt'=4,'src'=8] {'tgt'}, dimensions={1}, use_global_device_ids=true | all-gather | bytes 15360 | tf_op jit(solution)/shard_map/all_gather | solution.py:71
  134.1 15.1 %while.37 = (s32[]{:T(128)}, f32[4,3,512]{2,1,0:T(4,128)S(1)}, f32[4,3,512]{2,1,0:T(4,128)S(1)}, f32[1,3,1024]{2,1,0:T(4,128)S(1)}, f32[1,3,1024]{2,1,0:T(4,128)S(1)}, /*index=5*/s32[]{:T(128)}) while((s32[]{:T(128)}, f32[4,3,512]{2,1,0:T(4,128)S(1)}, f32[4,3,512]{2,1,0:T(4,128)S(1)}, f32[1,3,1024]{2,1,0:T(4,128)S(1)}, ...), condition=%wide.region_16.17_spmd, body=%wide.region_12.16_spmd.sunk | while | flops 17824256 | bytes 16873548 | solution.py:47
  134.1 1.1 fusion.47
  136.2 1.6 fusion.48
  137.8 1.1 fusion.47
  140.0 1.6 fusion.48
  141.6 1.1 fusion.47
  143.7 1.6 fusion.48
  145.4 1.1 fusion.47
  147.5 1.6 fusion.48
  149.1 1.4 copy.169
  150.7 29.3 %reduce-scatter.9.cloned.1.call-done = f32[3,256]{0,1:T(8,128)} async-done(((f32[3,2048]{0,1:T(8,128)}), f32[3,256]{0,1:T(8,128)}) %reduce-scatter.9.cloned.1.call-update) | async-done | bytes 3088 | tf_op jit(solution)/shard_map/reduce_scatter | solution.py:73
  180.9 8.1 %gather_fusion.4 = f32[3072,3]{1,0:T(8,128)S(1)} fusion(f32[3,256]{0,1:T(8,128)S(1)} %multiply_add_fusion.1, s32[3072]{0:T(1024)S(1)} %broadcast_clamp_fusion), kind=kCustom, calls=%fused_computation.4 | custom fusion | bytes 86016 | tf_op jit(solution)/shard_map/gather | solution.py:116
  189.1 20.4 %all_gather.42 = f32[3,2048]{0,1:T(8,128)S(1)} all-gather(f32[3,256]{0,1:T(8,128)S(1)} %multiply_add_fusion.1), channel_id=1, replica_groups=mesh['tgt'=4,'src'=8] {'src'}, dimensions={1}, use_global_device_ids=true | all-gather | bytes 27648 | tf_op jit(solution)/shard_map/all_gather | solution.py:67
  209.4 8.4 %all_gather.43 = f32[3,1024]{0,1:T(8,128)S(1)} all-gather(f32[3,256]{0,1:T(8,128)S(1)} %multiply_add_fusion.1), channel_id=1, replica_groups=mesh['tgt'=4,'src'=8] {'tgt'}, dimensions={1}, use_global_device_ids=true | all-gather | bytes 15360 | tf_op jit(solution)/shard_map/all_gather | solution.py:70
  218.9 5.7 %all_gather.44 = f32[3,1024]{1,0:T(4,128)S(1)} all-gather(f32[3,256]{1,0:T(4,128)S(1)} %fusion.36), channel_id=1, replica_groups=mesh['tgt'=4,'src'=8] {'tgt'}, dimensions={1}, use_global_device_ids=true | all-gather | bytes 15360 | tf_op jit(solution)/shard_map/all_gather | solution.py:71
  225.1 14.9 %while.38 = (s32[]{:T(128)}, f32[4,3,512]{2,1,0:T(4,128)S(1)}, f32[4,3,512]{2,1,0:T(4,128)S(1)}, f32[1,3,1024]{2,1,0:T(4,128)S(1)}, f32[1,3,1024]{2,1,0:T(4,128)S(1)}, /*index=5*/s32[]{:T(128)}) while((s32[]{:T(128)}, f32[4,3,512]{2,1,0:T(4,128)S(1)}, f32[4,3,512]{2,1,0:T(4,128)S(1)}, f32[1,3,1024]{2,1,0:T(4,128)S(1)}, ...), condition=%wide.region_25.26_spmd, body=%wide.region_21.25_spmd.sunk | while | flops 17824256 | bytes 16873548 | solution.py:47
  225.1 1.1 fusion.49
  227.3 1.6 fusion.50
  228.9 1.1 fusion.49
  231.0 1.6 fusion.50
  232.6 1.1 fusion.49
  234.7 1.6 fusion.50
  236.3 1.1 fusion.49
  238.5 1.6 fusion.50
  240.1 1.4 copy.174
  241.5 30.0 %reduce-scatter.11.cloned.1.call-done = f32[3,256]{0,1:T(8,128)} async-done(((f32[3,2048]{0,1:T(8,128)}), f32[3,256]{0,1:T(8,128)}) %reduce-scatter.11.cloned.1.call-update) | async-done | bytes 3088 | tf_op jit(solution)/shard_map/reduce_scatter | solution.py:73
  272.5 8.1 %gather_fusion.5 = f32[3072,3]{1,0:T(8,128)S(1)} fusion(f32[3,256]{0,1:T(8,128)S(1)} %multiply_add_fusion, s32[3072]{0:T(1024)S(1)} %broadcast_clamp_fusion), kind=kCustom, calls=%fused_computation.5 | custom fusion | bytes 86016 | tf_op jit(solution)/shard_map/gather | solution.py:116
  280.6 20.2 %all_gather.45 = f32[3,2048]{0,1:T(8,128)S(1)} all-gather(f32[3,256]{0,1:T(8,128)S(1)} %multiply_add_fusion), channel_id=1, replica_groups=mesh['tgt'=4,'src'=8] {'src'}, dimensions={1}, use_global_device_ids=true | all-gather | bytes 27648 | tf_op jit(solution)/shard_map/all_gather | solution.py:67
  300.8 9.2 %all_gather.46 = f32[3,1024]{0,1:T(8,128)S(1)} all-gather(f32[3,256]{0,1:T(8,128)S(1)} %multiply_add_fusion), channel_id=1, replica_groups=mesh['tgt'=4,'src'=8] {'tgt'}, dimensions={1}, use_global_device_ids=true | all-gather | bytes 15360 | tf_op jit(solution)/shard_map/all_gather | solution.py:70
  311.0 5.5 %all_gather.47 = f32[3,1024]{1,0:T(4,128)S(1)} all-gather(f32[3,256]{1,0:T(4,128)S(1)} %fusion.32), channel_id=1, replica_groups=mesh['tgt'=4,'src'=8] {'tgt'}, dimensions={1}, use_global_device_ids=true | all-gather | bytes 15360 | tf_op jit(solution)/shard_map/all_gather | solution.py:71
  317.1 15.1 %while.39 = (s32[]{:T(128)}, f32[4,3,512]{2,1,0:T(4,128)S(1)}, f32[4,3,512]{2,1,0:T(4,128)S(1)}, f32[1,3,1024]{2,1,0:T(4,128)S(1)}, f32[1,3,1024]{2,1,0:T(4,128)S(1)}, /*index=5*/s32[]{:T(128)}) while((s32[]{:T(128)}, f32[4,3,512]{2,1,0:T(4,128)S(1)}, f32[4,3,512]{2,1,0:T(4,128)S(1)}, f32[1,3,1024]{2,1,0:T(4,128)S(1)}, ...), condition=%wide.region_34.35_spmd, body=%wide.region_30.34_spmd.sunk | while | flops 17824256 | bytes 16873548 | solution.py:47
  317.1 1.1 fusion.51
  319.2 1.6 fusion.52
  320.9 1.1 fusion.51
  323.0 1.6 fusion.52
  324.6 1.1 fusion.51
  326.8 1.6 fusion.52
  328.4 1.1 fusion.51
  330.5 1.6 fusion.52
  332.1 1.4 copy.181
  334.2 29.2 %reduce-scatter.13.cloned.1.call-done = f32[256,3]{1,0:T(8,128)} async-done(((f32[2048,3]{1,0:T(8,128)}), f32[256,3]{1,0:T(8,128)}) %reduce-scatter.13.cloned.1.call-update) | async-done | bytes 3088
  (139 shorter events, 35.1 us)
Async XLA Ops:
  7.2 78.3 %reduce-scatter.7.cloned.1.call-start = ((), (), s32[]{:S(2)}) async-start(), calls=%async_computation.7 | async-start | bytes 1179648 | tf_op jit(solution)/shard_map/reduce_scatter | solution.py:73
  50.1 1.5 copy-start.4
  50.1 10.8 %copy-start.3 = (s32[12,256]{1,0:T(8,128)S(1)}, s32[12,256]{1,0:T(8,128)}, u32[]{:S(2)}) copy-start(s32[12,256]{1,0:T(8,128)} %param.17) | copy-start | bytes 36868
  50.2 10.8 %copy-start.5 = (s32[256,1]{0,1:T(1,128)S(1)}, s32[256,1]{0,1:T(1,128)}, u32[]{:S(2)}) copy-start(s32[256,1]{0,1:T(1,128)} %param.18) | copy-start | bytes 3076
  50.2 11.8 %copy-start.1 = (f32[3,256]{1,0:T(4,128)S(1)}, f32[3,256]{1,0:T(4,128)}, u32[]{:S(2)}) copy-start(f32[3,256]{1,0:T(4,128)} %param.15) | copy-start | bytes 9220
  50.2 12.0 %copy-start = (f32[6,1280]{1,0:T(8,128)S(1)}, f32[6,1280]{1,0:T(8,128)}, u32[]{:S(2)}) copy-start(f32[6,1280]{1,0:T(8,128)} %param.19) | copy-start | bytes 92164
  50.2 12.9 %copy-start.2 = (f32[3,1280]{1,0:T(4,128)S(1)}, f32[3,1280]{1,0:T(4,128)}, u32[]{:S(2)}) copy-start(f32[3,1280]{1,0:T(4,128)} %param.21) | copy-start | bytes 46084
  51.7 42.8 %copy-start.6 = (f32[12]{0:T(128)S(1)}, f32[12]{0:T(128)}, u32[]{:S(2)}) copy-start(f32[12]{0:T(128)} %constant.142.clone.1) | copy-start | bytes 148
  52.3 15.7 %all-to-all-start = ((f32[2,32,40]{2,0,1:T(2,128)}), f32[2,32,40]{2,0,1:T(2,128)S(1)}, u32[]{:S(2)}, u32[]{:S(2)}) async-start(f32[2,32,40]{2,0,1:T(2,128)} %copy.157), calls=%async_computation.1 | async-start | bytes 65536 | tf_op jit(solution)/shard_map/all_to_all | solution.py:93
  68.1 10.8 %all-to-all-start.2 = ((f32[3,32,40]{2,0,1:T(4,128)}), f32[3,32,40]{2,0,1:T(4,128)S(1)}, u32[]{:S(2)}, u32[]{:S(2)}) async-start(f32[3,32,40]{2,0,1:T(4,128)} %copy.164), calls=%async_computation.3 | async-start | bytes 131072 | tf_op jit(solution)/shard_map/all_to_all | solution.py:100
  78.8 46.3 %all-to-all-start.1 = ((f32[32,1,240]{2,1,0:T(1,128)}), f32[32,1,240]{2,1,0:T(1,128)S(1)}, u32[]{:S(2)}, u32[]{:S(2)}) async-start(f32[32,1,240]{2,1,0:T(1,128)} %reshape.244), calls=%async_computation.2 | async-start | bytes 65536 | tf_op jit(solution)/shard_map/all_to_all | solution.py:86
  81.2 98.8 %reduce-scatter.9.cloned.1.call-start = ((), (), s32[]{:S(2)}) async-start(), calls=%async_computation.8 | async-start | bytes 1179648 | tf_op jit(solution)/shard_map/reduce_scatter | solution.py:73
  150.5 121.0 %reduce-scatter.11.cloned.1.call-start = ((), (), s32[]{:S(2)}) async-start(), calls=%async_computation.9 | async-start | bytes 1179648 | tf_op jit(solution)/shard_map/reduce_scatter | solution.py:73
  241.4 122.0 %reduce-scatter.13.cloned.1.call-start = ((), (), s32[]{:S(2)}) async-start(), calls=%async_computation.10 | async-start | bytes 1179648
Sparse Core Ops, SparseCore 0:
  51.7 33.6 reduce-scatter.6
  150.6 29.3 reduce-scatter.8
  241.6 29.9 reduce-scatter.10
  333.6 29.7 reduce-scatter.12
where the time goes:
time: 376 us; the launch traced here: 372 us
  blocking collectives  133 us (35%)
  waiting for transfers between devices  103 us (27%)
  other arithmetic  66.5 us (18%)
  local copies, waits for them, and re-layouts  40.7 us (11%)
  between operations  14.2 us (4%)
  starting transfers between devices  13.9 us (4%)
    all_gather x4, blocking collectives, evaluate(): targets = lax.all_gather(current, 'src', axis=1, tiled=True)  76.6 us
    reduce_scatter x3, waiting for transfers between devices, evaluate(): return lax.psum_scatter(partial_sum, 'src', scatter_dimension=1, tiled=True)  62.4 us
    all_gather x4, blocking collectives, evaluate(): lax.all_gather(current, 'tgt', axis=1, tiled=True)  33.3 us
    unnamed x5, waiting for transfers between devices  29.3 us
    reduce_sum x16, other arithmetic, stokes_block(): jnp.sum(direct[None] * source_force[:, None, :] + tensor[None] * delta, a...  25.3 us
    gather x3, local copies, waits for them, and re-layouts, body(): edges = current[:, neighbours] - current[:, None, :]  24.4 us
    all_gather x4, blocking collectives, evaluate(): lax.all_gather(load, 'tgt', axis=1, tiled=True)  22.8 us
    reduce_sum x16, other arithmetic, stokes_block(): radius_sq = jnp.sum(delta * delta, axis=0)  17.4 us
  transfers between devices with their start and end apart: 7, of which 6 were waited for; matrix products, arithmetic and copies ran while one was open for 4% of the time, Pallas kernels for 0%

commit v1 on v0

v1 whole, which is shorter than its diff:
```python
import functools
import math

import jax
import jax.numpy as jnp
from jax import lax
from jax.experimental import pallas as pl
from jax.experimental.pallas import tpu as pltpu
from jax.sharding import PartitionSpec as P

STEPS = 3
LANES = 128
ROWS = 8
TARGET_ROWS = 32
PARAMS = 16

blob_square = 0.0025
time_step = 0.5

AXES = ("tgt", "src")
VMEM = pl.BlockSpec(memory_space=pltpu.VMEM)
GRANT = pltpu.CompilerParams(vmem_limit_bytes=32 * 1024 * 1024)


def pack_kernel(length_ref, moduli_ref, bend_ref, out_ref):
    devices, _, capacity = out_ref.shape
    for device in range(devices):
        cut = slice(device * capacity, (device + 1) * capacity)
        out_ref[device, 0:6, :] = length_ref[:, cut]
        out_ref[device, 6:8, :] = moduli_ref[:, cut]
        out_ref[device, 8:11, :] = bend_ref[:, cut]
        out_ref[device, 11:PARAMS, :] = jnp.zeros((PARAMS - 11, capacity), jnp.float32)


def pack_slots(rest_length, moduli, rest_bend, devices):
    capacity = rest_length.shape[1] // devices
    return pl.pallas_call(
        pack_kernel,
        out_shape=jax.ShapeDtypeStruct((devices, PARAMS, capacity), jnp.float32),
        in_specs=[VMEM] * 3,
        out_specs=VMEM,
        compiler_params=GRANT,
    )(rest_length, moduli, rest_bend)


def pick_kernel(slots_ref, owner_ref, out_ref):
    devices, _, capacity = slots_ref.shape
    nodes = owner_ref.shape[1]
    owner = owner_ref[...]
    across = jnp.broadcast_to(owner, (nodes, nodes))
    down = across.T
    earlier = lax.broadcasted_iota(jnp.int32, (nodes, nodes), 0) < lax.broadcasted_iota(
        jnp.int32, (nodes, nodes), 1
    )
    rank = jnp.sum(jnp.where((across == down) & earlier, 1, 0), axis=0, keepdims=True)
    for at in range(0, nodes, LANES):
        place = jnp.broadcast_to(rank[:, at : at + LANES], (ROWS, LANES))
        named = jnp.broadcast_to(owner[:, at : at + LANES], (ROWS, LANES))
        for row in range(0, PARAMS, ROWS):

            def choose(device, chosen):
                block = slots_ref[device, row : row + ROWS, :]
                block = jnp.concatenate([block, jnp.zeros((ROWS, LANES - capacity), jnp.float32)], axis=1)
                taken = jnp.take_along_axis(block, place, axis=1, mode="promise_in_bounds")
                return jnp.where(named == device, taken, chosen)

            out_ref[row : row + ROWS, at : at + LANES] = lax.fori_loop(
                0, devices, choose, jnp.zeros((ROWS, LANES), jnp.float32), unroll=4
            )


def pick_slots(slots, owner):
    return pl.pallas_call(
        pick_kernel,
        out_shape=jax.ShapeDtypeStruct((PARAMS, owner.shape[1]), jnp.float32),
        in_specs=[VMEM] * 2,
        out_specs=VMEM,
        compiler_params=GRANT,
    )(slots, owner)


def pair_sums(all_ref, own_ref, column_ref, sum_ref):
    devices, _, nodes = all_ref.shape
    for c in range(3):
        for at in range(0, nodes, LANES):
            row = own_ref[c : c + 1, at : at + LANES]
            column_ref[c, at : at + LANES, :] = jnp.broadcast_to(row, (LANES, LANES)).T

    def per_target(block, _):
        rows = pl.ds(pl.multiple_of(block * TARGET_ROWS, TARGET_ROWS), TARGET_ROWS)
        target = [column_ref[c, rows, :] for c in range(3)]

        def per_source(device, totals):
            for at in range(0, nodes, LANES):
                x = [all_ref[device, c : c + 1, at : at + LANES] for c in range(3)]
                f = [all_ref[device, 3 + c : 4 + c, at : at + LANES] for c in range(3)]
                d = [target[c] - x[c] for c in range(3)]
                shifted = d[0] * d[0] + (d[1] * d[1] + (d[2] * d[2] + blob_square))
                r = lax.rsqrt(shifted)
                cube = r * (r * r)
                direct = r + blob_square * cube
                along = (d[0] * f[0] + d[1] * f[1] + d[2] * f[2]) * cube
                totals = tuple(totals[c] + (direct * f[c] + along * d[c]) for c in range(3))
            return totals

        zero = jnp.zeros((TARGET_ROWS, LANES), jnp.float32)
        totals = lax.fori_loop(0, devices, per_source, (zero, zero, zero), unroll=2)
        for c in range(3):
            sum_ref[c, rows, :] = totals[c]
        return 0

    lax.fori_loop(0, nodes // TARGET_ROWS, per_target, 0)
    scale = 1.0 / math.sqrt(devices * nodes)
    velocity = []
    for c in range(3):
        parts = [
            jnp.sum(sum_ref[c, at : at + LANES, :].T, axis=0, keepdims=True)
            for at in range(0, nodes, LANES)
        ]
        velocity.append(jnp.concatenate(parts, axis=1) * scale)
    return velocity


def membrane(x, neighbours_ref, params_ref):
    nodes = x[0].shape[1]
    force = [[], [], []]
    for at in range(0, nodes, LANES):
        here = slice(at, at + LANES)
        points = [neighbours_ref[0:6, here], neighbours_ref[6:12, here]]
        edges = []
        for index in points:
            local = index & (LANES - 1)
            group = index // LANES
            component = []
            for c in range(3):
                found = jnp.zeros(index.shape, jnp.float32)
                for part in range(nodes // LANES):
                    source = jnp.broadcast_to(x[c][:, part * LANES : (part + 1) * LANES], index.shape)
                    taken = jnp.take_along_axis(source, local, axis=1, mode="promise_in_bounds")
                    found = jnp.where(group == part, taken, found)
                component.append(found - x[c][:, here])
            edges.append(component)
        near, far = edges
        length = params_ref[0:6, here]
        stretch = (near[0] * near[0] + near[1] * near[1] + near[2] * near[2]) / (length * length)
        tension = (stretch - 1.0) / (stretch + 1.0) / length
        for c in range(3):
            surface = jnp.sum(tension * near[c], axis=0, keepdims=True)
            bending = jnp.sum((2.0 / 9.0) * near[c] - (1.0 / 18.0) * far[c], axis=0, keepdims=True)
            bending = bending - params_ref[8 + c : 9 + c, here]
            force[c].append(params_ref[6:7, here] * surface + params_ref[7:8, here] * bending)
    return [jnp.concatenate(parts, axis=1) for parts in force]


def step_kernel(all_ref, own_ref, neighbours_ref, params_ref, out_ref, column_ref, sum_ref):
    velocity = pair_sums(all_ref, own_ref, column_ref, sum_ref)
    x = [own_ref[c : c + 1, :] + time_step * velocity[c] for c in range(3)]
    force = membrane(x, neighbours_ref, params_ref)
    for c in range(3):
        out_ref[c : c + 1, :] = x[c]
        out_ref[3 + c : 4 + c, :] = force[c]
    out_ref[6:ROWS, :] = jnp.zeros((ROWS - 6, x[0].shape[1]), jnp.float32)


def last_kernel(all_ref, own_ref, position_ref, velocity_ref, column_ref, sum_ref):
    velocity = pair_sums(all_ref, own_ref, column_ref, sum_ref)
    position_ref[...] = own_ref[0:3, :]
    for c in range(3):
        velocity_ref[c : c + 1, :] = velocity[c]


def scratch(nodes):
    return [pltpu.VMEM((3, nodes, LANES), jnp.float32), pltpu.VMEM((3, nodes, LANES), jnp.float32)]


def gather_state(state):
    return lax.all_gather(state, AXES, axis=0)


def body(positions, forces, neighbours, patch_owner, rest_length, moduli, rest_bend):
    devices = lax.axis_size("tgt") * lax.axis_size("src")
    nodes = positions.shape[1]
    slots = lax.all_to_all(
        pack_slots(rest_length, moduli, rest_bend, devices), AXES, split_axis=0, concat_axis=0, tiled=True
    )
    state = jnp.concatenate([positions, forces, jnp.zeros((ROWS - 6, nodes), jnp.float32)], axis=0)
    params = pick_slots(slots, patch_owner.reshape(1, nodes))
    for _ in range(STEPS):
        state = pl.pallas_call(
            step_kernel,
            out_shape=jax.ShapeDtypeStruct((ROWS, nodes), jnp.float32),
            in_specs=[VMEM] * 4,
            out_specs=VMEM,
            scratch_shapes=scratch(nodes),
            compiler_params=GRANT,
        )(gather_state(state), state, neighbours, params)
    return pl.pallas_call(
        last_kernel,
        out_shape=(jax.ShapeDtypeStruct((3, nodes), jnp.float32),) * 2,
        in_specs=[VMEM] * 2,
        out_specs=(VMEM,) * 2,
        scratch_shapes=scratch(nodes),
        compiler_params=GRANT,
    )(gather_state(state), state)


def solution(mesh):
    placed = (
        P(None, AXES),
        P(None, AXES),
        P(None, AXES),
        P(AXES, None),
        P(None, AXES),
        P(None, AXES),
        P(None, AXES),
    )
    return jax.shard_map(
        body,
        mesh=mesh,
        in_specs=placed,
        out_specs=(P(None, AXES), P(None, AXES)),
        check_vma=False,
    )
```

time: 376 us -> 215 us (0.57)
  waiting for transfers between devices: 103 us -> 0.01 us
  other arithmetic: 66.5 us -> 0.91 us
  Pallas kernels: 0 us -> 43.6 us
  local copies, waits for them, and re-layouts: 40.7 us -> 4.53 us
  blocking collectives: 133 us -> 157 us
  between operations: 14.2 us -> 0.72 us
  starting transfers between devices: 13.9 us -> 7.1 us
    reduce_scatter x3 -> x0, waiting for transfers between devices: 62.4 us -> none  [evaluate(): return lax.psum_scatter(partial_sum, 'src', scatter_dimension=1, tiled=True)]
    reduce_sum x42 -> x0, other arithmetic: 45.2 us -> none  [the longest x16 25.3 us: stokes_block(): jnp.sum(direct[None] * source_force[:, None, :] + tensor[None] * delta, a...]
    pallas_call x0 -> x6, Pallas kernels: none -> 43.6 us  [the longest x3 30.4 us: body(): pl.pallas_call(step_kernel, out_shape=jax.ShapeDtypeStruct((ROWS, nodes),...]
    unnamed x5 -> x0, waiting for transfers between devices: 29.3 us -> none
    gather x8 -> x0, local copies, waits for them, and re-layouts: 26.7 us -> none  [the longest x3 24.4 us: body(): edges = current[:, neighbours] - current[:, None, :]]
    all_gather x12 -> x4, blocking collectives: 133 us -> 157 us  [gather_state(): return lax.all_gather(state, AXES, axis=0)]
    mul x17 -> x0, other arithmetic: 17 us -> none  [the longest x16 16.4 us: stokes_block(): direct = (radius_sq + 2.0 * blob_square) * inverse]
    all_to_all x3 -> x1, waiting for transfers between devices: 11.2 us -> 0.01 us  [body(): lax.all_to_all(pack_slots(rest_length, moduli, rest_bend, devices), AXES,...]
  transfers between devices with their start and end apart: 7 -> 1, of which waited for: 6 -> 0; matrix products, arithmetic and copies ran while one was open for 4% -> 0% of each run, Pallas kernels for 0% -> 0%
where the time goes in v1:
time: 215 us; the launch traced here: 214 us
  blocking collectives  157 us (73%)
  Pallas kernels  43.6 us (20%)
  starting transfers between devices  7.1 us (3%)
  local copies, waits for them, and re-layouts  4.53 us (2%)
    all_gather x4, blocking collectives, gather_state(): return lax.all_gather(state, AXES, axis=0)  157 us
    pallas_call x3, Pallas kernels, body(): pl.pallas_call(step_kernel, out_shape=jax.ShapeDtypeStruct((ROWS, nodes),...  30.4 us
    pallas_call x1, Pallas kernels, body(): pl.pallas_call(last_kernel, out_shape=(jax.ShapeDtypeStruct((3, nodes), j...  10.6 us
    all_to_all x1, starting transfers between devices, body(): lax.all_to_all(pack_slots(rest_length, moduli, rest_bend, devices), AXES,...  7.1 us
  transfers between devices with their start and end apart: 1, of which 0 were waited for; matrix products, arithmetic and copies ran while one was open for 0% of the time, Pallas kernels for 0%

profile of v1, /device:TPU:1, one launch (start us, length us, event | category | flops | bytes accessed | tf_op | source)
XLA Modules:
  0.0 214.3 jit_solution(1972611967548676190)
XLA Ops:
  0.6 0.0 copy-start.1
  0.6 0.8 copy-done.1
  1.4 0.0 copy-start.2
  1.4 0.7 copy-done.2
  2.1 0.0 copy-start.3
  2.1 0.7 copy-done.3
  2.8 0.2 shard_map.86
  3.0 0.9 reshape.12
  3.9 0.0 copy-start.5
  3.9 0.0 copy-start.6
  3.9 7.1 %all-to-all-start = ((f32[32,1,640]{2,1,0:T(1,128)}), f32[32,1,640]{2,1,0:T(1,128)S(1)}, u32[]{:S(2)}, u32[]{:S(2)}) async-start(f32[32,1,640]{2,1,0:T(1,128)} %reshape.12), calls=%async_computation | async-start | bytes 163840 | tf_op jit(solution)/shard_map/all_to_all | solution.py:183
  11.0 0.1 pad.2.clone
  11.1 0.0 copy-done.5
  11.1 0.0 copy-done.6
  11.1 0.1 maximum_maximum_fusion.own_ref
  11.2 43.0 %all-gather = f32[256,256]{1,0:T(8,128)S(1)} all-gather(f32[8,256]{1,0:T(8,128)S(1)} %maximum_maximum_fusion.own_ref), channel_id=2, replica_groups=mesh['tgt'=4,'src'=8] {'tgt','src'}, dimensions={0}, use_global_device_ids=true | all-gather | bytes 270336 | tf_op jit(solution)/shard_map/all_gather | solution.py:177
  54.1 0.0 all-to-all-done
  54.1 0.5 broadcast.2
  54.7 0.8 reduce
  55.5 0.2 reshape.13.slots_ref
  55.7 0.0 copy-start.4
  55.7 0.7 copy-done.4
  56.4 0.0 copy-start
  56.4 2.4 %shard_map.87.params_ref = f32[16,256]{1,0:T(8,128)S(1)} custom-call(f32[32,16,40]{2,1,0:T(8,128)S(1)} %reshape.13.slots_ref, s32[1,256]{1,0:T(1,128)S(1)} %bitcast.9), custom_call_target="tpu_custom_call" | custom-call | tf_op jit(solution)/shard_map/pallas_call | solution.py:73
  58.8 0.0 copy-done
  58.8 10.1 %shard_map.88.own_ref = f32[8,256]{1,0:T(8,128)S(1)} custom-call(f32[32,8,256]{2,1,0:T(8,128)S(1)} %bitcast.5, f32[8,256]{1,0:T(8,128)S(1)} %maximum_maximum_fusion.own_ref, s32[12,256]{1,0:T(8,128)S(1)} %copy-done, f32[16,256]{1,0:T(8,128)S(1)} %shard_map.87.params_ref), custom_call_target="tpu_custom_call" | custom-call | tf_op jit(solution)/shard_map/pallas_call | solution.py:189
  68.9 37.7 %all-gather.1 = f32[256,256]{1,0:T(8,128)S(1)} all-gather(f32[8,256]{1,0:T(8,128)S(1)} %shard_map.88.own_ref), channel_id=3, replica_groups=mesh['tgt'=4,'src'=8] {'tgt','src'}, dimensions={0}, use_global_device_ids=true | all-gather | bytes 270336 | tf_op jit(solution)/shard_map/all_gather | solution.py:177
  106.6 10.2 %shard_map.89.own_ref = f32[8,256]{1,0:T(8,128)S(1)} custom-call(f32[32,8,256]{2,1,0:T(8,128)S(1)} %bitcast.8, f32[8,256]{1,0:T(8,128)S(1)} %shard_map.88.own_ref, s32[12,256]{1,0:T(8,128)S(1)} %copy-done, f32[16,256]{1,0:T(8,128)S(1)} %shard_map.87.params_ref), custom_call_target="tpu_custom_call" | custom-call | tf_op jit(solution)/shard_map/pallas_call | solution.py:189
  116.8 39.0 %all-gather.2 = f32[256,256]{1,0:T(8,128)S(1)} all-gather(f32[8,256]{1,0:T(8,128)S(1)} %shard_map.89.own_ref), channel_id=4, replica_groups=mesh['tgt'=4,'src'=8] {'tgt','src'}, dimensions={0}, use_global_device_ids=true | all-gather | bytes 270336 | tf_op jit(solution)/shard_map/all_gather | solution.py:177
  155.8 10.2 %shard_map.90.own_ref = f32[8,256]{1,0:T(8,128)S(1)} custom-call(f32[32,8,256]{2,1,0:T(8,128)S(1)} %bitcast.7, f32[8,256]{1,0:T(8,128)S(1)} %shard_map.89.own_ref, s32[12,256]{1,0:T(8,128)S(1)} %copy-done, f32[16,256]{1,0:T(8,128)S(1)} %shard_map.87.params_ref), custom_call_target="tpu_custom_call" | custom-call | tf_op jit(solution)/shard_map/pallas_call | solution.py:189
  166.0 37.7 %all-gather.3 = f32[256,256]{1,0:T(8,128)S(1)} all-gather(f32[8,256]{1,0:T(8,128)S(1)} %shard_map.90.own_ref), channel_id=5, replica_groups=mesh['tgt'=4,'src'=8] {'tgt','src'}, dimensions={0}, use_global_device_ids=true | all-gather | bytes 270336 | tf_op jit(solution)/shard_map/all_gather | solution.py:177
  203.7 10.6 %shard_map.91 = (f32[3,256]{1,0:T(4,128)}, f32[3,256]{1,0:T(4,128)}) custom-call(f32[32,8,256]{2,1,0:T(8,128)S(1)} %bitcast.6, f32[8,256]{1,0:T(8,128)S(1)} %shard_map.90.own_ref), custom_call_target="tpu_custom_call" | custom-call | tf_op jit(solution)/shard_map/pallas_call | solution.py:197
  (1 shorter events, 0.0 us)
Async XLA Ops:
  0.6 0.8 copy-start.1
  1.4 0.7 copy-start.2
  2.1 0.7 copy-start.3
  3.9 7.2 %copy-start.5 = (f32[3,256]{1,0:T(4,128)S(1)}, f32[3,256]{1,0:T(4,128)}, u32[]{:S(2)}) copy-start(f32[3,256]{1,0:T(4,128)} %param.8) | copy-start | bytes 9220
  3.9 7.2 %copy-start.6 = (f32[3,256]{1,0:T(4,128)S(1)}, f32[3,256]{1,0:T(4,128)}, u32[]{:S(2)}) copy-start(f32[3,256]{1,0:T(4,128)} %param.7) | copy-start | bytes 9220
  3.9 50.2 %all-to-all-start = ((f32[32,1,640]{2,1,0:T(1,128)}), f32[32,1,640]{2,1,0:T(1,128)S(1)}, u32[]{:S(2)}, u32[]{:S(2)}) async-start(f32[32,1,640]{2,1,0:T(1,128)} %reshape.12), calls=%async_computation | async-start | bytes 163840 | tf_op jit(solution)/shard_map/all_to_all | solution.py:183
  55.7 0.7 copy-start.4
  56.4 2.4 %copy-start = (s32[12,256]{1,0:T(8,128)S(1)}, s32[12,256]{1,0:T(8,128)}, u32[]{:S(2)}) copy-start(s32[12,256]{1,0:T(8,128)} %neighbours_ref.5) | copy-start | bytes 36868

commit v2 on v1

--- a/solution.py
+++ b/solution.py
@@ -23,28 +23,28 @@
 
 
 def pack_kernel(length_ref, moduli_ref, bend_ref, out_ref):
-    devices, _, capacity = out_ref.shape
+    devices = out_ref.shape[0]
+    capacity = length_ref.shape[1] // devices
+    out_ref[...] = jnp.zeros(out_ref.shape, jnp.float32)
     for device in range(devices):
         cut = slice(device * capacity, (device + 1) * capacity)
-        out_ref[device, 0:6, :] = length_ref[:, cut]
-        out_ref[device, 6:8, :] = moduli_ref[:, cut]
-        out_ref[device, 8:11, :] = bend_ref[:, cut]
-        out_ref[device, 11:PARAMS, :] = jnp.zeros((PARAMS - 11, capacity), jnp.float32)
+        out_ref[device, 0:6, 0:capacity] = length_ref[:, cut]
+        out_ref[device, 6:8, 0:capacity] = moduli_ref[:, cut]
+        out_ref[device, 0:3, capacity : 2 * capacity] = bend_ref[:, cut]
 
 
 def pack_slots(rest_length, moduli, rest_bend, devices):
-    capacity = rest_length.shape[1] // devices
     return pl.pallas_call(
         pack_kernel,
-        out_shape=jax.ShapeDtypeStruct((devices, PARAMS, capacity), jnp.float32),
+        out_shape=jax.ShapeDtypeStruct((devices, ROWS, LANES), jnp.float32),
         in_specs=[VMEM] * 3,
         out_specs=VMEM,
         compiler_params=GRANT,
     )(rest_length, moduli, rest_bend)
 
 
-def pick_kernel(slots_ref, owner_ref, out_ref):
-    devices, _, capacity = slots_ref.shape
+def pick_kernel(capacity, slots_ref, owner_ref, out_ref):
+    devices = slots_ref.shape[0]
     nodes = owner_ref.shape[1]
     owner = owner_ref[...]
     across = jnp.broadcast_to(owner, (nodes, nodes))
@@ -56,22 +56,22 @@
     for at in range(0, nodes, LANES):
         place = jnp.broadcast_to(rank[:, at : at + LANES], (ROWS, LANES))
         named = jnp.broadcast_to(owner[:, at : at + LANES], (ROWS, LANES))
-        for row in range(0, PARAMS, ROWS):
+        for part in range(PARAMS // ROWS):
 
             def choose(device, chosen):
-                block = slots_ref[device, row : row + ROWS, :]
-                block = jnp.concatenate([block, jnp.zeros((ROWS, LANES - capacity), jnp.float32)], axis=1)
-                taken = jnp.take_along_axis(block, place, axis=1, mode="promise_in_bounds")
+                taken = jnp.take_along_axis(
+                    slots_ref[device], place + part * capacity, axis=1, mode="promise_in_bounds"
+                )
                 return jnp.where(named == device, taken, chosen)
 
-            out_ref[row : row + ROWS, at : at + LANES] = lax.fori_loop(
+            out_ref[part * ROWS : (part + 1) * ROWS, at : at + LANES] = lax.fori_loop(
                 0, devices, choose, jnp.zeros((ROWS, LANES), jnp.float32), unroll=4
             )
 
 
-def pick_slots(slots, owner):
+def pick_slots(slots, owner, capacity):
     return pl.pallas_call(
-        pick_kernel,
+        functools.partial(pick_kernel, capacity),
         out_shape=jax.ShapeDtypeStruct((PARAMS, owner.shape[1]), jnp.float32),
         in_specs=[VMEM] * 2,
         out_specs=VMEM,
@@ -173,8 +173,9 @@
     return [pltpu.VMEM((3, nodes, LANES), jnp.float32), pltpu.VMEM((3, nodes, LANES), jnp.float32)]
 
 
-def gather_state(state):
-    return lax.all_gather(state, AXES, axis=0)
+def gather_state(state, devices):
+    spread = jnp.broadcast_to(state[None], (devices,) + state.shape)
+    return lax.all_to_all(spread, AXES, split_axis=0, concat_axis=0, tiled=True)
 
 
 def body(positions, forces, neighbours, patch_owner, rest_length, moduli, rest_bend):
@@ -184,7 +185,7 @@
         pack_slots(rest_length, moduli, rest_bend, devices), AXES, split_axis=0, concat_axis=0, tiled=True
     )
     state = jnp.concatenate([positions, forces, jnp.zeros((ROWS - 6, nodes), jnp.float32)], axis=0)
-    params = pick_slots(slots, patch_owner.reshape(1, nodes))
+    params = pick_slots(slots, patch_owner.reshape(1, nodes), rest_length.shape[1] // devices)
     for _ in range(STEPS):
         state = pl.pallas_call(
             step_kernel,
@@ -193,7 +194,7 @@
             out_specs=VMEM,
             scratch_shapes=scratch(nodes),
             compiler_params=GRANT,
-        )(gather_state(state), state, neighbours, params)
+        )(gather_state(state, devices), state, neighbours, params)
     return pl.pallas_call(
         last_kernel,
         out_shape=(jax.ShapeDtypeStruct((3, nodes), jnp.float32),) * 2,
@@ -201,7 +202,7 @@
         out_specs=(VMEM,) * 2,
         scratch_shapes=scratch(nodes),
         compiler_params=GRANT,
-    )(gather_state(state), state)
+    )(gather_state(state, devices), state)
 
 
 def solution(mesh):

time: 215 us -> 112 us (0.52)
  blocking collectives: 157 us -> 38 us
  waiting for transfers between devices: 0.01 us -> 15.6 us
  starting transfers between devices: 7.1 us -> 9.48 us
    all_gather x4 -> x0, blocking collectives: 157 us -> none  [gather_state(): return lax.all_gather(state, AXES, axis=0)]
    all_to_all x0 -> x3, blocking collectives: none -> 38 us  [gather_state(): return lax.all_to_all(spread, AXES, split_axis=0, concat_axis=0, tiled=True)]
    all_to_all x1, waiting for transfers between devices: 0.01 us -> 8.07 us  [body(): lax.all_to_all(pack_slots(rest_length, moduli, rest_bend, devices), AXES,...]
    all_to_all x0 -> x1, waiting for transfers between devices: none -> 7.5 us  [gather_state(): return lax.all_to_all(spread, AXES, split_axis=0, concat_axis=0, tiled=True)]
    all_to_all x0 -> x1, starting transfers between devices: none -> 2.38 us  [gather_state(): return lax.all_to_all(spread, AXES, split_axis=0, concat_axis=0, tiled=True)]
  transfers between devices with their start and end apart: 1 -> 2, of which waited for: 0 -> 2; matrix products, arithmetic and copies ran while one was open for 0% -> 0% of each run, Pallas kernels for 0% -> 2%
where the time goes in v2:
time: 112 us
  Pallas kernels  44.3 us (40%)
  blocking collectives  38 us (34%)
  waiting for transfers between devices  15.6 us (14%)
  starting transfers between devices  9.48 us (8%)
  local copies, waits for them, and re-layouts  3.75 us (3%)
    all_to_all x3, blocking collectives, gather_state(): return lax.all_to_all(spread, AXES, split_axis=0, concat_axis=0, tiled=True)  38 us
    pallas_call x3, Pallas kernels, body(): pl.pallas_call(step_kernel, out_shape=jax.ShapeDtypeStruct((ROWS, nodes),...  30.3 us
    pallas_call x1, Pallas kernels, body(): pl.pallas_call(last_kernel, out_shape=(jax.ShapeDtypeStruct((3, nodes), j...  10.6 us
    all_to_all x1, waiting for transfers between devices, body(): lax.all_to_all(pack_slots(rest_length, moduli, rest_bend, devices), AXES,...  8.07 us
    all_to_all x1, waiting for transfers between devices, gather_state(): return lax.all_to_all(spread, AXES, split_axis=0, concat_axis=0, tiled=True)  7.5 us
    all_to_all x1, starting transfers between devices, body(): lax.all_to_all(pack_slots(rest_length, moduli, rest_bend, devices), AXES,...  7.1 us
    unnamed x14, local copies, waits for them, and re-layouts  2.89 us
    pallas_call x1, Pallas kernels, pick_slots(): pl.pallas_call(functools.partial(pick_kernel, capacity), out_shape=jax.Sh...  2.46 us
  transfers between devices with their start and end apart: 2, of which 2 were waited for; matrix products, arithmetic and copies ran while one was open for 0% of the time, Pallas kernels for 2%

profile of v2, /device:TPU:1, one launch (start us, length us, event | category | flops | bytes accessed | tf_op | source)
XLA Modules:
  0.0 111.9 jit_solution(11531353103099310156)
XLA Ops:
  0.6 0.0 copy-start.1
  0.6 0.8 copy-done.1
  1.4 0.0 copy-start.2
  1.4 0.7 copy-done.2
  2.1 0.0 copy-start.3
  2.1 0.7 copy-done.3
  2.8 0.8 shard_map.86
  3.7 0.0 copy-start.5
  3.7 0.0 copy-start.6
  3.7 7.1 %all-to-all-start.1 = ((f32[32,8,128]{2,1,0:T(8,128)}), f32[32,8,128]{2,1,0:T(8,128)S(1)}, u32[]{:S(2)}, u32[]{:S(2)}) async-start(f32[32,8,128]{2,1,0:T(8,128)} %shard_map.86), calls=%async_computation.1 | async-start | bytes 262144 | tf_op jit(solution)/shard_map/all_to_all | solution.py:184
  10.8 0.1 pad.2.clone
  10.9 0.0 copy-done.5
  10.9 0.0 copy-done.6
  10.9 0.1 maximum_maximum_fusion.own_ref
  10.9 8.1 %all-to-all-done.1.slots_ref = f32[32,8,128]{2,1,0:T(8,128)S(1)} async-done(((f32[32,8,128]{2,1,0:T(8,128)}), f32[32,8,128]{2,1,0:T(8,128)S(1)}, u32[]{:S(2)}, u32[]{:S(2)}) %all-to-all-start.1) | async-done | bytes 131104 | tf_op jit(solution)/shard_map/all_to_all | solution.py:184
  19.0 0.7 broadcast_in_dim.11
  19.7 2.4 %all-to-all-start = ((f32[32,8,256]{2,1,0:T(8,128)}), f32[32,8,256]{2,1,0:T(8,128)S(1)}, u32[]{:S(2)}, u32[]{:S(2)}) async-start(f32[32,8,256]{2,1,0:T(8,128)} %broadcast_in_dim.11), calls=%async_computation | async-start | bytes 524288 | tf_op jit(solution)/shard_map/all_to_all | solution.py:178
  22.1 0.0 copy-start.4
  22.1 0.7 copy-done.4
  22.8 0.0 copy-start
  22.8 2.5 %shard_map.87.params_ref = f32[16,256]{1,0:T(8,128)S(1)} custom-call(f32[32,8,128]{2,1,0:T(8,128)S(1)} %all-to-all-done.1.slots_ref, s32[1,256]{1,0:T(1,128)S(1)} %bitcast.1), custom_call_target="tpu_custom_call" | custom-call | tf_op jit(solution)/shard_map/pallas_call | solution.py:73
  25.3 7.5 %all-to-all-done.all_ref = f32[32,8,256]{2,1,0:T(8,128)S(1)} async-done(((f32[32,8,256]{2,1,0:T(8,128)}), f32[32,8,256]{2,1,0:T(8,128)S(1)}, u32[]{:S(2)}, u32[]{:S(2)}) %all-to-all-start) | async-done | bytes 262176 | tf_op jit(solution)/shard_map/all_to_all | solution.py:178
  32.8 0.0 copy-done
  32.8 10.0 %shard_map.88.own_ref = f32[8,256]{1,0:T(8,128)S(1)} custom-call(f32[32,8,256]{2,1,0:T(8,128)S(1)} %all-to-all-done.all_ref, f32[8,256]{1,0:T(8,128)S(1)} %maximum_maximum_fusion.own_ref, s32[12,256]{1,0:T(8,128)S(1)} %copy-done, f32[16,256]{1,0:T(8,128)S(1)} %shard_map.87.params_ref), custom_call_target="tpu_custom_call" | custom-call | tf_op jit(solution)/shard_map/pallas_call | solution.py:190
  42.9 12.6 %all_to_all.25.all_ref = f32[32,8,256]{2,1,0:T(8,128)S(1)} all-to-all(f32[32,8,256]{2,1,0:T(8,128)S(1)} %broadcast_in_dim.12), channel_id=1, replica_groups=mesh['tgt'=4,'src'=8] {'tgt','src'}, dimensions={0} | all-to-all | bytes 524288 | tf_op jit(solution)/shard_map/all_to_all | solution.py:178
  55.5 10.2 %shard_map.89.own_ref = f32[8,256]{1,0:T(8,128)S(1)} custom-call(f32[32,8,256]{2,1,0:T(8,128)S(1)} %all_to_all.25.all_ref, f32[8,256]{1,0:T(8,128)S(1)} %shard_map.88.own_ref, s32[12,256]{1,0:T(8,128)S(1)} %copy-done, f32[16,256]{1,0:T(8,128)S(1)} %shard_map.87.params_ref), custom_call_target="tpu_custom_call" | custom-call | tf_op jit(solution)/shard_map/pallas_call | solution.py:190
  65.7 12.7 %all_to_all.26.all_ref = f32[32,8,256]{2,1,0:T(8,128)S(1)} all-to-all(f32[32,8,256]{2,1,0:T(8,128)S(1)} %broadcast_in_dim.13), channel_id=1, replica_groups=mesh['tgt'=4,'src'=8] {'tgt','src'}, dimensions={0} | all-to-all | bytes 524288 | tf_op jit(solution)/shard_map/all_to_all | solution.py:178
  78.4 10.2 %shard_map.90.own_ref = f32[8,256]{1,0:T(8,128)S(1)} custom-call(f32[32,8,256]{2,1,0:T(8,128)S(1)} %all_to_all.26.all_ref, f32[8,256]{1,0:T(8,128)S(1)} %shard_map.89.own_ref, s32[12,256]{1,0:T(8,128)S(1)} %copy-done, f32[16,256]{1,0:T(8,128)S(1)} %shard_map.87.params_ref), custom_call_target="tpu_custom_call" | custom-call | tf_op jit(solution)/shard_map/pallas_call | solution.py:190
  88.6 12.7 %all_to_all.27.all_ref = f32[32,8,256]{2,1,0:T(8,128)S(1)} all-to-all(f32[32,8,256]{2,1,0:T(8,128)S(1)} %broadcast_in_dim.14), channel_id=1, replica_groups=mesh['tgt'=4,'src'=8] {'tgt','src'}, dimensions={0} | all-to-all | bytes 524288 | tf_op jit(solution)/shard_map/all_to_all | solution.py:178
  101.3 10.6 %shard_map.91 = (f32[3,256]{1,0:T(4,128)}, f32[3,256]{1,0:T(4,128)}) custom-call(f32[32,8,256]{2,1,0:T(8,128)S(1)} %all_to_all.27.all_ref, f32[8,256]{1,0:T(8,128)S(1)} %shard_map.90.own_ref), custom_call_target="tpu_custom_call" | custom-call | tf_op jit(solution)/shard_map/pallas_call | solution.py:198
  (4 shorter events, 0.1 us)
Async XLA Ops:
  0.6 0.8 copy-start.1
  1.4 0.7 copy-start.2
  2.1 0.7 copy-start.3
  3.7 7.2 %copy-start.5 = (f32[3,256]{1,0:T(4,128)S(1)}, f32[3,256]{1,0:T(4,128)}, u32[]{:S(2)}) copy-start(f32[3,256]{1,0:T(4,128)} %param.8) | copy-start | bytes 9220
  3.7 7.2 %copy-start.6 = (f32[3,256]{1,0:T(4,128)S(1)}, f32[3,256]{1,0:T(4,128)}, u32[]{:S(2)}) copy-start(f32[3,256]{1,0:T(4,128)} %param.7) | copy-start | bytes 9220
  3.7 15.3 %all-to-all-start.1 = ((f32[32,8,128]{2,1,0:T(8,128)}), f32[32,8,128]{2,1,0:T(8,128)S(1)}, u32[]{:S(2)}, u32[]{:S(2)}) async-start(f32[32,8,128]{2,1,0:T(8,128)} %shard_map.86), calls=%async_computation.1 | async-start | bytes 262144 | tf_op jit(solution)/shard_map/all_to_all | solution.py:184
  19.7 13.0 %all-to-all-start = ((f32[32,8,256]{2,1,0:T(8,128)}), f32[32,8,256]{2,1,0:T(8,128)S(1)}, u32[]{:S(2)}, u32[]{:S(2)}) async-start(f32[32,8,256]{2,1,0:T(8,128)} %broadcast_in_dim.11), calls=%async_computation | async-start | bytes 524288 | tf_op jit(solution)/shard_map/all_to_all | solution.py:178
  22.1 0.7 copy-start.4
  22.8 10.0 %copy-start = (s32[12,256]{1,0:T(8,128)S(1)}, s32[12,256]{1,0:T(8,128)}, u32[]{:S(2)}) copy-start(s32[12,256]{1,0:T(8,128)} %neighbours_ref.5) | copy-start | bytes 36868

commit v3 on v2

--- a/solution.py
+++ b/solution.py
@@ -79,38 +79,48 @@
     )(slots, owner)
 
 
-def pair_sums(all_ref, own_ref, column_ref, sum_ref):
-    devices, _, nodes = all_ref.shape
-    for c in range(3):
-        for at in range(0, nodes, LANES):
+def spread_columns(own_ref, column_ref):
+    for c in range(3):
+        for at in range(0, own_ref.shape[1], LANES):
             row = own_ref[c : c + 1, at : at + LANES]
             column_ref[c, at : at + LANES, :] = jnp.broadcast_to(row, (LANES, LANES)).T
+
+
+def pair_sums(source_refs, column_ref, start_ref, sum_ref):
+    nodes = column_ref.shape[1]
 
     def per_target(block, _):
         rows = pl.ds(pl.multiple_of(block * TARGET_ROWS, TARGET_ROWS), TARGET_ROWS)
         target = [column_ref[c, rows, :] for c in range(3)]
-
-        def per_source(device, totals):
-            for at in range(0, nodes, LANES):
-                x = [all_ref[device, c : c + 1, at : at + LANES] for c in range(3)]
-                f = [all_ref[device, 3 + c : 4 + c, at : at + LANES] for c in range(3)]
-                d = [target[c] - x[c] for c in range(3)]
-                shifted = d[0] * d[0] + (d[1] * d[1] + (d[2] * d[2] + blob_square))
-                r = lax.rsqrt(shifted)
-                cube = r * (r * r)
-                direct = r + blob_square * cube
-                along = (d[0] * f[0] + d[1] * f[1] + d[2] * f[2]) * cube
-                totals = tuple(totals[c] + (direct * f[c] + along * d[c]) for c in range(3))
-            return totals
-
-        zero = jnp.zeros((TARGET_ROWS, LANES), jnp.float32)
-        totals = lax.fori_loop(0, devices, per_source, (zero, zero, zero), unroll=2)
+        if start_ref is None:
+            totals = (jnp.zeros((TARGET_ROWS, LANES), jnp.float32),) * 3
+        else:
+            totals = tuple(start_ref[c, rows, :] for c in range(3))
+        for source_ref in source_refs:
+
+            def per_source(device, totals):
+                for at in range(0, nodes, LANES):
+                    x = [source_ref[device, c : c + 1, at : at + LANES] for c in range(3)]
+                    f = [source_ref[device, 3 + c : 4 + c, at : at + LANES] for c in range(3)]
+                    d = [target[c] - x[c] for c in range(3)]
+                    shifted = d[0] * d[0] + (d[1] * d[1] + (d[2] * d[2] + blob_square))
+                    r = lax.rsqrt(shifted)
+                    cube = r * (r * r)
+                    direct = r + blob_square * cube
+                    along = (d[0] * f[0] + d[1] * f[1] + d[2] * f[2]) * cube
+                    totals = tuple(totals[c] + (direct * f[c] + along * d[c]) for c in range(3))
+                return totals
+
+            totals = lax.fori_loop(0, source_ref.shape[0], per_source, totals, unroll=2)
         for c in range(3):
             sum_ref[c, rows, :] = totals[c]
         return 0
 
     lax.fori_loop(0, nodes // TARGET_ROWS, per_target, 0)
-    scale = 1.0 / math.sqrt(devices * nodes)
+
+
+def velocity_rows(sum_ref, scale):
+    nodes = sum_ref.shape[1]
     velocity = []
     for c in range(3):
         parts = [
@@ -152,8 +162,15 @@
     return [jnp.concatenate(parts, axis=1) for parts in force]
 
 
-def step_kernel(all_ref, own_ref, neighbours_ref, params_ref, out_ref, column_ref, sum_ref):
-    velocity = pair_sums(all_ref, own_ref, column_ref, sum_ref)
+def near_kernel(source_ref, own_ref, column_ref, sum_ref):
+    spread_columns(own_ref, column_ref)
+    pair_sums([source_ref], column_ref, None, sum_ref)
+
+
+def step_kernel(others, scale, *refs):
+    own_ref, column_ref, start_ref, neighbours_ref, params_ref, out_ref, sum_ref = refs[others:]
+    pair_sums(refs[:others], column_ref, start_ref, sum_ref)
+    velocity = velocity_rows(sum_ref, scale)
     x = [own_ref[c : c + 1, :] + time_step * velocity[c] for c in range(3)]
     force = membrane(x, neighbours_ref, params_ref)
     for c in range(3):
@@ -162,47 +179,70 @@
     out_ref[6:ROWS, :] = jnp.zeros((ROWS - 6, x[0].shape[1]), jnp.float32)
 
 
-def last_kernel(all_ref, own_ref, position_ref, velocity_ref, column_ref, sum_ref):
-    velocity = pair_sums(all_ref, own_ref, column_ref, sum_ref)
+def last_kernel(others, scale, *refs):
+    own_ref, column_ref, start_ref, position_ref, velocity_ref, sum_ref = refs[others:]
+    pair_sums(refs[:others], column_ref, start_ref, sum_ref)
+    velocity = velocity_rows(sum_ref, scale)
     position_ref[...] = own_ref[0:3, :]
     for c in range(3):
         velocity_ref[c : c + 1, :] = velocity[c]
 
 
-def scratch(nodes):
-    return [pltpu.VMEM((3, nodes, LANES), jnp.float32), pltpu.VMEM((3, nodes, LANES), jnp.float32)]
-
-
-def gather_state(state, devices):
-    spread = jnp.broadcast_to(state[None], (devices,) + state.shape)
-    return lax.all_to_all(spread, AXES, split_axis=0, concat_axis=0, tiled=True)
+def exchange(block, axis):
+    size = lax.axis_size(axis)
+    return [
+        lax.ppermute(
+            block, axis, [(i, (i + shift) % size if size & (size - 1) else i ^ shift) for i in range(size)]
+        )
+        for shift in range(1, size)
+    ]
+
+
+def near_sums(near, state):
+    nodes = state.shape[1]
+    shape = jax.ShapeDtypeStruct((3, nodes, LANES), jnp.float32)
+    pairs = near.shape[0] * nodes * nodes
+    return pl.pallas_call(
+        near_kernel,
+        out_shape=(shape, shape),
+        in_specs=[VMEM] * 2,
+        out_specs=(VMEM,) * 2,
+        compiler_params=GRANT,
+        cost_estimate=pl.CostEstimate(flops=31 * pairs, bytes_accessed=8 * 3 * nodes * LANES, transcendentals=pairs),
+    )(near, state)
 
 
 def body(positions, forces, neighbours, patch_owner, rest_length, moduli, rest_bend):
     devices = lax.axis_size("tgt") * lax.axis_size("src")
     nodes = positions.shape[1]
+    scale = 1.0 / math.sqrt(devices * nodes)
     slots = lax.all_to_all(
         pack_slots(rest_length, moduli, rest_bend, devices), AXES, split_axis=0, concat_axis=0, tiled=True
     )
     state = jnp.concatenate([positions, forces, jnp.zeros((ROWS - 6, nodes), jnp.float32)], axis=0)
     params = pick_slots(slots, patch_owner.reshape(1, nodes), rest_length.shape[1] // devices)
-    for _ in range(STEPS):
-        state = pl.pallas_call(
-            step_kernel,
-            out_shape=jax.ShapeDtypeStruct((ROWS, nodes), jnp.float32),
-            in_specs=[VMEM] * 4,
-            out_specs=VMEM,
-            scratch_shapes=scratch(nodes),
-            compiler_params=GRANT,
-        )(gather_state(state, devices), state, neighbours, params)
-    return pl.pallas_call(
-        last_kernel,
+    sums = [pltpu.VMEM((3, nodes, LANES), jnp.float32)]
+    for step in range(STEPS + 1):
+        near = jnp.stack([state] + exchange(state, "src"))
+        far = exchange(near, "tgt")
+        column, start = near_sums(near, state)
+        if step < STEPS:
+            state = pl.pallas_call(
+                functools.partial(step_kernel, len(far), scale),
+                out_shape=jax.ShapeDtypeStruct((ROWS, nodes), jnp.float32),
+                in_specs=[VMEM] * (len(far) + 5),
+                out_specs=VMEM,
+                scratch_shapes=sums,
+                compiler_params=GRANT,
+            )(*far, state, column, start, neighbours, params)
+    return pl.pallas_call(
+        functools.partial(last_kernel, len(far), scale),
         out_shape=(jax.ShapeDtypeStruct((3, nodes), jnp.float32),) * 2,
-        in_specs=[VMEM] * 2,
+        in_specs=[VMEM] * (len(far) + 3),
         out_specs=(VMEM,) * 2,
-        scratch_shapes=scratch(nodes),
-        compiler_params=GRANT,
-    )(gather_state(state, devices), state)
+        scratch_shapes=sums,
+        compiler_params=GRANT,
+    )(*far, state, column, start)
 
 
 def solution(mesh):

time: 112 us -> 127 us (1.13); the launches traced: 112 us -> 125 us
  starting transfers between devices: 9.48 us -> 61.3 us
  blocking collectives: 38 us -> 0 us
  local copies, waits for them, and re-layouts: 3.75 us -> 1.6 us
    ppermute x0 -> x40, starting transfers between devices: none -> 55.5 us  [exchange(): lax.ppermute(block, axis, [(i, (i + shift) % size if size & size - 1 else...]
    all_to_all x3 -> x0, blocking collectives: 38 us -> none  [gather_state(): return lax.all_to_all(spread, AXES, split_axis=0, concat_axis=0, tiled=True)]
    ppermute x0 -> x40, waiting for transfers between devices: none -> 16.2 us  [exchange(): lax.ppermute(block, axis, [(i, (i + shift) % size if size & size - 1 else...]
    all_to_all x1, waiting for transfers between devices: 8.07 us -> 0.01 us  [body(): lax.all_to_all(pack_slots(rest_length, moduli, rest_bend, devices), AXES,...]
    all_to_all x1 -> x0, waiting for transfers between devices: 7.5 us -> none  [gather_state(): return lax.all_to_all(spread, AXES, split_axis=0, concat_axis=0, tiled=True)]
    all_to_all x1 -> x0, starting transfers between devices: 2.38 us -> none  [gather_state(): return lax.all_to_all(spread, AXES, split_axis=0, concat_axis=0, tiled=True)]
    unnamed x14 -> x37, local copies, waits for them, and re-layouts: 2.89 us -> 1.51 us
    pallas_call x4 -> x8, Pallas kernels: 41 us -> 40.6 us  [the longest x3 22.3 us: body(): pl.pallas_call(functools.partial(step_kernel, len(far), scale), out_shape...]
  transfers between devices with their start and end apart: 2 -> 41, of which waited for: 2 -> 16; matrix products, arithmetic and copies ran while one was open for 0% -> 0% of each run, Pallas kernels for 2% -> 11%
where the time goes in v3:
time: 127 us; the launch traced here: 125 us
  starting transfers between devices  61.3 us (48%)
  Pallas kernels  43.9 us (35%)
  waiting for transfers between devices  16.2 us (13%)
  local copies, waits for them, and re-layouts  1.6 us (1%)
    ppermute x40, starting transfers between devices, exchange(): lax.ppermute(block, axis, [(i, (i + shift) % size if size & size - 1 else...  55.5 us
    pallas_call x3, Pallas kernels, body(): pl.pallas_call(functools.partial(step_kernel, len(far), scale), out_shape...  22.3 us
    ppermute x40, waiting for transfers between devices, exchange(): lax.ppermute(block, axis, [(i, (i + shift) % size if size & size - 1 else...  16.2 us
    pallas_call x4, Pallas kernels, near_sums(): pl.pallas_call(near_kernel, out_shape=(shape, shape), in_specs=[VMEM] * 2...  10.4 us
    pallas_call x1, Pallas kernels, body(): pl.pallas_call(functools.partial(last_kernel, len(far), scale), out_shape...  7.86 us
    all_to_all x1, starting transfers between devices, body(): lax.all_to_all(pack_slots(rest_length, moduli, rest_bend, devices), AXES,...  5.86 us
  transfers between devices with their start and end apart: 41, of which 16 were waited for; matrix products, arithmetic and copies ran while one was open for 0% of the time, Pallas kernels for 11%

profile of v3, /device:TPU:1, one launch (start us, length us, event | category | flops | bytes accessed | tf_op | source)
XLA Modules:
  0.0 124.8 jit_solution(231847343884797549)
XLA Ops:
  0.7 0.8 constant_dynamic-update-slice_fusion.7
  1.6 4.7 %collective-permute-start.6 = (f32[8,256]{1,0:T(8,128)S(1)}, f32[8,256]{1,0:T(8,128)S(1)}, u32[]{:S(2)}, u32[]{:S(2)}) collective-permute-start(f32[8,256]{1,0:T(8,128)S(1)} %get-tuple-element.19.own_ref.refs_3_), channel_id=1, source_target_pairs={{0,7},{1,6},{2,5},{3,4},{4,3},{5,2},{6,1},{7,0},{8,15},{9,14},{10,... | collective-permute-start | bytes 24584 | tf_op jit(solution)/shard_map/ppermute | solution.py:194
  6.4 1.0 collective-permute-start.4
  7.4 1.7 %collective-permute-start.3 = (f32[8,256]{1,0:T(8,128)S(1)}, f32[8,256]{1,0:T(8,128)S(1)}, u32[]{:S(2)}, u32[]{:S(2)}) collective-permute-start(f32[8,256]{1,0:T(8,128)S(1)} %get-tuple-element.19.own_ref.refs_3_), channel_id=1, source_target_pairs={{0,4},{1,5},{2,6},{3,7},{4,0},{5,1},{6,2},{7,3},{8,12},{9,13},{10,... | collective-permute-start | bytes 24584 | tf_op jit(solution)/shard_map/ppermute | solution.py:194
  9.1 0.8 copy-done.1
  9.8 0.8 shard_map.87
  10.7 5.9 %all-to-all-start = ((f32[32,8,128]{2,1,0:T(8,128)}), f32[32,8,128]{2,1,0:T(8,128)S(1)}, u32[]{:S(2)}, u32[]{:S(2)}) async-start(f32[32,8,128]{2,1,0:T(8,128)} %shard_map.87), calls=%async_computation | async-start | bytes 262144 | tf_op jit(solution)/shard_map/all_to_all | solution.py:219
  16.6 1.5 %collective-permute-start.1 = (f32[8,256]{1,0:T(8,128)S(1)}, f32[8,256]{1,0:T(8,128)S(1)}, u32[]{:S(2)}, u32[]{:S(2)}) collective-permute-start(f32[8,256]{1,0:T(8,128)S(1)} %get-tuple-element.19.own_ref.refs_3_), channel_id=1, source_target_pairs={{0,2},{1,3},{2,0},{3,1},{4,6},{5,7},{6,4},{7,5},{8,10},{9,11},{10,... | collective-permute-start | bytes 24584 | tf_op jit(solution)/shard_map/ppermute | solution.py:194
  18.0 1.4 %collective-permute-done.1 = f32[8,256]{1,0:T(8,128)S(1)} collective-permute-done((f32[8,256]{1,0:T(8,128)S(1)}, f32[8,256]{1,0:T(8,128)S(1)}, u32[]{:S(2)}, u32[]{:S(2)}) %collective-permute-start.1) | collective-permute-done | bytes 8224 | tf_op jit(solution)/shard_map/ppermute | solution.py:194
  19.4 2.5 %collective-permute-start.2 = (f32[8,256]{1,0:T(8,128)S(1)}, f32[8,256]{1,0:T(8,128)S(1)}, u32[]{:S(2)}, u32[]{:S(2)}) collective-permute-start(f32[8,256]{1,0:T(8,128)S(1)} %get-tuple-element.19.own_ref.refs_3_), channel_id=1, source_target_pairs={{0,3},{1,2},{2,1},{3,0},{4,7},{5,6},{6,5},{7,4},{8,11},{9,10},{10,... | collective-permute-start | bytes 24584 | tf_op jit(solution)/shard_map/ppermute | solution.py:194
  21.9 1.6 %collective-permute-done.2 = f32[8,256]{1,0:T(8,128)S(1)} collective-permute-done((f32[8,256]{1,0:T(8,128)S(1)}, f32[8,256]{1,0:T(8,128)S(1)}, u32[]{:S(2)}, u32[]{:S(2)}) %collective-permute-start.2) | collective-permute-done | bytes 8224 | tf_op jit(solution)/shard_map/ppermute | solution.py:194
  23.6 2.2 %collective-permute-start.9 = (f32[8,8,256]{2,1,0:T(8,128)S(1)}, f32[8,8,256]{2,1,0:T(8,128)S(1)}, u32[]{:S(2)}, u32[]{:S(2)}) collective-permute-start(f32[8,8,256]{2,1,0:T(8,128)S(1)} %constant_dynamic-update-slice_fusion.source_ref), channel_id=1, source_target_pairs={{0,24},{8,16},{16,8},{24,0},{1,25},{9,17},{17,9},{25,1},{2,26},{10... | collective-permute-start | bytes 196616 | tf_op jit(solution)/shard_map/ppermute | solution.py:194
  25.8 0.4 collective-permute-start.8
  26.2 0.1 collective-permute-start.7
  26.3 2.6 %shard_map.86 = (f32[3,256,128]{2,1,0:T(8,128)S(1)}, f32[3,256,128]{2,1,0:T(8,128)S(1)}) custom-call(f32[8,8,256]{2,1,0:T(8,128)S(1)} %constant_dynamic-update-slice_fusion.source_ref, f32[8,256]{1,0:T(8,128)S(1)} %get-tuple-element.19.own_ref.refs_3_), custom_call_target="tpu_custom_call" | custom-call | flops 16252928 | bytes 786432 | tf_op jit(solution)/shard_map/pallas_call | solution.py:205
  29.0 0.7 copy-done.4
  29.6 2.5 %shard_map.88.refs_7_ = f32[16,256]{1,0:T(8,128)S(1)} custom-call(f32[32,8,128]{2,1,0:T(8,128)S(1)} %all-to-all-done.slots_ref, s32[1,256]{1,0:T(1,128)S(1)} %bitcast.65), custom_call_target="tpu_custom_call" | custom-call | tf_op jit(solution)/shard_map/pallas_call | solution.py:73
  32.2 7.4 %shard_map.89.own_ref.refs_3_ = f32[8,256]{1,0:T(8,128)S(1)} custom-call(f32[8,8,256]{2,1,0:T(8,128)S(1)} %collective-permute-done.7.refs_0_, f32[8,8,256]{2,1,0:T(8,128)S(1)} %collective-permute-done.8.refs_1_, f32[8,8,256]{2,1,0:T(8,128)S(1)} %collective-permute-done.9.refs_2_, f32[8,256]{1,0:T(8,128)S(1)} %get-tuple-element.19.own_ref.refs_3_, ...), custom_call_target="tpu_custom_call" | custom-call | tf_op jit(solution)/shard_map/pallas_call | solution.py:230
  39.6 4.3 %collective-permute-start.16 = (f32[8,256]{1,0:T(8,128)S(1)}, f32[8,256]{1,0:T(8,128)S(1)}, u32[]{:S(2)}, u32[]{:S(2)}) collective-permute-start(f32[8,256]{1,0:T(8,128)S(1)} %shard_map.89.own_ref.refs_3_), channel_id=1, source_target_pairs={{0,7},{1,6},{2,5},{3,4},{4,3},{5,2},{6,1},{7,0},{8,15},{9,14},{10,... | collective-permute-start | bytes 24584 | tf_op jit(solution)/shard_map/ppermute | solution.py:194
  43.9 0.5 collective-permute-start.14
  44.4 2.2 %collective-permute-start.13 = (f32[8,256]{1,0:T(8,128)S(1)}, f32[8,256]{1,0:T(8,128)S(1)}, u32[]{:S(2)}, u32[]{:S(2)}) collective-permute-start(f32[8,256]{1,0:T(8,128)S(1)} %shard_map.89.own_ref.refs_3_), channel_id=1, source_target_pairs={{0,4},{1,5},{2,6},{3,7},{4,0},{5,1},{6,2},{7,3},{8,12},{9,13},{10,... | collective-permute-start | bytes 24584 | tf_op jit(solution)/shard_map/ppermute | solution.py:194
  46.6 0.3 collective-permute-start.10
  46.9 0.8 collective-permute-done.10
  47.8 0.9 collective-permute-start.11
  48.6 1.6 %collective-permute-done.11 = f32[8,256]{1,0:T(8,128)S(1)} collective-permute-done((f32[8,256]{1,0:T(8,128)S(1)}, f32[8,256]{1,0:T(8,128)S(1)}, u32[]{:S(2)}, u32[]{:S(2)}) %collective-permute-start.11) | collective-permute-done | bytes 8224 | tf_op jit(solution)/shard_map/ppermute | solution.py:194
  50.3 2.2 %collective-permute-start.12 = (f32[8,256]{1,0:T(8,128)S(1)}, f32[8,256]{1,0:T(8,128)S(1)}, u32[]{:S(2)}, u32[]{:S(2)}) collective-permute-start(f32[8,256]{1,0:T(8,128)S(1)} %shard_map.89.own_ref.refs_3_), channel_id=1, source_target_pairs={{0,3},{1,2},{2,1},{3,0},{4,7},{5,6},{6,5},{7,4},{8,11},{9,10},{10,... | collective-permute-start | bytes 24584 | tf_op jit(solution)/shard_map/ppermute | solution.py:194
  52.5 1.3 %collective-permute-done.12 = f32[8,256]{1,0:T(8,128)S(1)} collective-permute-done((f32[8,256]{1,0:T(8,128)S(1)}, f32[8,256]{1,0:T(8,128)S(1)}, u32[]{:S(2)}, u32[]{:S(2)}) %collective-permute-start.12) | collective-permute-done | bytes 8224 | tf_op jit(solution)/shard_map/ppermute | solution.py:194
  53.9 2.2 %collective-permute-start.19 = (f32[8,8,256]{2,1,0:T(8,128)S(1)}, f32[8,8,256]{2,1,0:T(8,128)S(1)}, u32[]{:S(2)}, u32[]{:S(2)}) collective-permute-start(f32[8,8,256]{2,1,0:T(8,128)S(1)} %constant_dynamic-update-slice_fusion.8.source_ref), channel_id=1, source_target_pairs={{0,24},{8,16},{16,8},{24,0},{1,25},{9,17},{17,9},{25,1},{2,26},{10... | collective-permute-start | bytes 196616 | tf_op jit(solution)/shard_map/ppermute | solution.py:194
  56.1 0.3 collective-permute-start.18
  56.3 0.3 collective-permute-start.17
  56.6 2.6 %shard_map.90 = (f32[3,256,128]{2,1,0:T(8,128)S(1)}, f32[3,256,128]{2,1,0:T(8,128)S(1)}) custom-call(f32[8,8,256]{2,1,0:T(8,128)S(1)} %constant_dynamic-update-slice_fusion.8.source_ref, f32[8,256]{1,0:T(8,128)S(1)} %shard_map.89.own_ref.refs_3_), custom_call_target="tpu_custom_call" | custom-call | flops 16252928 | bytes 786432 | tf_op jit(solution)/shard_map/pallas_call | solution.py:205
  59.2 0.6 collective-permute-done.18.refs_1_
  59.9 0.1 collective-permute-done.17.refs_0_
  60.0 7.4 %shard_map.91.own_ref.refs_3_ = f32[8,256]{1,0:T(8,128)S(1)} custom-call(f32[8,8,256]{2,1,0:T(8,128)S(1)} %collective-permute-done.17.refs_0_, f32[8,8,256]{2,1,0:T(8,128)S(1)} %collective-permute-done.18.refs_1_, f32[8,8,256]{2,1,0:T(8,128)S(1)} %collective-permute-done.19.refs_2_, f32[8,256]{1,0:T(8,128)S(1)} %shard_map.89.own_ref.refs_3_, ...), custom_call_target="tpu_custom_call" | custom-call | tf_op jit(solution)/shard_map/pallas_call | solution.py:230
  67.5 5.3 %collective-permute-start.26 = (f32[8,256]{1,0:T(8,128)S(1)}, f32[8,256]{1,0:T(8,128)S(1)}, u32[]{:S(2)}, u32[]{:S(2)}) collective-permute-start(f32[8,256]{1,0:T(8,128)S(1)} %shard_map.91.own_ref.refs_3_), channel_id=1, source_target_pairs={{0,7},{1,6},{2,5},{3,4},{4,3},{5,2},{6,1},{7,0},{8,15},{9,14},{10,... | collective-permute-start | bytes 24584 | tf_op jit(solution)/shard_map/ppermute | solution.py:194
  72.8 0.2 collective-permute-start.25
  72.9 2.5 %collective-permute-start.23 = (f32[8,256]{1,0:T(8,128)S(1)}, f32[8,256]{1,0:T(8,128)S(1)}, u32[]{:S(2)}, u32[]{:S(2)}) collective-permute-start(f32[8,256]{1,0:T(8,128)S(1)} %shard_map.91.own_ref.refs_3_), channel_id=1, source_target_pairs={{0,4},{1,5},{2,6},{3,7},{4,0},{5,1},{6,2},{7,3},{8,12},{9,13},{10,... | collective-permute-start | bytes 24584 | tf_op jit(solution)/shard_map/ppermute | solution.py:194
  75.5 0.5 collective-permute-start.20
  76.0 0.8 collective-permute-done.20
  76.8 0.7 collective-permute-start.21
  77.5 1.8 %collective-permute-done.21 = f32[8,256]{1,0:T(8,128)S(1)} collective-permute-done((f32[8,256]{1,0:T(8,128)S(1)}, f32[8,256]{1,0:T(8,128)S(1)}, u32[]{:S(2)}, u32[]{:S(2)}) %collective-permute-start.21) | collective-permute-done | bytes 8224 | tf_op jit(solution)/shard_map/ppermute | solution.py:194
  79.3 2.1 %collective-permute-start.22 = (f32[8,256]{1,0:T(8,128)S(1)}, f32[8,256]{1,0:T(8,128)S(1)}, u32[]{:S(2)}, u32[]{:S(2)}) collective-permute-start(f32[8,256]{1,0:T(8,128)S(1)} %shard_map.91.own_ref.refs_3_), channel_id=1, source_target_pairs={{0,3},{1,2},{2,1},{3,0},{4,7},{5,6},{6,5},{7,4},{8,11},{9,10},{10,... | collective-permute-start | bytes 24584 | tf_op jit(solution)/shard_map/ppermute | solution.py:194
  81.4 1.3 %collective-permute-done.22 = f32[8,256]{1,0:T(8,128)S(1)} collective-permute-done((f32[8,256]{1,0:T(8,128)S(1)}, f32[8,256]{1,0:T(8,128)S(1)}, u32[]{:S(2)}, u32[]{:S(2)}) %collective-permute-start.22) | collective-permute-done | bytes 8224 | tf_op jit(solution)/shard_map/ppermute | solution.py:194
  82.8 1.3 %collective-permute-start.29 = (f32[8,8,256]{2,1,0:T(8,128)S(1)}, f32[8,8,256]{2,1,0:T(8,128)S(1)}, u32[]{:S(2)}, u32[]{:S(2)}) collective-permute-start(f32[8,8,256]{2,1,0:T(8,128)S(1)} %constant_dynamic-update-slice_fusion.16.source_ref), channel_id=1, source_target_pairs={{0,24},{8,16},{16,8},{24,0},{1,25},{9,17},{17,9},{25,1},{2,26},{10... | collective-permute-start | bytes 196616 | tf_op jit(solution)/shard_map/ppermute | solution.py:194
  84.1 0.3 collective-permute-start.28
  84.3 1.2 collective-permute-start.27
  85.5 2.6 %shard_map.92 = (f32[3,256,128]{2,1,0:T(8,128)S(1)}, f32[3,256,128]{2,1,0:T(8,128)S(1)}) custom-call(f32[8,8,256]{2,1,0:T(8,128)S(1)} %constant_dynamic-update-slice_fusion.16.source_ref, f32[8,256]{1,0:T(8,128)S(1)} %shard_map.91.own_ref.refs_3_), custom_call_target="tpu_custom_call" | custom-call | flops 16252928 | bytes 786432 | tf_op jit(solution)/shard_map/pallas_call | solution.py:205
  88.2 7.4 %shard_map.93.own_ref.refs_3_ = f32[8,256]{1,0:T(8,128)S(1)} custom-call(f32[8,8,256]{2,1,0:T(8,128)S(1)} %collective-permute-done.27.refs_0_, f32[8,8,256]{2,1,0:T(8,128)S(1)} %collective-permute-done.28.refs_1_, f32[8,8,256]{2,1,0:T(8,128)S(1)} %collective-permute-done.29.refs_2_, f32[8,256]{1,0:T(8,128)S(1)} %shard_map.91.own_ref.refs_3_, ...), custom_call_target="tpu_custom_call" | custom-call | tf_op jit(solution)/shard_map/pallas_call | solution.py:230
  95.6 5.2 %collective-permute-start.36 = (f32[8,256]{1,0:T(8,128)S(1)}, f32[8,256]{1,0:T(8,128)S(1)}, u32[]{:S(2)}, u32[]{:S(2)}) collective-permute-start(f32[8,256]{1,0:T(8,128)S(1)} %shard_map.93.own_ref.refs_3_), channel_id=1, source_target_pairs={{0,7},{1,6},{2,5},{3,4},{4,3},{5,2},{6,1},{7,0},{8,15},{9,14},{10,... | collective-permute-start | bytes 24584 | tf_op jit(solution)/shard_map/ppermute | solution.py:194
  100.8 0.6 collective-permute-start.34
  101.4 2.1 %collective-permute-start.33 = (f32[8,256]{1,0:T(8,128)S(1)}, f32[8,256]{1,0:T(8,128)S(1)}, u32[]{:S(2)}, u32[]{:S(2)}) collective-permute-start(f32[8,256]{1,0:T(8,128)S(1)} %shard_map.93.own_ref.refs_3_), channel_id=1, source_target_pairs={{0,4},{1,5},{2,6},{3,7},{4,0},{5,1},{6,2},{7,3},{8,12},{9,13},{10,... | collective-permute-start | bytes 24584 | tf_op jit(solution)/shard_map/ppermute | solution.py:194
  103.5 0.3 collective-permute-start.30
  103.9 0.8 collective-permute-done.30
  104.7 0.9 collective-permute-start.31
  105.6 1.6 %collective-permute-done.31 = f32[8,256]{1,0:T(8,128)S(1)} collective-permute-done((f32[8,256]{1,0:T(8,128)S(1)}, f32[8,256]{1,0:T(8,128)S(1)}, u32[]{:S(2)}, u32[]{:S(2)}) %collective-permute-start.31) | collective-permute-done | bytes 8224 | tf_op jit(solution)/shard_map/ppermute | solution.py:194
  107.2 2.2 %collective-permute-start.32 = (f32[8,256]{1,0:T(8,128)S(1)}, f32[8,256]{1,0:T(8,128)S(1)}, u32[]{:S(2)}, u32[]{:S(2)}) collective-permute-start(f32[8,256]{1,0:T(8,128)S(1)} %shard_map.93.own_ref.refs_3_), channel_id=1, source_target_pairs={{0,3},{1,2},{2,1},{3,0},{4,7},{5,6},{6,5},{7,4},{8,11},{9,10},{10,... | collective-permute-start | bytes 24584 | tf_op jit(solution)/shard_map/ppermute | solution.py:194
  109.4 1.3 %collective-permute-done.32 = f32[8,256]{1,0:T(8,128)S(1)} collective-permute-done((f32[8,256]{1,0:T(8,128)S(1)}, f32[8,256]{1,0:T(8,128)S(1)}, u32[]{:S(2)}, u32[]{:S(2)}) %collective-permute-start.32) | collective-permute-done | bytes 8224 | tf_op jit(solution)/shard_map/ppermute | solution.py:194
  110.8 2.2 %collective-permute-start.39 = (f32[8,8,256]{2,1,0:T(8,128)S(1)}, f32[8,8,256]{2,1,0:T(8,128)S(1)}, u32[]{:S(2)}, u32[]{:S(2)}) collective-permute-start(f32[8,8,256]{2,1,0:T(8,128)S(1)} %constant_dynamic-update-slice_fusion.24.source_ref), channel_id=1, source_target_pairs={{0,24},{8,16},{16,8},{24,0},{1,25},{9,17},{17,9},{25,1},{2,26},{10... | collective-permute-start | bytes 196616 | tf_op jit(solution)/shard_map/ppermute | solution.py:194
  113.0 0.3 collective-permute-start.38
  113.3 0.3 collective-permute-start.37
  113.6 2.6 %shard_map.94 = (f32[3,256,128]{2,1,0:T(8,128)S(1)}, f32[3,256,128]{2,1,0:T(8,128)S(1)}) custom-call(f32[8,8,256]{2,1,0:T(8,128)S(1)} %constant_dynamic-update-slice_fusion.24.source_ref, f32[8,256]{1,0:T(8,128)S(1)} %shard_map.93.own_ref.refs_3_), custom_call_target="tpu_custom_call" | custom-call | flops 16252928 | bytes 786432 | tf_op jit(solution)/shard_map/pallas_call | solution.py:205
  116.2 0.6 collective-permute-done.38.refs_1_
  116.8 0.1 collective-permute-done.37.refs_0_
  117.0 7.9 %shard_map.95 = (f32[3,256]{1,0:T(4,128)}, f32[3,256]{1,0:T(4,128)}) custom-call(f32[8,8,256]{2,1,0:T(8,128)S(1)} %collective-permute-done.37.refs_0_, f32[8,8,256]{2,1,0:T(8,128)S(1)} %collective-permute-done.38.refs_1_, f32[8,8,256]{2,1,0:T(8,128)S(1)} %collective-permute-done.39.refs_2_, f32[8,256]{1,0:T(8,128)S(1)} %shard_map.93.own_ref.refs_3_, ...), custom_call_target="tpu_custom_call" | custom-call | tf_op jit(solution)/shard_map/pallas_call | solution.py:238
  (72 shorter events, 0.5 us)
Async XLA Ops:
  0.6 8.4 %copy-start.2 = (f32[3,1280]{1,0:T(4,128)S(1)}, f32[3,1280]{1,0:T(4,128)}, u32[]{:S(2)}) copy-start(f32[3,1280]{1,0:T(4,128)} %bend_ref.1) | copy-start | bytes 46084
  0.7 8.3 %copy-start.3 = (f32[2,1280]{1,0:T(2,128)S(1)}, f32[2,1280]{1,0:T(2,128)}, u32[]{:S(2)}) copy-start(f32[2,1280]{1,0:T(2,128)} %moduli_ref.1) | copy-start | bytes 30724
  1.5 15.0 %collective-permute-start = (f32[8,256]{1,0:T(8,128)S(1)}, f32[8,256]{1,0:T(8,128)S(1)}, u32[]{:S(2)}, u32[]{:S(2)}) collective-permute-start(f32[8,256]{1,0:T(8,128)S(1)} %get-tuple-element.19.own_ref.refs_3_), channel_id=1, source_target_pairs={{0,1},{1,0},{2,3},{3,2},{4,5},{5,4},{6,7},{7,6},{8,9},{9,8},{10,11... | collective-permute-start | bytes 24584 | tf_op jit(solution)/shard_map/ppermute | solution.py:194
  1.6 22.0 %collective-permute-start.6 = (f32[8,256]{1,0:T(8,128)S(1)}, f32[8,256]{1,0:T(8,128)S(1)}, u32[]{:S(2)}, u32[]{:S(2)}) collective-permute-start(f32[8,256]{1,0:T(8,128)S(1)} %get-tuple-element.19.own_ref.refs_3_), channel_id=1, source_target_pairs={{0,7},{1,6},{2,5},{3,4},{4,3},{5,2},{6,1},{7,0},{8,15},{9,14},{10,... | collective-permute-start | bytes 24584 | tf_op jit(solution)/shard_map/ppermute | solution.py:194
  6.3 17.3 %collective-permute-start.5 = (f32[8,256]{1,0:T(8,128)S(1)}, f32[8,256]{1,0:T(8,128)S(1)}, u32[]{:S(2)}, u32[]{:S(2)}) collective-permute-start(f32[8,256]{1,0:T(8,128)S(1)} %get-tuple-element.19.own_ref.refs_3_), channel_id=1, source_target_pairs={{0,6},{1,7},{2,4},{3,5},{4,2},{5,3},{6,0},{7,1},{8,14},{9,15},{10,... | collective-permute-start | bytes 24584 | tf_op jit(solution)/shard_map/ppermute | solution.py:194
  6.4 17.2 %collective-permute-start.4 = (f32[8,256]{1,0:T(8,128)S(1)}, f32[8,256]{1,0:T(8,128)S(1)}, u32[]{:S(2)}, u32[]{:S(2)}) collective-permute-start(f32[8,256]{1,0:T(8,128)S(1)} %get-tuple-element.19.own_ref.refs_3_), channel_id=1, source_target_pairs={{0,5},{1,4},{2,7},{3,6},{4,1},{5,0},{6,3},{7,2},{8,13},{9,12},{10,... | collective-permute-start | bytes 24584 | tf_op jit(solution)/shard_map/ppermute | solution.py:194
  7.4 16.2 %collective-permute-start.3 = (f32[8,256]{1,0:T(8,128)S(1)}, f32[8,256]{1,0:T(8,128)S(1)}, u32[]{:S(2)}, u32[]{:S(2)}) collective-permute-start(f32[8,256]{1,0:T(8,128)S(1)} %get-tuple-element.19.own_ref.refs_3_), channel_id=1, source_target_pairs={{0,4},{1,5},{2,6},{3,7},{4,0},{5,1},{6,2},{7,3},{8,12},{9,13},{10,... | collective-permute-start | bytes 24584 | tf_op jit(solution)/shard_map/ppermute | solution.py:194
  9.1 0.8 copy-start.1
  10.7 18.3 %all-to-all-start = ((f32[32,8,128]{2,1,0:T(8,128)}), f32[32,8,128]{2,1,0:T(8,128)S(1)}, u32[]{:S(2)}, u32[]{:S(2)}) async-start(f32[32,8,128]{2,1,0:T(8,128)} %shard_map.87), calls=%async_computation | async-start | bytes 262144 | tf_op jit(solution)/shard_map/all_to_all | solution.py:219
  16.6 2.9 %collective-permute-start.1 = (f32[8,256]{1,0:T(8,128)S(1)}, f32[8,256]{1,0:T(8,128)S(1)}, u32[]{:S(2)}, u32[]{:S(2)}) collective-permute-start(f32[8,256]{1,0:T(8,128)S(1)} %get-tuple-element.19.own_ref.refs_3_), channel_id=1, source_target_pairs={{0,2},{1,3},{2,0},{3,1},{4,6},{5,7},{6,4},{7,5},{8,10},{9,11},{10,... | collective-permute-start | bytes 24584 | tf_op jit(solution)/shard_map/ppermute | solution.py:194
  19.4 4.1 %collective-permute-start.2 = (f32[8,256]{1,0:T(8,128)S(1)}, f32[8,256]{1,0:T(8,128)S(1)}, u32[]{:S(2)}, u32[]{:S(2)}) collective-permute-start(f32[8,256]{1,0:T(8,128)S(1)} %get-tuple-element.19.own_ref.refs_3_), channel_id=1, source_target_pairs={{0,3},{1,2},{2,1},{3,0},{4,7},{5,6},{6,5},{7,4},{8,11},{9,10},{10,... | collective-permute-start | bytes 24584 | tf_op jit(solution)/shard_map/ppermute | solution.py:194
  23.6 8.5 %collective-permute-start.9 = (f32[8,8,256]{2,1,0:T(8,128)S(1)}, f32[8,8,256]{2,1,0:T(8,128)S(1)}, u32[]{:S(2)}, u32[]{:S(2)}) collective-permute-start(f32[8,8,256]{2,1,0:T(8,128)S(1)} %constant_dynamic-update-slice_fusion.source_ref), channel_id=1, source_target_pairs={{0,24},{8,16},{16,8},{24,0},{1,25},{9,17},{17,9},{25,1},{2,26},{10... | collective-permute-start | bytes 196616 | tf_op jit(solution)/shard_map/ppermute | solution.py:194
  25.8 6.4 %collective-permute-start.8 = (f32[8,8,256]{2,1,0:T(8,128)S(1)}, f32[8,8,256]{2,1,0:T(8,128)S(1)}, u32[]{:S(2)}, u32[]{:S(2)}) collective-permute-start(f32[8,8,256]{2,1,0:T(8,128)S(1)} %constant_dynamic-update-slice_fusion.source_ref), channel_id=1, source_target_pairs={{0,16},{8,24},{16,0},{24,8},{1,17},{9,25},{17,1},{25,9},{2,18},{10... | collective-permute-start | bytes 196616 | tf_op jit(solution)/shard_map/ppermute | solution.py:194
  26.2 5.9 %collective-permute-start.7 = (f32[8,8,256]{2,1,0:T(8,128)S(1)}, f32[8,8,256]{2,1,0:T(8,128)S(1)}, u32[]{:S(2)}, u32[]{:S(2)}) collective-permute-start(f32[8,8,256]{2,1,0:T(8,128)S(1)} %constant_dynamic-update-slice_fusion.source_ref), channel_id=1, source_target_pairs={{0,8},{8,0},{16,24},{24,16},{1,9},{9,1},{17,25},{25,17},{2,10},{10... | collective-permute-start | bytes 196616 | tf_op jit(solution)/shard_map/ppermute | solution.py:194
  28.9 0.7 copy-start.4
  29.6 2.6 %copy-start = (s32[12,256]{1,0:T(8,128)S(1)}, s32[12,256]{1,0:T(8,128)}, u32[]{:S(2)}) copy-start(s32[12,256]{1,0:T(8,128)} %refs_6_.5) | copy-start | bytes 36868
  39.6 14.3 %collective-permute-start.16 = (f32[8,256]{1,0:T(8,128)S(1)}, f32[8,256]{1,0:T(8,128)S(1)}, u32[]{:S(2)}, u32[]{:S(2)}) collective-permute-start(f32[8,256]{1,0:T(8,128)S(1)} %shard_map.89.own_ref.refs_3_), channel_id=1, source_target_pairs={{0,7},{1,6},{2,5},{3,4},{4,3},{5,2},{6,1},{7,0},{8,15},{9,14},{10,... | collective-permute-start | bytes 24584 | tf_op jit(solution)/shard_map/ppermute | solution.py:194
  43.8 10.0 %collective-permute-start.15 = (f32[8,256]{1,0:T(8,128)S(1)}, f32[8,256]{1,0:T(8,128)S(1)}, u32[]{:S(2)}, u32[]{:S(2)}) collective-permute-start(f32[8,256]{1,0:T(8,128)S(1)} %shard_map.89.own_ref.refs_3_), channel_id=1, source_target_pairs={{0,6},{1,7},{2,4},{3,5},{4,2},{5,3},{6,0},{7,1},{8,14},{9,15},{10,... | collective-permute-start | bytes 24584 | tf_op jit(solution)/shard_map/ppermute | solution.py:194
  43.9 10.0 %collective-permute-start.14 = (f32[8,256]{1,0:T(8,128)S(1)}, f32[8,256]{1,0:T(8,128)S(1)}, u32[]{:S(2)}, u32[]{:S(2)}) collective-permute-start(f32[8,256]{1,0:T(8,128)S(1)} %shard_map.89.own_ref.refs_3_), channel_id=1, source_target_pairs={{0,5},{1,4},{2,7},{3,6},{4,1},{5,0},{6,3},{7,2},{8,13},{9,12},{10,... | collective-permute-start | bytes 24584 | tf_op jit(solution)/shard_map/ppermute | solution.py:194
  44.4 9.4 %collective-permute-start.13 = (f32[8,256]{1,0:T(8,128)S(1)}, f32[8,256]{1,0:T(8,128)S(1)}, u32[]{:S(2)}, u32[]{:S(2)}) collective-permute-start(f32[8,256]{1,0:T(8,128)S(1)} %shard_map.89.own_ref.refs_3_), channel_id=1, source_target_pairs={{0,4},{1,5},{2,6},{3,7},{4,0},{5,1},{6,2},{7,3},{8,12},{9,13},{10,... | collective-permute-start | bytes 24584 | tf_op jit(solution)/shard_map/ppermute | solution.py:194
  46.6 1.2 collective-permute-start.10
  47.8 2.5 %collective-permute-start.11 = (f32[8,256]{1,0:T(8,128)S(1)}, f32[8,256]{1,0:T(8,128)S(1)}, u32[]{:S(2)}, u32[]{:S(2)}) collective-permute-start(f32[8,256]{1,0:T(8,128)S(1)} %shard_map.89.own_ref.refs_3_), channel_id=1, source_target_pairs={{0,2},{1,3},{2,0},{3,1},{4,6},{5,7},{6,4},{7,5},{8,10},{9,11},{10,... | collective-permute-start | bytes 24584 | tf_op jit(solution)/shard_map/ppermute | solution.py:194
  50.3 3.6 %collective-permute-start.12 = (f32[8,256]{1,0:T(8,128)S(1)}, f32[8,256]{1,0:T(8,128)S(1)}, u32[]{:S(2)}, u32[]{:S(2)}) collective-permute-start(f32[8,256]{1,0:T(8,128)S(1)} %shard_map.89.own_ref.refs_3_), channel_id=1, source_target_pairs={{0,3},{1,2},{2,1},{3,0},{4,7},{5,6},{6,5},{7,4},{8,11},{9,10},{10,... | collective-permute-start | bytes 24584 | tf_op jit(solution)/shard_map/ppermute | solution.py:194
  53.9 5.3 %collective-permute-start.19 = (f32[8,8,256]{2,1,0:T(8,128)S(1)}, f32[8,8,256]{2,1,0:T(8,128)S(1)}, u32[]{:S(2)}, u32[]{:S(2)}) collective-permute-start(f32[8,8,256]{2,1,0:T(8,128)S(1)} %constant_dynamic-update-slice_fusion.8.source_ref), channel_id=1, source_target_pairs={{0,24},{8,16},{16,8},{24,0},{1,25},{9,17},{17,9},{25,1},{2,26},{10... | collective-permute-start | bytes 196616 | tf_op jit(solution)/shard_map/ppermute | solution.py:194
  56.1 3.8 %collective-permute-start.18 = (f32[8,8,256]{2,1,0:T(8,128)S(1)}, f32[8,8,256]{2,1,0:T(8,128)S(1)}, u32[]{:S(2)}, u32[]{:S(2)}) collective-permute-start(f32[8,8,256]{2,1,0:T(8,128)S(1)} %constant_dynamic-update-slice_fusion.8.source_ref), channel_id=1, source_target_pairs={{0,16},{8,24},{16,0},{24,8},{1,17},{9,25},{17,1},{25,9},{2,18},{10... | collective-permute-start | bytes 196616 | tf_op jit(solution)/shard_map/ppermute | solution.py:194
  56.3 3.7 %collective-permute-start.17 = (f32[8,8,256]{2,1,0:T(8,128)S(1)}, f32[8,8,256]{2,1,0:T(8,128)S(1)}, u32[]{:S(2)}, u32[]{:S(2)}) collective-permute-start(f32[8,8,256]{2,1,0:T(8,128)S(1)} %constant_dynamic-update-slice_fusion.8.source_ref), channel_id=1, source_target_pairs={{0,8},{8,0},{16,24},{24,16},{1,9},{9,1},{17,25},{25,17},{2,10},{10... | collective-permute-start | bytes 196616 | tf_op jit(solution)/shard_map/ppermute | solution.py:194
  67.5 15.4 %collective-permute-start.26 = (f32[8,256]{1,0:T(8,128)S(1)}, f32[8,256]{1,0:T(8,128)S(1)}, u32[]{:S(2)}, u32[]{:S(2)}) collective-permute-start(f32[8,256]{1,0:T(8,128)S(1)} %shard_map.91.own_ref.refs_3_), channel_id=1, source_target_pairs={{0,7},{1,6},{2,5},{3,4},{4,3},{5,2},{6,1},{7,0},{8,15},{9,14},{10,... | collective-permute-start | bytes 24584 | tf_op jit(solution)/shard_map/ppermute | solution.py:194
  72.8 10.0 %collective-permute-start.25 = (f32[8,256]{1,0:T(8,128)S(1)}, f32[8,256]{1,0:T(8,128)S(1)}, u32[]{:S(2)}, u32[]{:S(2)}) collective-permute-start(f32[8,256]{1,0:T(8,128)S(1)} %shard_map.91.own_ref.refs_3_), channel_id=1, source_target_pairs={{0,6},{1,7},{2,4},{3,5},{4,2},{5,3},{6,0},{7,1},{8,14},{9,15},{10,... | collective-permute-start | bytes 24584 | tf_op jit(solution)/shard_map/ppermute | solution.py:194
  72.9 9.8 %collective-permute-start.24 = (f32[8,256]{1,0:T(8,128)S(1)}, f32[8,256]{1,0:T(8,128)S(1)}, u32[]{:S(2)}, u32[]{:S(2)}) collective-permute-start(f32[8,256]{1,0:T(8,128)S(1)} %shard_map.91.own_ref.refs_3_), channel_id=1, source_target_pairs={{0,5},{1,4},{2,7},{3,6},{4,1},{5,0},{6,3},{7,2},{8,13},{9,12},{10,... | collective-permute-start | bytes 24584 | tf_op jit(solution)/shard_map/ppermute | solution.py:194
  72.9 9.8 %collective-permute-start.23 = (f32[8,256]{1,0:T(8,128)S(1)}, f32[8,256]{1,0:T(8,128)S(1)}, u32[]{:S(2)}, u32[]{:S(2)}) collective-permute-start(f32[8,256]{1,0:T(8,128)S(1)} %shard_map.91.own_ref.refs_3_), channel_id=1, source_target_pairs={{0,4},{1,5},{2,6},{3,7},{4,0},{5,1},{6,2},{7,3},{8,12},{9,13},{10,... | collective-permute-start | bytes 24584 | tf_op jit(solution)/shard_map/ppermute | solution.py:194
  75.5 1.3 %collective-permute-start.20 = (f32[8,256]{1,0:T(8,128)S(1)}, f32[8,256]{1,0:T(8,128)S(1)}, u32[]{:S(2)}, u32[]{:S(2)}) collective-permute-start(f32[8,256]{1,0:T(8,128)S(1)} %shard_map.91.own_ref.refs_3_), channel_id=1, source_target_pairs={{0,1},{1,0},{2,3},{3,2},{4,5},{5,4},{6,7},{7,6},{8,9},{9,8},{10,11... | collective-permute-start | bytes 24584 | tf_op jit(solution)/shard_map/ppermute | solution.py:194
  76.8 2.5 %collective-permute-start.21 = (f32[8,256]{1,0:T(8,128)S(1)}, f32[8,256]{1,0:T(8,128)S(1)}, u32[]{:S(2)}, u32[]{:S(2)}) collective-permute-start(f32[8,256]{1,0:T(8,128)S(1)} %shard_map.91.own_ref.refs_3_), channel_id=1, source_target_pairs={{0,2},{1,3},{2,0},{3,1},{4,6},{5,7},{6,4},{7,5},{8,10},{9,11},{10,... | collective-permute-start | bytes 24584 | tf_op jit(solution)/shard_map/ppermute | solution.py:194
  79.3 3.4 %collective-permute-start.22 = (f32[8,256]{1,0:T(8,128)S(1)}, f32[8,256]{1,0:T(8,128)S(1)}, u32[]{:S(2)}, u32[]{:S(2)}) collective-permute-start(f32[8,256]{1,0:T(8,128)S(1)} %shard_map.91.own_ref.refs_3_), channel_id=1, source_target_pairs={{0,3},{1,2},{2,1},{3,0},{4,7},{5,6},{6,5},{7,4},{8,11},{9,10},{10,... | collective-permute-start | bytes 24584 | tf_op jit(solution)/shard_map/ppermute | solution.py:194
  82.8 5.3 %collective-permute-start.29 = (f32[8,8,256]{2,1,0:T(8,128)S(1)}, f32[8,8,256]{2,1,0:T(8,128)S(1)}, u32[]{:S(2)}, u32[]{:S(2)}) collective-permute-start(f32[8,8,256]{2,1,0:T(8,128)S(1)} %constant_dynamic-update-slice_fusion.16.source_ref), channel_id=1, source_target_pairs={{0,24},{8,16},{16,8},{24,0},{1,25},{9,17},{17,9},{25,1},{2,26},{10... | collective-permute-start | bytes 196616 | tf_op jit(solution)/shard_map/ppermute | solution.py:194
  84.1 4.1 %collective-permute-start.28 = (f32[8,8,256]{2,1,0:T(8,128)S(1)}, f32[8,8,256]{2,1,0:T(8,128)S(1)}, u32[]{:S(2)}, u32[]{:S(2)}) collective-permute-start(f32[8,8,256]{2,1,0:T(8,128)S(1)} %constant_dynamic-update-slice_fusion.16.source_ref), channel_id=1, source_target_pairs={{0,16},{8,24},{16,0},{24,8},{1,17},{9,25},{17,1},{25,9},{2,18},{10... | collective-permute-start | bytes 196616 | tf_op jit(solution)/shard_map/ppermute | solution.py:194
  84.3 3.8 %collective-permute-start.27 = (f32[8,8,256]{2,1,0:T(8,128)S(1)}, f32[8,8,256]{2,1,0:T(8,128)S(1)}, u32[]{:S(2)}, u32[]{:S(2)}) collective-permute-start(f32[8,8,256]{2,1,0:T(8,128)S(1)} %constant_dynamic-update-slice_fusion.16.source_ref), channel_id=1, source_target_pairs={{0,8},{8,0},{16,24},{24,16},{1,9},{9,1},{17,25},{25,17},{2,10},{10... | collective-permute-start | bytes 196616 | tf_op jit(solution)/shard_map/ppermute | solution.py:194
  95.6 15.2 %collective-permute-start.36 = (f32[8,256]{1,0:T(8,128)S(1)}, f32[8,256]{1,0:T(8,128)S(1)}, u32[]{:S(2)}, u32[]{:S(2)}) collective-permute-start(f32[8,256]{1,0:T(8,128)S(1)} %shard_map.93.own_ref.refs_3_), channel_id=1, source_target_pairs={{0,7},{1,6},{2,5},{3,4},{4,3},{5,2},{6,1},{7,0},{8,15},{9,14},{10,... | collective-permute-start | bytes 24584 | tf_op jit(solution)/shard_map/ppermute | solution.py:194
  100.8 10.0 %collective-permute-start.35 = (f32[8,256]{1,0:T(8,128)S(1)}, f32[8,256]{1,0:T(8,128)S(1)}, u32[]{:S(2)}, u32[]{:S(2)}) collective-permute-start(f32[8,256]{1,0:T(8,128)S(1)} %shard_map.93.own_ref.refs_3_), channel_id=1, source_target_pairs={{0,6},{1,7},{2,4},{3,5},{4,2},{5,3},{6,0},{7,1},{8,14},{9,15},{10,... | collective-permute-start | bytes 24584 | tf_op jit(solution)/shard_map/ppermute | solution.py:194
  100.8 10.0 %collective-permute-start.34 = (f32[8,256]{1,0:T(8,128)S(1)}, f32[8,256]{1,0:T(8,128)S(1)}, u32[]{:S(2)}, u32[]{:S(2)}) collective-permute-start(f32[8,256]{1,0:T(8,128)S(1)} %shard_map.93.own_ref.refs_3_), channel_id=1, source_target_pairs={{0,5},{1,4},{2,7},{3,6},{4,1},{5,0},{6,3},{7,2},{8,13},{9,12},{10,... | collective-permute-start | bytes 24584 | tf_op jit(solution)/shard_map/ppermute | solution.py:194
  101.4 9.3 %collective-permute-start.33 = (f32[8,256]{1,0:T(8,128)S(1)}, f32[8,256]{1,0:T(8,128)S(1)}, u32[]{:S(2)}, u32[]{:S(2)}) collective-permute-start(f32[8,256]{1,0:T(8,128)S(1)} %shard_map.93.own_ref.refs_3_), channel_id=1, source_target_pairs={{0,4},{1,5},{2,6},{3,7},{4,0},{5,1},{6,2},{7,3},{8,12},{9,13},{10,... | collective-permute-start | bytes 24584 | tf_op jit(solution)/shard_map/ppermute | solution.py:194
  103.5 1.2 collective-permute-start.30
  104.7 2.5 %collective-permute-start.31 = (f32[8,256]{1,0:T(8,128)S(1)}, f32[8,256]{1,0:T(8,128)S(1)}, u32[]{:S(2)}, u32[]{:S(2)}) collective-permute-start(f32[8,256]{1,0:T(8,128)S(1)} %shard_map.93.own_ref.refs_3_), channel_id=1, source_target_pairs={{0,2},{1,3},{2,0},{3,1},{4,6},{5,7},{6,4},{7,5},{8,10},{9,11},{10,... | collective-permute-start | bytes 24584 | tf_op jit(solution)/shard_map/ppermute | solution.py:194
  107.2 3.6 %collective-permute-start.32 = (f32[8,256]{1,0:T(8,128)S(1)}, f32[8,256]{1,0:T(8,128)S(1)}, u32[]{:S(2)}, u32[]{:S(2)}) collective-permute-start(f32[8,256]{1,0:T(8,128)S(1)} %shard_map.93.own_ref.refs_3_), channel_id=1, source_target_pairs={{0,3},{1,2},{2,1},{3,0},{4,7},{5,6},{6,5},{7,4},{8,11},{9,10},{10,... | collective-permute-start | bytes 24584 | tf_op jit(solution)/shard_map/ppermute | solution.py:194
  110.8 5.3 %collective-permute-start.39 = (f32[8,8,256]{2,1,0:T(8,128)S(1)}, f32[8,8,256]{2,1,0:T(8,128)S(1)}, u32[]{:S(2)}, u32[]{:S(2)}) collective-permute-start(f32[8,8,256]{2,1,0:T(8,128)S(1)} %constant_dynamic-update-slice_fusion.24.source_ref), channel_id=1, source_target_pairs={{0,24},{8,16},{16,8},{24,0},{1,25},{9,17},{17,9},{25,1},{2,26},{10... | collective-permute-start | bytes 196616 | tf_op jit(solution)/shard_map/ppermute | solution.py:194
  113.0 3.8 %collective-permute-start.38 = (f32[8,8,256]{2,1,0:T(8,128)S(1)}, f32[8,8,256]{2,1,0:T(8,128)S(1)}, u32[]{:S(2)}, u32[]{:S(2)}) collective-permute-start(f32[8,8,256]{2,1,0:T(8,128)S(1)} %constant_dynamic-update-slice_fusion.24.source_ref), channel_id=1, source_target_pairs={{0,16},{8,24},{16,0},{24,8},{1,17},{9,25},{17,1},{25,9},{2,18},{10... | collective-permute-start | bytes 196616 | tf_op jit(solution)/shard_map/ppermute | solution.py:194
  113.3 3.7 %collective-permute-start.37 = (f32[8,8,256]{2,1,0:T(8,128)S(1)}, f32[8,8,256]{2,1,0:T(8,128)S(1)}, u32[]{:S(2)}, u32[]{:S(2)}) collective-permute-start(f32[8,8,256]{2,1,0:T(8,128)S(1)} %constant_dynamic-update-slice_fusion.24.source_ref), channel_id=1, source_target_pairs={{0,8},{8,0},{16,24},{24,16},{1,9},{9,1},{17,25},{25,17},{2,10},{10... | collective-permute-start | bytes 196616 | tf_op jit(solution)/shard_map/ppermute | solution.py:194

commit v4 on v3

--- a/solution.py
+++ b/solution.py
@@ -188,14 +188,12 @@
         velocity_ref[c : c + 1, :] = velocity[c]
 
 
-def exchange(block, axis):
-    size = lax.axis_size(axis)
-    return [
-        lax.ppermute(
-            block, axis, [(i, (i + shift) % size if size & (size - 1) else i ^ shift) for i in range(size)]
-        )
-        for shift in range(1, size)
-    ]
+def spread(state, devices):
+    parities = [list(range(parity, devices, 2)) for parity in range(2)]
+    copies = jnp.broadcast_to(state[None], (devices // 2,) + state.shape)
+    near = lax.all_to_all(copies, AXES, split_axis=0, concat_axis=0, axis_index_groups=parities, tiled=True)
+    far = lax.ppermute(near, AXES, [(i, i ^ 1) for i in range(devices)])
+    return near, far
 
 
 def near_sums(near, state):
@@ -216,33 +214,33 @@
     devices = lax.axis_size("tgt") * lax.axis_size("src")
     nodes = positions.shape[1]
     scale = 1.0 / math.sqrt(devices * nodes)
-    slots = lax.all_to_all(
-        pack_slots(rest_length, moduli, rest_bend, devices), AXES, split_axis=0, concat_axis=0, tiled=True
-    )
     state = jnp.concatenate([positions, forces, jnp.zeros((ROWS - 6, nodes), jnp.float32)], axis=0)
-    params = pick_slots(slots, patch_owner.reshape(1, nodes), rest_length.shape[1] // devices)
     sums = [pltpu.VMEM((3, nodes, LANES), jnp.float32)]
     for step in range(STEPS + 1):
-        near = jnp.stack([state] + exchange(state, "src"))
-        far = exchange(near, "tgt")
+        near, far = spread(state, devices)
+        if step == 0:
+            packed = pack_slots(rest_length, moduli, rest_bend, devices)
+            near, far, packed = lax.optimization_barrier((near, far, packed))
+            slots = lax.all_to_all(packed, AXES, split_axis=0, concat_axis=0, tiled=True)
+            params = pick_slots(slots, patch_owner.reshape(1, nodes), rest_length.shape[1] // devices)
         column, start = near_sums(near, state)
         if step < STEPS:
             state = pl.pallas_call(
-                functools.partial(step_kernel, len(far), scale),
+                functools.partial(step_kernel, 1, scale),
                 out_shape=jax.ShapeDtypeStruct((ROWS, nodes), jnp.float32),
-                in_specs=[VMEM] * (len(far) + 5),
+                in_specs=[VMEM] * (6),
                 out_specs=VMEM,
                 scratch_shapes=sums,
                 compiler_params=GRANT,
-            )(*far, state, column, start, neighbours, params)
-    return pl.pallas_call(
-        functools.partial(last_kernel, len(far), scale),
+            )(far, state, column, start, neighbours, params)
+    return pl.pallas_call(
+        functools.partial(last_kernel, 1, scale),
         out_shape=(jax.ShapeDtypeStruct((3, nodes), jnp.float32),) * 2,
-        in_specs=[VMEM] * (len(far) + 3),
+        in_specs=[VMEM] * (4),
         out_specs=(VMEM,) * 2,
         scratch_shapes=sums,
         compiler_params=GRANT,
-    )(*far, state, column, start)
+    )(far, state, column, start)
 
 
 def solution(mesh):

time: 127 us -> 103 us (0.81); the launches traced: 125 us -> 103 us
  starting transfers between devices: 61.3 us -> 10.3 us
  blocking collectives: 0 us -> 43 us
  waiting for transfers between devices: 16.2 us -> 3.51 us
  local copies, waits for them, and re-layouts: 1.6 us -> 0.15 us
    ppermute x40 -> x4, starting transfers between devices: 55.5 us -> 7.78 us  [spread(): far = lax.ppermute(near, AXES, [(i, i ^ 1) for i in range(devices)])]
    all_to_all x0 -> x4, blocking collectives: none -> 43 us  [spread(): lax.all_to_all(copies, AXES, split_axis=0, concat_axis=0, axis_index_grou...]
    ppermute x40 -> x4, waiting for transfers between devices: 16.2 us -> 0.15 us  [spread(): far = lax.ppermute(near, AXES, [(i, i ^ 1) for i in range(devices)])]
    pallas_call x4, Pallas kernels: 10.4 us -> 20.1 us  [near_sums(): pl.pallas_call(near_kernel, out_shape=(shape, shape), in_specs=[VMEM] * 2...]
    pallas_call x4, Pallas kernels: 30.1 us -> 20.9 us  [the longest x3 15.3 us: body(): pl.pallas_call(functools.partial(step_kernel, 1, scale), out_shape=jax.Sh...]
    all_to_all x1, waiting for transfers between devices: 0.01 us -> 3.37 us  [body(): lax.all_to_all(packed, AXES, split_axis=0, concat_axis=0, tiled=True)]
    all_to_all x1, starting transfers between devices: 5.86 us -> 2.53 us  [body(): lax.all_to_all(packed, AXES, split_axis=0, concat_axis=0, tiled=True)]
    unnamed x37 -> x10, local copies, waits for them, and re-layouts: 1.51 us -> 0.03 us
  transfers between devices with their start and end apart: 41 -> 5, of which waited for: 16 -> 2; matrix products, arithmetic and copies ran while one was open for 0% -> 0% of each run, Pallas kernels for 11% -> 20%
where the time goes in v4:
time: 103 us
  Pallas kernels  44.3 us (43%)
  blocking collectives  43 us (42%)
  starting transfers between devices  10.3 us (10%)
  waiting for transfers between devices  3.51 us (3%)
    all_to_all x4, blocking collectives, spread(): lax.all_to_all(copies, AXES, split_axis=0, concat_axis=0, axis_index_grou...  43 us
    pallas_call x4, Pallas kernels, near_sums(): pl.pallas_call(near_kernel, out_shape=(shape, shape), in_specs=[VMEM] * 2...  20.1 us
    pallas_call x3, Pallas kernels, body(): pl.pallas_call(functools.partial(step_kernel, 1, scale), out_shape=jax.Sh...  15.3 us
    ppermute x4, starting transfers between devices, spread(): far = lax.ppermute(near, AXES, [(i, i ^ 1) for i in range(devices)])  7.78 us
    pallas_call x1, Pallas kernels, body(): pl.pallas_call(functools.partial(last_kernel, 1, scale), out_shape=(jax.S...  5.57 us
    all_to_all x1, waiting for transfers between devices, body(): lax.all_to_all(packed, AXES, split_axis=0, concat_axis=0, tiled=True)  3.37 us
    all_to_all x1, starting transfers between devices, body(): lax.all_to_all(packed, AXES, split_axis=0, concat_axis=0, tiled=True)  2.53 us
    pallas_call x1, Pallas kernels, pick_slots(): pl.pallas_call(functools.partial(pick_kernel, capacity), out_shape=jax.Sh...  2.47 us
  transfers between devices with their start and end apart: 5, of which 2 were waited for; matrix products, arithmetic and copies ran while one was open for 0% of the time, Pallas kernels for 20%

profile of v4, /device:TPU:1, one launch (start us, length us, event | category | flops | bytes accessed | tf_op | source)
XLA Modules:
  0.0 102.9 jit_solution(15109832957464566710)
XLA Ops:
  0.6 0.1 pad.2.clone
  0.7 0.8 maximum_maximum_fusion.own_ref.refs_1_
  1.5 0.0 copy-start.1
  1.5 0.0 copy-start.2
  1.5 0.0 copy-start.3
  1.5 13.8 %all_to_all.25.source_ref = f32[16,8,256]{2,1,0:T(8,128)S(1)} all-to-all(f32[16,8,256]{2,1,0:T(8,128)S(1)} %broadcast_in_dim.11), channel_id=1, replica_groups={{0,2,4,6,8,10,12,14,16,18,20,22,24,26,28,30},{1,3,5,7,9,11,13,15,17,19,..., dimensions={0} | all-to-all | bytes 262144 | tf_op jit(solution)/shard_map/all_to_all | solution.py:194
  15.4 2.2 %collective-permute-start = (f32[16,8,256]{2,1,0:T(8,128)S(1)}, f32[16,8,256]{2,1,0:T(8,128)S(1)}, u32[]{:S(2)}, u32[]{:S(2)}) collective-permute-start(f32[16,8,256]{2,1,0:T(8,128)S(1)} %all_to_all.25.source_ref), channel_id=1, source_target_pairs={{0,1},{1,0},{2,3},{3,2},{4,5},{5,4},{6,7},{7,6},{8,9},{9,8},{10,11... | collective-permute-start | bytes 393224 | tf_op jit(solution)/shard_map/ppermute | solution.py:195
  17.5 0.0 copy-done.1
  17.5 0.0 copy-done.2
  17.5 0.0 copy-done.3
  17.5 0.8 shard_map.86
  18.4 0.1 collective-permute-done.refs_0_
  18.5 2.5 %all-to-all-start.1 = ((f32[32,8,128]{2,1,0:T(8,128)}), f32[32,8,128]{2,1,0:T(8,128)S(1)}, u32[]{:S(2)}, u32[]{:S(2)}) async-start(f32[32,8,128]{2,1,0:T(8,128)} %shard_map.86), calls=%async_computation.1 | async-start | bytes 262144 | tf_op jit(solution)/shard_map/all_to_all | solution.py:224
  21.1 5.0 %shard_map.87 = (f32[3,256,128]{2,1,0:T(8,128)S(1)}, f32[3,256,128]{2,1,0:T(8,128)S(1)}) custom-call(f32[16,8,256]{2,1,0:T(8,128)S(1)} %all_to_all.25.source_ref, f32[8,256]{1,0:T(8,128)S(1)} %maximum_maximum_fusion.own_ref.refs_1_), custom_call_target="tpu_custom_call" | custom-call | flops 32505856 | bytes 786432 | tf_op jit(solution)/shard_map/pallas_call | solution.py:203
  26.1 0.0 copy-start.4
  26.1 3.4 %all-to-all-done.1.slots_ref = f32[32,8,128]{2,1,0:T(8,128)S(1)} async-done(((f32[32,8,128]{2,1,0:T(8,128)}), f32[32,8,128]{2,1,0:T(8,128)S(1)}, u32[]{:S(2)}, u32[]{:S(2)}) %all-to-all-start.1) | async-done | bytes 131104 | tf_op jit(solution)/shard_map/all_to_all | solution.py:224
  29.4 0.0 copy-done.4
  29.4 0.0 copy-start
  29.4 2.5 %shard_map.88.refs_5_ = f32[16,256]{1,0:T(8,128)S(1)} custom-call(f32[32,8,128]{2,1,0:T(8,128)S(1)} %all-to-all-done.1.slots_ref, s32[1,256]{1,0:T(1,128)S(1)} %bitcast.1), custom_call_target="tpu_custom_call" | custom-call | tf_op jit(solution)/shard_map/pallas_call | solution.py:73
  31.9 0.0 copy-done
  31.9 5.1 %shard_map.89.own_ref.refs_1_ = f32[8,256]{1,0:T(8,128)S(1)} custom-call(f32[16,8,256]{2,1,0:T(8,128)S(1)} %collective-permute-done.refs_0_, f32[8,256]{1,0:T(8,128)S(1)} %maximum_maximum_fusion.own_ref.refs_1_, f32[3,256,128]{2,1,0:T(8,128)S(1)} %get-tuple-element.15.refs_2_, f32[3,256,128]{2,1,0:T(8,128)S(1)} %get-tuple-element.16.refs_3_, ...), custom_call_target="tpu_custom_call" | custom-call | tf_op jit(solution)/shard_map/pallas_call | solution.py:228
  37.1 10.2 %all_to_all.26.source_ref = f32[16,8,256]{2,1,0:T(8,128)S(1)} all-to-all(f32[16,8,256]{2,1,0:T(8,128)S(1)} %broadcast_in_dim.12), channel_id=1, replica_groups={{0,2,4,6,8,10,12,14,16,18,20,22,24,26,28,30},{1,3,5,7,9,11,13,15,17,19,..., dimensions={0} | all-to-all | bytes 262144 | tf_op jit(solution)/shard_map/all_to_all | solution.py:194
  47.3 2.3 %collective-permute-start.1 = (f32[16,8,256]{2,1,0:T(8,128)S(1)}, f32[16,8,256]{2,1,0:T(8,128)S(1)}, u32[]{:S(2)}, u32[]{:S(2)}) collective-permute-start(f32[16,8,256]{2,1,0:T(8,128)S(1)} %all_to_all.26.source_ref), channel_id=1, source_target_pairs={{0,1},{1,0},{2,3},{3,2},{4,5},{5,4},{6,7},{7,6},{8,9},{9,8},{10,11... | collective-permute-start | bytes 393224 | tf_op jit(solution)/shard_map/ppermute | solution.py:195
  49.6 5.0 %shard_map.90 = (f32[3,256,128]{2,1,0:T(8,128)S(1)}, f32[3,256,128]{2,1,0:T(8,128)S(1)}) custom-call(f32[16,8,256]{2,1,0:T(8,128)S(1)} %all_to_all.26.source_ref, f32[8,256]{1,0:T(8,128)S(1)} %shard_map.89.own_ref.refs_1_), custom_call_target="tpu_custom_call" | custom-call | flops 32505856 | bytes 786432 | tf_op jit(solution)/shard_map/pallas_call | solution.py:203
  54.7 0.0 collective-permute-done.1.refs_0_
  54.7 5.1 %shard_map.91.own_ref.refs_1_ = f32[8,256]{1,0:T(8,128)S(1)} custom-call(f32[16,8,256]{2,1,0:T(8,128)S(1)} %collective-permute-done.1.refs_0_, f32[8,256]{1,0:T(8,128)S(1)} %shard_map.89.own_ref.refs_1_, f32[3,256,128]{2,1,0:T(8,128)S(1)} %get-tuple-element.18.refs_2_, f32[3,256,128]{2,1,0:T(8,128)S(1)} %get-tuple-element.19.refs_3_, s32[12,256]{1,0:T(8,128)S(1)} %copy-done, ...), custom_call_target="tpu_custom_call" | custom-call | tf_op jit(solution)/shard_map/pallas_call | solution.py:228
  59.8 9.7 %all_to_all.27.source_ref = f32[16,8,256]{2,1,0:T(8,128)S(1)} all-to-all(f32[16,8,256]{2,1,0:T(8,128)S(1)} %broadcast_in_dim.13), channel_id=1, replica_groups={{0,2,4,6,8,10,12,14,16,18,20,22,24,26,28,30},{1,3,5,7,9,11,13,15,17,19,..., dimensions={0} | all-to-all | bytes 262144 | tf_op jit(solution)/shard_map/all_to_all | solution.py:194
  69.5 1.2 %collective-permute-start.2 = (f32[16,8,256]{2,1,0:T(8,128)S(1)}, f32[16,8,256]{2,1,0:T(8,128)S(1)}, u32[]{:S(2)}, u32[]{:S(2)}) collective-permute-start(f32[16,8,256]{2,1,0:T(8,128)S(1)} %all_to_all.27.source_ref), channel_id=1, source_target_pairs={{0,1},{1,0},{2,3},{3,2},{4,5},{5,4},{6,7},{7,6},{8,9},{9,8},{10,11... | collective-permute-start | bytes 393224 | tf_op jit(solution)/shard_map/ppermute | solution.py:195
  70.8 5.0 %shard_map.92 = (f32[3,256,128]{2,1,0:T(8,128)S(1)}, f32[3,256,128]{2,1,0:T(8,128)S(1)}) custom-call(f32[16,8,256]{2,1,0:T(8,128)S(1)} %all_to_all.27.source_ref, f32[8,256]{1,0:T(8,128)S(1)} %shard_map.91.own_ref.refs_1_), custom_call_target="tpu_custom_call" | custom-call | flops 32505856 | bytes 786432 | tf_op jit(solution)/shard_map/pallas_call | solution.py:203
  75.8 0.0 collective-permute-done.2.refs_0_
  75.8 5.1 %shard_map.93.own_ref.refs_1_ = f32[8,256]{1,0:T(8,128)S(1)} custom-call(f32[16,8,256]{2,1,0:T(8,128)S(1)} %collective-permute-done.2.refs_0_, f32[8,256]{1,0:T(8,128)S(1)} %shard_map.91.own_ref.refs_1_, f32[3,256,128]{2,1,0:T(8,128)S(1)} %get-tuple-element.20.refs_2_, f32[3,256,128]{2,1,0:T(8,128)S(1)} %get-tuple-element.21.refs_3_, s32[12,256]{1,0:T(8,128)S(1)} %copy-done, ...), custom_call_target="tpu_custom_call" | custom-call | tf_op jit(solution)/shard_map/pallas_call | solution.py:228
  80.9 9.3 %all_to_all.28.source_ref = f32[16,8,256]{2,1,0:T(8,128)S(1)} all-to-all(f32[16,8,256]{2,1,0:T(8,128)S(1)} %broadcast_in_dim.14), channel_id=1, replica_groups={{0,2,4,6,8,10,12,14,16,18,20,22,24,26,28,30},{1,3,5,7,9,11,13,15,17,19,..., dimensions={0} | all-to-all | bytes 262144 | tf_op jit(solution)/shard_map/all_to_all | solution.py:194
  90.2 2.0 %collective-permute-start.3 = (f32[16,8,256]{2,1,0:T(8,128)S(1)}, f32[16,8,256]{2,1,0:T(8,128)S(1)}, u32[]{:S(2)}, u32[]{:S(2)}) collective-permute-start(f32[16,8,256]{2,1,0:T(8,128)S(1)} %all_to_all.28.source_ref), channel_id=1, source_target_pairs={{0,1},{1,0},{2,3},{3,2},{4,5},{5,4},{6,7},{7,6},{8,9},{9,8},{10,11... | collective-permute-start | bytes 393224 | tf_op jit(solution)/shard_map/ppermute | solution.py:195
  92.2 5.0 %shard_map.94 = (f32[3,256,128]{2,1,0:T(8,128)S(1)}, f32[3,256,128]{2,1,0:T(8,128)S(1)}) custom-call(f32[16,8,256]{2,1,0:T(8,128)S(1)} %all_to_all.28.source_ref, f32[8,256]{1,0:T(8,128)S(1)} %shard_map.93.own_ref.refs_1_), custom_call_target="tpu_custom_call" | custom-call | flops 32505856 | bytes 786432 | tf_op jit(solution)/shard_map/pallas_call | solution.py:203
  97.3 0.0 collective-permute-done.3.refs_0_
  97.3 5.6 %shard_map.95 = (f32[3,256]{1,0:T(4,128)}, f32[3,256]{1,0:T(4,128)}) custom-call(f32[16,8,256]{2,1,0:T(8,128)S(1)} %collective-permute-done.3.refs_0_, f32[8,256]{1,0:T(8,128)S(1)} %shard_map.93.own_ref.refs_1_, f32[3,256,128]{2,1,0:T(8,128)S(1)} %get-tuple-element.22.refs_2_, f32[3,256,128]{2,1,0:T(8,128)S(1)} %get-tuple-element.23.refs_3_), custom_call_target="tpu_custom_call" | custom-call | tf_op jit(solution)/shard_map/pallas_call | solution.py:236
  (5 shorter events, 0.0 us)
Async XLA Ops:
  1.5 16.0 %copy-start.1 = (f32[6,1280]{1,0:T(8,128)S(1)}, f32[6,1280]{1,0:T(8,128)}, u32[]{:S(2)}) copy-start(f32[6,1280]{1,0:T(8,128)} %length_ref.1) | copy-start | bytes 92164
  1.5 16.0 %copy-start.2 = (f32[3,1280]{1,0:T(4,128)S(1)}, f32[3,1280]{1,0:T(4,128)}, u32[]{:S(2)}) copy-start(f32[3,1280]{1,0:T(4,128)} %bend_ref.1) | copy-start | bytes 46084
  1.5 16.0 %copy-start.3 = (f32[2,1280]{1,0:T(2,128)S(1)}, f32[2,1280]{1,0:T(2,128)}, u32[]{:S(2)}) copy-start(f32[2,1280]{1,0:T(2,128)} %moduli_ref.1) | copy-start | bytes 30724
  15.4 3.2 %collective-permute-start = (f32[16,8,256]{2,1,0:T(8,128)S(1)}, f32[16,8,256]{2,1,0:T(8,128)S(1)}, u32[]{:S(2)}, u32[]{:S(2)}) collective-permute-start(f32[16,8,256]{2,1,0:T(8,128)S(1)} %all_to_all.25.source_ref), channel_id=1, source_target_pairs={{0,1},{1,0},{2,3},{3,2},{4,5},{5,4},{6,7},{7,6},{8,9},{9,8},{10,11... | collective-permute-start | bytes 393224 | tf_op jit(solution)/shard_map/ppermute | solution.py:195
  18.5 10.9 %all-to-all-start.1 = ((f32[32,8,128]{2,1,0:T(8,128)}), f32[32,8,128]{2,1,0:T(8,128)S(1)}, u32[]{:S(2)}, u32[]{:S(2)}) async-start(f32[32,8,128]{2,1,0:T(8,128)} %shard_map.86), calls=%async_computation.1 | async-start | bytes 262144 | tf_op jit(solution)/shard_map/all_to_all | solution.py:224
  26.1 3.4 %copy-start.4 = (s32[256,1]{0,1:T(1,128)S(1)}, s32[256,1]{0,1:T(1,128)}, u32[]{:S(2)}) copy-start(s32[256,1]{0,1:T(1,128)} %param.10) | copy-start | bytes 3076
  29.4 2.5 %copy-start = (s32[12,256]{1,0:T(8,128)S(1)}, s32[12,256]{1,0:T(8,128)}, u32[]{:S(2)}) copy-start(s32[12,256]{1,0:T(8,128)} %refs_4_.5) | copy-start | bytes 36868
  47.3 7.4 %collective-permute-start.1 = (f32[16,8,256]{2,1,0:T(8,128)S(1)}, f32[16,8,256]{2,1,0:T(8,128)S(1)}, u32[]{:S(2)}, u32[]{:S(2)}) collective-permute-start(f32[16,8,256]{2,1,0:T(8,128)S(1)} %all_to_all.26.source_ref), channel_id=1, source_target_pairs={{0,1},{1,0},{2,3},{3,2},{4,5},{5,4},{6,7},{7,6},{8,9},{9,8},{10,11... | collective-permute-start | bytes 393224 | tf_op jit(solution)/shard_map/ppermute | solution.py:195
  69.5 6.3 %collective-permute-start.2 = (f32[16,8,256]{2,1,0:T(8,128)S(1)}, f32[16,8,256]{2,1,0:T(8,128)S(1)}, u32[]{:S(2)}, u32[]{:S(2)}) collective-permute-start(f32[16,8,256]{2,1,0:T(8,128)S(1)} %all_to_all.27.source_ref), channel_id=1, source_target_pairs={{0,1},{1,0},{2,3},{3,2},{4,5},{5,4},{6,7},{7,6},{8,9},{9,8},{10,11... | collective-permute-start | bytes 393224 | tf_op jit(solution)/shard_map/ppermute | solution.py:195
  90.2 7.1 %collective-permute-start.3 = (f32[16,8,256]{2,1,0:T(8,128)S(1)}, f32[16,8,256]{2,1,0:T(8,128)S(1)}, u32[]{:S(2)}, u32[]{:S(2)}) collective-permute-start(f32[16,8,256]{2,1,0:T(8,128)S(1)} %all_to_all.28.source_ref), channel_id=1, source_target_pairs={{0,1},{1,0},{2,3},{3,2},{4,5},{5,4},{6,7},{7,6},{8,9},{9,8},{10,11... | collective-permute-start | bytes 393224 | tf_op jit(solution)/shard_map/ppermute | solution.py:195

commit v5 on v3

--- a/solution.py
+++ b/solution.py
@@ -111,7 +111,7 @@
                     totals = tuple(totals[c] + (direct * f[c] + along * d[c]) for c in range(3))
                 return totals
 
-            totals = lax.fori_loop(0, source_ref.shape[0], per_source, totals, unroll=2)
+            totals = lax.fori_loop(0, source_ref.shape[0], per_source, totals, unroll=min(2, source_ref.shape[0]))
         for c in range(3):
             sum_ref[c, rows, :] = totals[c]
         return 0
@@ -162,87 +162,85 @@
     return [jnp.concatenate(parts, axis=1) for parts in force]
 
 
-def near_kernel(source_ref, own_ref, column_ref, sum_ref):
-    spread_columns(own_ref, column_ref)
+def first_kernel(source_ref, column_ref, sum_ref):
+    spread_columns(source_ref.at[0], column_ref)
     pair_sums([source_ref], column_ref, None, sum_ref)
 
 
-def step_kernel(others, scale, *refs):
-    own_ref, column_ref, start_ref, neighbours_ref, params_ref, out_ref, sum_ref = refs[others:]
-    pair_sums(refs[:others], column_ref, start_ref, sum_ref)
+def more_kernel(source_ref, column_ref, start_ref, sum_ref):
+    pair_sums([source_ref], column_ref, start_ref, sum_ref)
+
+
+def step_kernel(scale, source_ref, own_ref, column_ref, start_ref, neighbours_ref, params_ref, out_ref, sum_ref):
+    pair_sums([source_ref], column_ref, start_ref, sum_ref)
     velocity = velocity_rows(sum_ref, scale)
-    x = [own_ref[c : c + 1, :] + time_step * velocity[c] for c in range(3)]
+    x = [own_ref[0, c : c + 1, :] + time_step * velocity[c] for c in range(3)]
     force = membrane(x, neighbours_ref, params_ref)
     for c in range(3):
-        out_ref[c : c + 1, :] = x[c]
-        out_ref[3 + c : 4 + c, :] = force[c]
-    out_ref[6:ROWS, :] = jnp.zeros((ROWS - 6, x[0].shape[1]), jnp.float32)
-
-
-def last_kernel(others, scale, *refs):
-    own_ref, column_ref, start_ref, position_ref, velocity_ref, sum_ref = refs[others:]
-    pair_sums(refs[:others], column_ref, start_ref, sum_ref)
+        out_ref[0, c : c + 1, :] = x[c]
+        out_ref[0, 3 + c : 4 + c, :] = force[c]
+    out_ref[0, 6:ROWS, :] = jnp.zeros((ROWS - 6, x[0].shape[1]), jnp.float32)
+
+
+def last_kernel(scale, source_ref, own_ref, column_ref, start_ref, position_ref, velocity_ref, sum_ref):
+    pair_sums([source_ref], column_ref, start_ref, sum_ref)
     velocity = velocity_rows(sum_ref, scale)
-    position_ref[...] = own_ref[0:3, :]
+    position_ref[...] = own_ref[0, 0:3, :]
     for c in range(3):
         velocity_ref[c : c + 1, :] = velocity[c]
 
 
-def exchange(block, axis):
-    size = lax.axis_size(axis)
-    return [
-        lax.ppermute(
-            block, axis, [(i, (i + shift) % size if size & (size - 1) else i ^ shift) for i in range(size)]
-        )
-        for shift in range(1, size)
-    ]
-
-
-def near_sums(near, state):
-    nodes = state.shape[1]
-    shape = jax.ShapeDtypeStruct((3, nodes, LANES), jnp.float32)
-    pairs = near.shape[0] * nodes * nodes
+def call(kernel, out_shape, operands, sources, scratch=()):
+    nodes = sources.shape[2]
+    pairs = sources.shape[0] * nodes * nodes
     return pl.pallas_call(
-        near_kernel,
-        out_shape=(shape, shape),
-        in_specs=[VMEM] * 2,
-        out_specs=(VMEM,) * 2,
+        kernel,
+        out_shape=out_shape,
+        in_specs=[VMEM] * len(operands),
+        out_specs=jax.tree.map(lambda _: VMEM, out_shape),
+        scratch_shapes=scratch,
         compiler_params=GRANT,
         cost_estimate=pl.CostEstimate(flops=31 * pairs, bytes_accessed=8 * 3 * nodes * LANES, transcendentals=pairs),
-    )(near, state)
+    )(*operands)
+
+
+def exchange_order(devices):
+    return [1 << bit for bit in range(1, devices.bit_length() - 1)] + [1]
 
 
 def body(positions, forces, neighbours, patch_owner, rest_length, moduli, rest_bend):
     devices = lax.axis_size("tgt") * lax.axis_size("src")
     nodes = positions.shape[1]
     scale = 1.0 / math.sqrt(devices * nodes)
+    sums = jax.ShapeDtypeStruct((3, nodes, LANES), jnp.float32)
+    row = jax.ShapeDtypeStruct((3, nodes), jnp.float32)
     slots = lax.all_to_all(
         pack_slots(rest_length, moduli, rest_bend, devices), AXES, split_axis=0, concat_axis=0, tiled=True
     )
-    state = jnp.concatenate([positions, forces, jnp.zeros((ROWS - 6, nodes), jnp.float32)], axis=0)
     params = pick_slots(slots, patch_owner.reshape(1, nodes), rest_length.shape[1] // devices)
-    sums = [pltpu.VMEM((3, nodes, LANES), jnp.float32)]
+    state = jnp.concatenate([positions, forces, jnp.zeros((ROWS - 6, nodes), jnp.float32)], axis=0)[None]
+    scratch = [pltpu.VMEM(sums.shape, jnp.float32)]
     for step in range(STEPS + 1):
-        near = jnp.stack([state] + exchange(state, "src"))
-        far = exchange(near, "tgt")
-        column, start = near_sums(near, state)
+        held = newest = state
+        column = total = None
+        for distance in exchange_order(devices):
+            arriving = lax.ppermute(held, AXES, [(i, i ^ distance) for i in range(devices)])
+            if total is None:
+                column, total = call(first_kernel, (sums, sums), (newest,), newest)
+            else:
+                total = call(more_kernel, sums, (newest, column, total), newest)
+            arriving, total = lax.optimization_barrier((arriving, total))
+            held = jnp.concatenate([held, arriving], axis=0)
+            newest = arriving
         if step < STEPS:
-            state = pl.pallas_call(
-                functools.partial(step_kernel, len(far), scale),
-                out_shape=jax.ShapeDtypeStruct((ROWS, nodes), jnp.float32),
-                in_specs=[VMEM] * (len(far) + 5),
-                out_specs=VMEM,
-                scratch_shapes=sums,
-                compiler_params=GRANT,
-            )(*far, state, column, start, neighbours, params)
-    return pl.pallas_call(
-        functools.partial(last_kernel, len(far), scale),
-        out_shape=(jax.ShapeDtypeStruct((3, nodes), jnp.float32),) * 2,
-        in_specs=[VMEM] * (len(far) + 3),
-        out_specs=(VMEM,) * 2,
-        scratch_shapes=sums,
-        compiler_params=GRANT,
-    )(*far, state, column, start)
+            state = call(
+                functools.partial(step_kernel, scale),
+                jax.ShapeDtypeStruct((1, ROWS, nodes), jnp.float32),
+                (newest, state, column, total, neighbours, params),
+                newest,
+                scratch,
+            )
+    return call(functools.partial(last_kernel, scale), (row, row), (newest, state, column, total), newest, scratch)
 
 
 def solution(mesh):

time: 127 us -> 115 us (0.906); the launches traced: 125 us -> 114 us
  starting transfers between devices: 61.3 us -> 39.2 us
  waiting for transfers between devices: 16.2 us -> 27.2 us
    ppermute x40 -> x20, starting transfers between devices: 55.5 us -> 33.7 us  [body(): lax.ppermute(held, AXES, [(i, i ^ distance) for i in range(devices)])]
    ppermute x40 -> x20, waiting for transfers between devices: 16.2 us -> 27.2 us  [body(): lax.ppermute(held, AXES, [(i, i ^ distance) for i in range(devices)])]
    pallas_call x8 -> x24, Pallas kernels: 40.6 us -> 41.2 us  [call(): pl.pallas_call(kernel, out_shape=out_shape, in_specs=[VMEM] * len(operand...]
  transfers between devices with their start and end apart: 41 -> 21, of which waited for: 16 -> 15; matrix products, arithmetic and copies ran while one was open for 0% -> 0% of each run, Pallas kernels for 11% -> 15%
where the time goes in v5:
time: 115 us; the launch traced here: 114 us
  Pallas kernels  44.5 us (39%)
  starting transfers between devices  39.2 us (34%)
  waiting for transfers between devices  27.2 us (24%)
  local copies, waits for them, and re-layouts  1.58 us (1%)
    pallas_call x24, Pallas kernels, call(): pl.pallas_call(kernel, out_shape=out_shape, in_specs=[VMEM] * len(operand...  41.2 us
    ppermute x20, starting transfers between devices, body(): lax.ppermute(held, AXES, [(i, i ^ distance) for i in range(devices)])  33.7 us
    ppermute x20, waiting for transfers between devices, body(): lax.ppermute(held, AXES, [(i, i ^ distance) for i in range(devices)])  27.2 us
    all_to_all x1, starting transfers between devices, body(): lax.all_to_all(pack_slots(rest_length, moduli, rest_bend, devices), AXES,...  5.53 us
    pallas_call x1, Pallas kernels, pick_slots(): pl.pallas_call(functools.partial(pick_kernel, capacity), out_shape=jax.Sh...  2.46 us
  transfers between devices with their start and end apart: 21, of which 15 were waited for; matrix products, arithmetic and copies ran while one was open for 0% of the time, Pallas kernels for 15%

profile of v5, /device:TPU:1, one launch (start us, length us, event | category | flops | bytes accessed | tf_op | source)
XLA Modules:
  0.0 114.2 jit_solution(9446295035454356956)
XLA Ops:
  0.7 0.8 constant_dynamic-update-slice_fusion.4
  1.5 2.1 %collective-permute-start = (f32[1,8,256]{2,1,0:T(8,128)S(1)}, f32[1,8,256]{2,1,0:T(8,128)S(1)}, u32[]{:S(2)}, u32[]{:S(2)}) collective-permute-start(f32[1,8,256]{2,1,0:T(8,128)S(1)} %get-tuple-element.99.source_ref.own_ref), channel_id=1, source_target_pairs={{0,2},{1,3},{2,0},{3,1},{4,6},{5,7},{6,4},{7,5},{8,10},{9,11},{10,... | collective-permute-start | bytes 24584 | tf_op jit(solution)/shard_map/ppermute | solution.py:227
  3.6 0.8 copy-done
  4.4 0.8 shard_map.91
  5.3 5.5 %all-to-all-start = ((f32[32,8,128]{2,1,0:T(8,128)}), f32[32,8,128]{2,1,0:T(8,128)S(1)}, u32[]{:S(2)}, u32[]{:S(2)}) async-start(f32[32,8,128]{2,1,0:T(8,128)} %shard_map.91), calls=%async_computation | async-start | bytes 262144 | tf_op jit(solution)/shard_map/all_to_all | solution.py:217
  10.8 0.5 shard_map.86
  11.3 2.4 %collective-permute-start.1 = (f32[2,8,256]{2,1,0:T(8,128)S(1)}, f32[2,8,256]{2,1,0:T(8,128)S(1)}, u32[]{:S(2)}, u32[]{:S(2)}) collective-permute-start(f32[2,8,256]{2,1,0:T(8,128)S(1)} %pad_maximum_fusion.8), channel_id=1, source_target_pairs={{0,4},{1,5},{2,6},{3,7},{4,0},{5,1},{6,2},{7,3},{8,12},{9,13},{10,... | collective-permute-start | bytes 49160 | tf_op jit(solution)/shard_map/ppermute | solution.py:227
  13.7 0.3 shard_map.87.start_ref
  14.0 2.4 %collective-permute-done.1.source_ref = f32[2,8,256]{2,1,0:T(8,128)S(1)} collective-permute-done((f32[2,8,256]{2,1,0:T(8,128)S(1)}, f32[2,8,256]{2,1,0:T(8,128)S(1)}, u32[]{:S(2)}, u32[]{:S(2)}) %collective-permute-start.1) | collective-permute-done | bytes 16416 | tf_op jit(solution)/shard_map/ppermute | solution.py:227
  16.4 1.2 %collective-permute-start.2 = (f32[4,8,256]{2,1,0:T(8,128)S(1)}, f32[4,8,256]{2,1,0:T(8,128)S(1)}, u32[]{:S(2)}, u32[]{:S(2)}) collective-permute-start(f32[4,8,256]{2,1,0:T(8,128)S(1)} %pad_maximum_fusion.4), channel_id=1, source_target_pairs={{0,8},{1,9},{2,10},{3,11},{4,12},{5,13},{6,14},{7,15},{8,0},{9,1},... | collective-permute-start | bytes 98312 | tf_op jit(solution)/shard_map/ppermute | solution.py:227
  17.6 0.6 shard_map.88.start_ref
  18.2 1.0 collective-permute-done.2.source_ref
  19.2 1.1 collective-permute-start.3
  20.3 1.3 %shard_map.89.start_ref = f32[3,256,128]{2,1,0:T(8,128)S(1)} custom-call(f32[4,8,256]{2,1,0:T(8,128)S(1)} %collective-permute-done.2.source_ref, f32[3,256,128]{2,1,0:T(8,128)S(1)} %get-tuple-element.52.column_ref, f32[3,256,128]{2,1,0:T(8,128)S(1)} %shard_map.88.start_ref), custom_call_target="tpu_custom_call" | custom-call | flops 8126464 | bytes 786432 | tf_op jit(solution)/shard_map/pallas_call | solution.py:196
  21.6 0.8 collective-permute-done.3.source_ref
  22.3 4.2 %collective-permute-start.4 = (f32[16,8,256]{2,1,0:T(8,128)S(1)}, f32[16,8,256]{2,1,0:T(8,128)S(1)}, u32[]{:S(2)}, u32[]{:S(2)}) collective-permute-start(f32[16,8,256]{2,1,0:T(8,128)S(1)} %constant_dynamic-update-slice_fusion), channel_id=1, source_target_pairs={{0,1},{1,0},{2,3},{3,2},{4,5},{5,4},{6,7},{7,6},{8,9},{9,8},{10,11... | collective-permute-start | bytes 393224 | tf_op jit(solution)/shard_map/ppermute | solution.py:227
  26.5 2.4 %shard_map.90.start_ref = f32[3,256,128]{2,1,0:T(8,128)S(1)} custom-call(f32[8,8,256]{2,1,0:T(8,128)S(1)} %collective-permute-done.3.source_ref, f32[3,256,128]{2,1,0:T(8,128)S(1)} %get-tuple-element.52.column_ref, f32[3,256,128]{2,1,0:T(8,128)S(1)} %shard_map.89.start_ref), custom_call_target="tpu_custom_call" | custom-call | flops 16252928 | bytes 786432 | tf_op jit(solution)/shard_map/pallas_call | solution.py:196
  29.0 0.6 copy-done.3
  29.7 2.5 %shard_map.92.params_ref = f32[16,256]{1,0:T(8,128)S(1)} custom-call(f32[32,8,128]{2,1,0:T(8,128)S(1)} %all-to-all-done.slots_ref, s32[1,256]{1,0:T(1,128)S(1)} %bitcast.4), custom_call_target="tpu_custom_call" | custom-call | tf_op jit(solution)/shard_map/pallas_call | solution.py:73
  32.2 5.1 %shard_map.93.source_ref.own_ref = f32[1,8,256]{2,1,0:T(8,128)S(1)} custom-call(f32[16,8,256]{2,1,0:T(8,128)S(1)} %collective-permute-done.4.source_ref, f32[1,8,256]{2,1,0:T(8,128)S(1)} %get-tuple-element.99.source_ref.own_ref, f32[3,256,128]{2,1,0:T(8,128)S(1)} %get-tuple-element.52.column_ref, f32[3,256,128]{2,1,0:T(8,128)S(1)} %shard_map.90.start_ref, ...), custom_call_target="tpu_custom_call" | custom-call | flops 32505856 | bytes 786432 | tf_op jit(solution)/shard_map/pallas_call | solution.py:196
  37.3 0.2 collective-permute-start.5
  37.5 0.5 shard_map.94
  38.0 1.8 %collective-permute-done.5.source_ref = f32[1,8,256]{2,1,0:T(8,128)S(1)} collective-permute-done((f32[1,8,256]{2,1,0:T(8,128)S(1)}, f32[1,8,256]{2,1,0:T(8,128)S(1)}, u32[]{:S(2)}, u32[]{:S(2)}) %collective-permute-start.5) | collective-permute-done | bytes 8224 | tf_op jit(solution)/shard_map/ppermute | solution.py:227
  39.9 0.3 collective-permute-start.6
  40.2 0.3 shard_map.95.start_ref
  40.5 2.9 %collective-permute-done.6.source_ref = f32[2,8,256]{2,1,0:T(8,128)S(1)} collective-permute-done((f32[2,8,256]{2,1,0:T(8,128)S(1)}, f32[2,8,256]{2,1,0:T(8,128)S(1)}, u32[]{:S(2)}, u32[]{:S(2)}) %collective-permute-start.6) | collective-permute-done | bytes 16416 | tf_op jit(solution)/shard_map/ppermute | solution.py:227
  43.4 1.2 %collective-permute-start.7 = (f32[4,8,256]{2,1,0:T(8,128)S(1)}, f32[4,8,256]{2,1,0:T(8,128)S(1)}, u32[]{:S(2)}, u32[]{:S(2)}) collective-permute-start(f32[4,8,256]{2,1,0:T(8,128)S(1)} %pad_maximum_fusion.5), channel_id=1, source_target_pairs={{0,8},{1,9},{2,10},{3,11},{4,12},{5,13},{6,14},{7,15},{8,0},{9,1},... | collective-permute-start | bytes 98312 | tf_op jit(solution)/shard_map/ppermute | solution.py:227
  44.6 0.6 shard_map.96.start_ref
  45.2 1.0 collective-permute-done.7.source_ref
  46.2 1.3 %shard_map.97.start_ref = f32[3,256,128]{2,1,0:T(8,128)S(1)} custom-call(f32[4,8,256]{2,1,0:T(8,128)S(1)} %collective-permute-done.7.source_ref, f32[3,256,128]{2,1,0:T(8,128)S(1)} %get-tuple-element.64.column_ref, f32[3,256,128]{2,1,0:T(8,128)S(1)} %shard_map.96.start_ref), custom_call_target="tpu_custom_call" | custom-call | flops 8126464 | bytes 786432 | tf_op jit(solution)/shard_map/pallas_call | solution.py:196
  47.5 1.3 %collective-permute-start.8 = (f32[8,8,256]{2,1,0:T(8,128)S(1)}, f32[8,8,256]{2,1,0:T(8,128)S(1)}, u32[]{:S(2)}, u32[]{:S(2)}) collective-permute-start(f32[8,8,256]{2,1,0:T(8,128)S(1)} %pad_maximum_fusion.1), channel_id=1, source_target_pairs={{0,16},{1,17},{2,18},{3,19},{4,20},{5,21},{6,22},{7,23},{8,24},{9,... | collective-permute-start | bytes 196616 | tf_op jit(solution)/shard_map/ppermute | solution.py:227
  48.8 1.9 %collective-permute-done.8.source_ref = f32[8,8,256]{2,1,0:T(8,128)S(1)} collective-permute-done((f32[8,8,256]{2,1,0:T(8,128)S(1)}, f32[8,8,256]{2,1,0:T(8,128)S(1)}, u32[]{:S(2)}, u32[]{:S(2)}) %collective-permute-start.8) | collective-permute-done | bytes 65568 | tf_op jit(solution)/shard_map/ppermute | solution.py:227
  50.7 4.6 %collective-permute-start.9 = (f32[16,8,256]{2,1,0:T(8,128)S(1)}, f32[16,8,256]{2,1,0:T(8,128)S(1)}, u32[]{:S(2)}, u32[]{:S(2)}) collective-permute-start(f32[16,8,256]{2,1,0:T(8,128)S(1)} %constant_dynamic-update-slice_fusion.5), channel_id=1, source_target_pairs={{0,1},{1,0},{2,3},{3,2},{4,5},{5,4},{6,7},{7,6},{8,9},{9,8},{10,11... | collective-permute-start | bytes 393224 | tf_op jit(solution)/shard_map/ppermute | solution.py:227
  55.3 2.4 %shard_map.98.start_ref = f32[3,256,128]{2,1,0:T(8,128)S(1)} custom-call(f32[8,8,256]{2,1,0:T(8,128)S(1)} %collective-permute-done.8.source_ref, f32[3,256,128]{2,1,0:T(8,128)S(1)} %get-tuple-element.64.column_ref, f32[3,256,128]{2,1,0:T(8,128)S(1)} %shard_map.97.start_ref), custom_call_target="tpu_custom_call" | custom-call | flops 16252928 | bytes 786432 | tf_op jit(solution)/shard_map/pallas_call | solution.py:196
  57.7 5.1 %shard_map.99.source_ref.own_ref = f32[1,8,256]{2,1,0:T(8,128)S(1)} custom-call(f32[16,8,256]{2,1,0:T(8,128)S(1)} %collective-permute-done.9.source_ref, f32[1,8,256]{2,1,0:T(8,128)S(1)} %shard_map.93.source_ref.own_ref, f32[3,256,128]{2,1,0:T(8,128)S(1)} %get-tuple-element.64.column_ref, f32[3,256,128]{2,1,0:T(8,128)S(1)} %shard_map.98.start_ref, ...), custom_call_target="tpu_custom_call" | custom-call | flops 32505856 | bytes 786432 | tf_op jit(solution)/shard_map/pallas_call | solution.py:196
  62.8 0.2 collective-permute-start.10
  63.0 0.5 shard_map.100
  63.5 1.9 %collective-permute-done.10.source_ref = f32[1,8,256]{2,1,0:T(8,128)S(1)} collective-permute-done((f32[1,8,256]{2,1,0:T(8,128)S(1)}, f32[1,8,256]{2,1,0:T(8,128)S(1)}, u32[]{:S(2)}, u32[]{:S(2)}) %collective-permute-start.10) | collective-permute-done | bytes 8224 | tf_op jit(solution)/shard_map/ppermute | solution.py:227
  65.4 0.3 collective-permute-start.11
  65.7 0.3 shard_map.101.start_ref
  66.0 2.9 %collective-permute-done.11.source_ref = f32[2,8,256]{2,1,0:T(8,128)S(1)} collective-permute-done((f32[2,8,256]{2,1,0:T(8,128)S(1)}, f32[2,8,256]{2,1,0:T(8,128)S(1)}, u32[]{:S(2)}, u32[]{:S(2)}) %collective-permute-start.11) | collective-permute-done | bytes 16416 | tf_op jit(solution)/shard_map/ppermute | solution.py:227
  68.9 1.2 %collective-permute-start.12 = (f32[4,8,256]{2,1,0:T(8,128)S(1)}, f32[4,8,256]{2,1,0:T(8,128)S(1)}, u32[]{:S(2)}, u32[]{:S(2)}) collective-permute-start(f32[4,8,256]{2,1,0:T(8,128)S(1)} %pad_maximum_fusion.6), channel_id=1, source_target_pairs={{0,8},{1,9},{2,10},{3,11},{4,12},{5,13},{6,14},{7,15},{8,0},{9,1},... | collective-permute-start | bytes 98312 | tf_op jit(solution)/shard_map/ppermute | solution.py:227
  70.1 0.6 shard_map.102.start_ref
  70.7 1.0 collective-permute-done.12.source_ref
  71.7 1.3 %shard_map.103.start_ref = f32[3,256,128]{2,1,0:T(8,128)S(1)} custom-call(f32[4,8,256]{2,1,0:T(8,128)S(1)} %collective-permute-done.12.source_ref, f32[3,256,128]{2,1,0:T(8,128)S(1)} %get-tuple-element.76.column_ref, f32[3,256,128]{2,1,0:T(8,128)S(1)} %shard_map.102.start_ref), custom_call_target="tpu_custom_call" | custom-call | flops 8126464 | bytes 786432 | tf_op jit(solution)/shard_map/pallas_call | solution.py:196
  72.9 1.3 %collective-permute-start.13 = (f32[8,8,256]{2,1,0:T(8,128)S(1)}, f32[8,8,256]{2,1,0:T(8,128)S(1)}, u32[]{:S(2)}, u32[]{:S(2)}) collective-permute-start(f32[8,8,256]{2,1,0:T(8,128)S(1)} %pad_maximum_fusion.2), channel_id=1, source_target_pairs={{0,16},{1,17},{2,18},{3,19},{4,20},{5,21},{6,22},{7,23},{8,24},{9,... | collective-permute-start | bytes 196616 | tf_op jit(solution)/shard_map/ppermute | solution.py:227
  74.2 1.9 %collective-permute-done.13.source_ref = f32[8,8,256]{2,1,0:T(8,128)S(1)} collective-permute-done((f32[8,8,256]{2,1,0:T(8,128)S(1)}, f32[8,8,256]{2,1,0:T(8,128)S(1)}, u32[]{:S(2)}, u32[]{:S(2)}) %collective-permute-start.13) | collective-permute-done | bytes 65568 | tf_op jit(solution)/shard_map/ppermute | solution.py:227
  76.1 4.6 %collective-permute-start.14 = (f32[16,8,256]{2,1,0:T(8,128)S(1)}, f32[16,8,256]{2,1,0:T(8,128)S(1)}, u32[]{:S(2)}, u32[]{:S(2)}) collective-permute-start(f32[16,8,256]{2,1,0:T(8,128)S(1)} %constant_dynamic-update-slice_fusion.10), channel_id=1, source_target_pairs={{0,1},{1,0},{2,3},{3,2},{4,5},{5,4},{6,7},{7,6},{8,9},{9,8},{10,11... | collective-permute-start | bytes 393224 | tf_op jit(solution)/shard_map/ppermute | solution.py:227
  80.7 2.4 %shard_map.104.start_ref = f32[3,256,128]{2,1,0:T(8,128)S(1)} custom-call(f32[8,8,256]{2,1,0:T(8,128)S(1)} %collective-permute-done.13.source_ref, f32[3,256,128]{2,1,0:T(8,128)S(1)} %get-tuple-element.76.column_ref, f32[3,256,128]{2,1,0:T(8,128)S(1)} %shard_map.103.start_ref), custom_call_target="tpu_custom_call" | custom-call | flops 16252928 | bytes 786432 | tf_op jit(solution)/shard_map/pallas_call | solution.py:196
  83.2 5.1 %shard_map.105.source_ref.own_ref = f32[1,8,256]{2,1,0:T(8,128)S(1)} custom-call(f32[16,8,256]{2,1,0:T(8,128)S(1)} %collective-permute-done.14.source_ref, f32[1,8,256]{2,1,0:T(8,128)S(1)} %shard_map.99.source_ref.own_ref, f32[3,256,128]{2,1,0:T(8,128)S(1)} %get-tuple-element.76.column_ref, f32[3,256,128]{2,1,0:T(8,128)S(1)} %shard_map.104.start_ref, ...), custom_call_target="tpu_custom_call" | custom-call | flops 32505856 | bytes 786432 | tf_op jit(solution)/shard_map/pallas_call | solution.py:196
  88.5 0.5 shard_map.106
  88.9 1.9 %collective-permute-done.15.source_ref = f32[1,8,256]{2,1,0:T(8,128)S(1)} collective-permute-done((f32[1,8,256]{2,1,0:T(8,128)S(1)}, f32[1,8,256]{2,1,0:T(8,128)S(1)}, u32[]{:S(2)}, u32[]{:S(2)}) %collective-permute-start.15) | collective-permute-done | bytes 8224 | tf_op jit(solution)/shard_map/ppermute | solution.py:227
  90.9 0.3 collective-permute-start.16
  91.1 0.3 shard_map.107.start_ref
  91.4 2.9 %collective-permute-done.16.source_ref = f32[2,8,256]{2,1,0:T(8,128)S(1)} collective-permute-done((f32[2,8,256]{2,1,0:T(8,128)S(1)}, f32[2,8,256]{2,1,0:T(8,128)S(1)}, u32[]{:S(2)}, u32[]{:S(2)}) %collective-permute-start.16) | collective-permute-done | bytes 16416 | tf_op jit(solution)/shard_map/ppermute | solution.py:227
  94.3 1.2 %collective-permute-start.17 = (f32[4,8,256]{2,1,0:T(8,128)S(1)}, f32[4,8,256]{2,1,0:T(8,128)S(1)}, u32[]{:S(2)}, u32[]{:S(2)}) collective-permute-start(f32[4,8,256]{2,1,0:T(8,128)S(1)} %pad_maximum_fusion.7), channel_id=1, source_target_pairs={{0,8},{1,9},{2,10},{3,11},{4,12},{5,13},{6,14},{7,15},{8,0},{9,1},... | collective-permute-start | bytes 98312 | tf_op jit(solution)/shard_map/ppermute | solution.py:227
  95.6 0.6 shard_map.108.start_ref
  96.1 1.0 collective-permute-done.17.source_ref
  97.1 1.3 %shard_map.109.start_ref = f32[3,256,128]{2,1,0:T(8,128)S(1)} custom-call(f32[4,8,256]{2,1,0:T(8,128)S(1)} %collective-permute-done.17.source_ref, f32[3,256,128]{2,1,0:T(8,128)S(1)} %get-tuple-element.88.column_ref, f32[3,256,128]{2,1,0:T(8,128)S(1)} %shard_map.108.start_ref), custom_call_target="tpu_custom_call" | custom-call | flops 8126464 | bytes 786432 | tf_op jit(solution)/shard_map/pallas_call | solution.py:196
  98.4 1.3 %collective-permute-start.18 = (f32[8,8,256]{2,1,0:T(8,128)S(1)}, f32[8,8,256]{2,1,0:T(8,128)S(1)}, u32[]{:S(2)}, u32[]{:S(2)}) collective-permute-start(f32[8,8,256]{2,1,0:T(8,128)S(1)} %pad_maximum_fusion.3), channel_id=1, source_target_pairs={{0,16},{1,17},{2,18},{3,19},{4,20},{5,21},{6,22},{7,23},{8,24},{9,... | collective-permute-start | bytes 196616 | tf_op jit(solution)/shard_map/ppermute | solution.py:227
  99.7 1.9 %collective-permute-done.18.source_ref = f32[8,8,256]{2,1,0:T(8,128)S(1)} collective-permute-done((f32[8,8,256]{2,1,0:T(8,128)S(1)}, f32[8,8,256]{2,1,0:T(8,128)S(1)}, u32[]{:S(2)}, u32[]{:S(2)}) %collective-permute-start.18) | collective-permute-done | bytes 65568 | tf_op jit(solution)/shard_map/ppermute | solution.py:227
  101.6 4.6 %collective-permute-start.19 = (f32[16,8,256]{2,1,0:T(8,128)S(1)}, f32[16,8,256]{2,1,0:T(8,128)S(1)}, u32[]{:S(2)}, u32[]{:S(2)}) collective-permute-start(f32[16,8,256]{2,1,0:T(8,128)S(1)} %constant_dynamic-update-slice_fusion.15), channel_id=1, source_target_pairs={{0,1},{1,0},{2,3},{3,2},{4,5},{5,4},{6,7},{7,6},{8,9},{9,8},{10,11... | collective-permute-start | bytes 393224 | tf_op jit(solution)/shard_map/ppermute | solution.py:227
  106.2 2.4 %shard_map.110.start_ref = f32[3,256,128]{2,1,0:T(8,128)S(1)} custom-call(f32[8,8,256]{2,1,0:T(8,128)S(1)} %collective-permute-done.18.source_ref, f32[3,256,128]{2,1,0:T(8,128)S(1)} %get-tuple-element.88.column_ref, f32[3,256,128]{2,1,0:T(8,128)S(1)} %shard_map.109.start_ref), custom_call_target="tpu_custom_call" | custom-call | flops 16252928 | bytes 786432 | tf_op jit(solution)/shard_map/pallas_call | solution.py:196
  108.6 5.6 %shard_map.111 = (f32[3,256]{1,0:T(4,128)}, f32[3,256]{1,0:T(4,128)}) custom-call(f32[16,8,256]{2,1,0:T(8,128)S(1)} %collective-permute-done.19.source_ref, f32[1,8,256]{2,1,0:T(8,128)S(1)} %shard_map.105.source_ref.own_ref, f32[3,256,128]{2,1,0:T(8,128)S(1)} %get-tuple-element.88.column_ref, f32[3,256,128]{2,1,0:T(8,128)S(1)} %shard_map.110.start_ref), custom_call_target="tpu_custom_call" | custom-call | flops 32505856 | bytes 786432 | tf_op jit(solution)/shard_map/pallas_call | solution.py:196
  (48 shorter events, 0.4 us)
Async XLA Ops:
  0.6 3.0 %copy-start.1 = (f32[3,1280]{1,0:T(4,128)S(1)}, f32[3,1280]{1,0:T(4,128)}, u32[]{:S(2)}) copy-start(f32[3,1280]{1,0:T(4,128)} %bend_ref.1) | copy-start | bytes 46084
  0.7 2.9 %copy-start.2 = (f32[2,1280]{1,0:T(2,128)S(1)}, f32[2,1280]{1,0:T(2,128)}, u32[]{:S(2)}) copy-start(f32[2,1280]{1,0:T(2,128)} %moduli_ref.1) | copy-start | bytes 30724
  1.5 9.8 %collective-permute-start = (f32[1,8,256]{2,1,0:T(8,128)S(1)}, f32[1,8,256]{2,1,0:T(8,128)S(1)}, u32[]{:S(2)}, u32[]{:S(2)}) collective-permute-start(f32[1,8,256]{2,1,0:T(8,128)S(1)} %get-tuple-element.99.source_ref.own_ref), channel_id=1, source_target_pairs={{0,2},{1,3},{2,0},{3,1},{4,6},{5,7},{6,4},{7,5},{8,10},{9,11},{10,... | collective-permute-start | bytes 24584 | tf_op jit(solution)/shard_map/ppermute | solution.py:227
  3.6 0.8 copy-start
  5.3 23.7 %all-to-all-start = ((f32[32,8,128]{2,1,0:T(8,128)}), f32[32,8,128]{2,1,0:T(8,128)S(1)}, u32[]{:S(2)}, u32[]{:S(2)}) async-start(f32[32,8,128]{2,1,0:T(8,128)} %shard_map.91), calls=%async_computation | async-start | bytes 262144 | tf_op jit(solution)/shard_map/all_to_all | solution.py:217
  11.3 5.1 %collective-permute-start.1 = (f32[2,8,256]{2,1,0:T(8,128)S(1)}, f32[2,8,256]{2,1,0:T(8,128)S(1)}, u32[]{:S(2)}, u32[]{:S(2)}) collective-permute-start(f32[2,8,256]{2,1,0:T(8,128)S(1)} %pad_maximum_fusion.8), channel_id=1, source_target_pairs={{0,4},{1,5},{2,6},{3,7},{4,0},{5,1},{6,2},{7,3},{8,12},{9,13},{10,... | collective-permute-start | bytes 49160 | tf_op jit(solution)/shard_map/ppermute | solution.py:227
  16.4 2.8 %collective-permute-start.2 = (f32[4,8,256]{2,1,0:T(8,128)S(1)}, f32[4,8,256]{2,1,0:T(8,128)S(1)}, u32[]{:S(2)}, u32[]{:S(2)}) collective-permute-start(f32[4,8,256]{2,1,0:T(8,128)S(1)} %pad_maximum_fusion.4), channel_id=1, source_target_pairs={{0,8},{1,9},{2,10},{3,11},{4,12},{5,13},{6,14},{7,15},{8,0},{9,1},... | collective-permute-start | bytes 98312 | tf_op jit(solution)/shard_map/ppermute | solution.py:227
  19.2 3.1 %collective-permute-start.3 = (f32[8,8,256]{2,1,0:T(8,128)S(1)}, f32[8,8,256]{2,1,0:T(8,128)S(1)}, u32[]{:S(2)}, u32[]{:S(2)}) collective-permute-start(f32[8,8,256]{2,1,0:T(8,128)S(1)} %pad_maximum_fusion), channel_id=1, source_target_pairs={{0,16},{1,17},{2,18},{3,19},{4,20},{5,21},{6,22},{7,23},{8,24},{9,... | collective-permute-start | bytes 196616 | tf_op jit(solution)/shard_map/ppermute | solution.py:227
  22.3 6.7 %collective-permute-start.4 = (f32[16,8,256]{2,1,0:T(8,128)S(1)}, f32[16,8,256]{2,1,0:T(8,128)S(1)}, u32[]{:S(2)}, u32[]{:S(2)}) collective-permute-start(f32[16,8,256]{2,1,0:T(8,128)S(1)} %constant_dynamic-update-slice_fusion), channel_id=1, source_target_pairs={{0,1},{1,0},{2,3},{3,2},{4,5},{5,4},{6,7},{7,6},{8,9},{9,8},{10,11... | collective-permute-start | bytes 393224 | tf_op jit(solution)/shard_map/ppermute | solution.py:227
  29.0 0.7 copy-start.3
  29.7 2.5 %copy-start.4 = (s32[12,256]{1,0:T(8,128)S(1)}, s32[12,256]{1,0:T(8,128)}, u32[]{:S(2)}) copy-start(s32[12,256]{1,0:T(8,128)} %neighbours_ref.5) | copy-start | bytes 36868
  37.3 2.6 %collective-permute-start.5 = (f32[1,8,256]{2,1,0:T(8,128)S(1)}, f32[1,8,256]{2,1,0:T(8,128)S(1)}, u32[]{:S(2)}, u32[]{:S(2)}) collective-permute-start(f32[1,8,256]{2,1,0:T(8,128)S(1)} %shard_map.93.source_ref.own_ref), channel_id=1, source_target_pairs={{0,2},{1,3},{2,0},{3,1},{4,6},{5,7},{6,4},{7,5},{8,10},{9,11},{10,... | collective-permute-start | bytes 24584 | tf_op jit(solution)/shard_map/ppermute | solution.py:227
  39.9 3.6 %collective-permute-start.6 = (f32[2,8,256]{2,1,0:T(8,128)S(1)}, f32[2,8,256]{2,1,0:T(8,128)S(1)}, u32[]{:S(2)}, u32[]{:S(2)}) collective-permute-start(f32[2,8,256]{2,1,0:T(8,128)S(1)} %pad_maximum_fusion.9), channel_id=1, source_target_pairs={{0,4},{1,5},{2,6},{3,7},{4,0},{5,1},{6,2},{7,3},{8,12},{9,13},{10,... | collective-permute-start | bytes 49160 | tf_op jit(solution)/shard_map/ppermute | solution.py:227
  43.4 2.8 %collective-permute-start.7 = (f32[4,8,256]{2,1,0:T(8,128)S(1)}, f32[4,8,256]{2,1,0:T(8,128)S(1)}, u32[]{:S(2)}, u32[]{:S(2)}) collective-permute-start(f32[4,8,256]{2,1,0:T(8,128)S(1)} %pad_maximum_fusion.5), channel_id=1, source_target_pairs={{0,8},{1,9},{2,10},{3,11},{4,12},{5,13},{6,14},{7,15},{8,0},{9,1},... | collective-permute-start | bytes 98312 | tf_op jit(solution)/shard_map/ppermute | solution.py:227
  47.5 3.2 %collective-permute-start.8 = (f32[8,8,256]{2,1,0:T(8,128)S(1)}, f32[8,8,256]{2,1,0:T(8,128)S(1)}, u32[]{:S(2)}, u32[]{:S(2)}) collective-permute-start(f32[8,8,256]{2,1,0:T(8,128)S(1)} %pad_maximum_fusion.1), channel_id=1, source_target_pairs={{0,16},{1,17},{2,18},{3,19},{4,20},{5,21},{6,22},{7,23},{8,24},{9,... | collective-permute-start | bytes 196616 | tf_op jit(solution)/shard_map/ppermute | solution.py:227
  50.7 7.1 %collective-permute-start.9 = (f32[16,8,256]{2,1,0:T(8,128)S(1)}, f32[16,8,256]{2,1,0:T(8,128)S(1)}, u32[]{:S(2)}, u32[]{:S(2)}) collective-permute-start(f32[16,8,256]{2,1,0:T(8,128)S(1)} %constant_dynamic-update-slice_fusion.5), channel_id=1, source_target_pairs={{0,1},{1,0},{2,3},{3,2},{4,5},{5,4},{6,7},{7,6},{8,9},{9,8},{10,11... | collective-permute-start | bytes 393224 | tf_op jit(solution)/shard_map/ppermute | solution.py:227
  62.8 2.6 %collective-permute-start.10 = (f32[1,8,256]{2,1,0:T(8,128)S(1)}, f32[1,8,256]{2,1,0:T(8,128)S(1)}, u32[]{:S(2)}, u32[]{:S(2)}) collective-permute-start(f32[1,8,256]{2,1,0:T(8,128)S(1)} %shard_map.99.source_ref.own_ref), channel_id=1, source_target_pairs={{0,2},{1,3},{2,0},{3,1},{4,6},{5,7},{6,4},{7,5},{8,10},{9,11},{10,... | collective-permute-start | bytes 24584 | tf_op jit(solution)/shard_map/ppermute | solution.py:227
  65.4 3.5 %collective-permute-start.11 = (f32[2,8,256]{2,1,0:T(8,128)S(1)}, f32[2,8,256]{2,1,0:T(8,128)S(1)}, u32[]{:S(2)}, u32[]{:S(2)}) collective-permute-start(f32[2,8,256]{2,1,0:T(8,128)S(1)} %pad_maximum_fusion.10), channel_id=1, source_target_pairs={{0,4},{1,5},{2,6},{3,7},{4,0},{5,1},{6,2},{7,3},{8,12},{9,13},{10,... | collective-permute-start | bytes 49160 | tf_op jit(solution)/shard_map/ppermute | solution.py:227
  68.9 2.8 %collective-permute-start.12 = (f32[4,8,256]{2,1,0:T(8,128)S(1)}, f32[4,8,256]{2,1,0:T(8,128)S(1)}, u32[]{:S(2)}, u32[]{:S(2)}) collective-permute-start(f32[4,8,256]{2,1,0:T(8,128)S(1)} %pad_maximum_fusion.6), channel_id=1, source_target_pairs={{0,8},{1,9},{2,10},{3,11},{4,12},{5,13},{6,14},{7,15},{8,0},{9,1},... | collective-permute-start | bytes 98312 | tf_op jit(solution)/shard_map/ppermute | solution.py:227
  72.9 3.2 %collective-permute-start.13 = (f32[8,8,256]{2,1,0:T(8,128)S(1)}, f32[8,8,256]{2,1,0:T(8,128)S(1)}, u32[]{:S(2)}, u32[]{:S(2)}) collective-permute-start(f32[8,8,256]{2,1,0:T(8,128)S(1)} %pad_maximum_fusion.2), channel_id=1, source_target_pairs={{0,16},{1,17},{2,18},{3,19},{4,20},{5,21},{6,22},{7,23},{8,24},{9,... | collective-permute-start | bytes 196616 | tf_op jit(solution)/shard_map/ppermute | solution.py:227
  76.1 7.1 %collective-permute-start.14 = (f32[16,8,256]{2,1,0:T(8,128)S(1)}, f32[16,8,256]{2,1,0:T(8,128)S(1)}, u32[]{:S(2)}, u32[]{:S(2)}) collective-permute-start(f32[16,8,256]{2,1,0:T(8,128)S(1)} %constant_dynamic-update-slice_fusion.10), channel_id=1, source_target_pairs={{0,1},{1,0},{2,3},{3,2},{4,5},{5,4},{6,7},{7,6},{8,9},{9,8},{10,11... | collective-permute-start | bytes 393224 | tf_op jit(solution)/shard_map/ppermute | solution.py:227
  88.3 2.6 %collective-permute-start.15 = (f32[1,8,256]{2,1,0:T(8,128)S(1)}, f32[1,8,256]{2,1,0:T(8,128)S(1)}, u32[]{:S(2)}, u32[]{:S(2)}) collective-permute-start(f32[1,8,256]{2,1,0:T(8,128)S(1)} %shard_map.105.source_ref.own_ref), channel_id=1, source_target_pairs={{0,2},{1,3},{2,0},{3,1},{4,6},{5,7},{6,4},{7,5},{8,10},{9,11},{10,... | collective-permute-start | bytes 24584 | tf_op jit(solution)/shard_map/ppermute | solution.py:227
  90.9 3.5 %collective-permute-start.16 = (f32[2,8,256]{2,1,0:T(8,128)S(1)}, f32[2,8,256]{2,1,0:T(8,128)S(1)}, u32[]{:S(2)}, u32[]{:S(2)}) collective-permute-start(f32[2,8,256]{2,1,0:T(8,128)S(1)} %pad_maximum_fusion.11), channel_id=1, source_target_pairs={{0,4},{1,5},{2,6},{3,7},{4,0},{5,1},{6,2},{7,3},{8,12},{9,13},{10,... | collective-permute-start | bytes 49160 | tf_op jit(solution)/shard_map/ppermute | solution.py:227
  94.3 2.8 %collective-permute-start.17 = (f32[4,8,256]{2,1,0:T(8,128)S(1)}, f32[4,8,256]{2,1,0:T(8,128)S(1)}, u32[]{:S(2)}, u32[]{:S(2)}) collective-permute-start(f32[4,8,256]{2,1,0:T(8,128)S(1)} %pad_maximum_fusion.7), channel_id=1, source_target_pairs={{0,8},{1,9},{2,10},{3,11},{4,12},{5,13},{6,14},{7,15},{8,0},{9,1},... | collective-permute-start | bytes 98312 | tf_op jit(solution)/shard_map/ppermute | solution.py:227
  98.4 3.2 %collective-permute-start.18 = (f32[8,8,256]{2,1,0:T(8,128)S(1)}, f32[8,8,256]{2,1,0:T(8,128)S(1)}, u32[]{:S(2)}, u32[]{:S(2)}) collective-permute-start(f32[8,8,256]{2,1,0:T(8,128)S(1)} %pad_maximum_fusion.3), channel_id=1, source_target_pairs={{0,16},{1,17},{2,18},{3,19},{4,20},{5,21},{6,22},{7,23},{8,24},{9,... | collective-permute-start | bytes 196616 | tf_op jit(solution)/shard_map/ppermute | solution.py:227
  101.6 7.1 %collective-permute-start.19 = (f32[16,8,256]{2,1,0:T(8,128)S(1)}, f32[16,8,256]{2,1,0:T(8,128)S(1)}, u32[]{:S(2)}, u32[]{:S(2)}) collective-permute-start(f32[16,8,256]{2,1,0:T(8,128)S(1)} %constant_dynamic-update-slice_fusion.15), channel_id=1, source_target_pairs={{0,1},{1,0},{2,3},{3,2},{4,5},{5,4},{6,7},{7,6},{8,9},{9,8},{10,11... | collective-permute-start | bytes 393224 | tf_op jit(solution)/shard_map/ppermute | solution.py:227

commit v6 on v4

--- a/solution.py
+++ b/solution.py
@@ -22,61 +22,81 @@
 GRANT = pltpu.CompilerParams(vmem_limit_bytes=32 * 1024 * 1024)
 
 
-def pack_kernel(length_ref, moduli_ref, bend_ref, out_ref):
-    devices = out_ref.shape[0]
-    capacity = length_ref.shape[1] // devices
-    out_ref[...] = jnp.zeros(out_ref.shape, jnp.float32)
-    for device in range(devices):
-        cut = slice(device * capacity, (device + 1) * capacity)
-        out_ref[device, 0:6, 0:capacity] = length_ref[:, cut]
-        out_ref[device, 6:8, 0:capacity] = moduli_ref[:, cut]
-        out_ref[device, 0:3, capacity : 2 * capacity] = bend_ref[:, cut]
-
-
-def pack_slots(rest_length, moduli, rest_bend, devices):
+def pack_kernel(*refs):
+    inputs, (out_ref, state_ref), copies, semaphores = refs[:5], refs[5:7], refs[7:12], refs[12]
+    loads = [pltpu.make_async_copy(inputs[i], copies[i], semaphores.at[i]) for i in range(5)]
+    for load in loads:
+        load.start()
+    for load in loads:
+        load.wait()
+    position_ref, force_ref, length_ref, moduli_ref, bend_ref = copies
+    chips = out_ref.shape[0]
+    nodes = position_ref.shape[1]
+    capacity = length_ref.shape[1] // (2 * chips)
+    state = jnp.concatenate(
+        [position_ref[...], force_ref[...], jnp.zeros((ROWS - 6, nodes), jnp.float32)], axis=0
+    )
+    state_ref[...] = state
+    for chip in range(chips):
+        out_ref[chip, 0:ROWS, :] = state
+        for core in range(2):
+            start = (2 * chip + core) * capacity
+            cut = slice(start, start + capacity)
+            lane = core * LANES
+            out_ref[chip, 8:14, lane : lane + capacity] = length_ref[:, cut]
+            out_ref[chip, 14:16, lane : lane + capacity] = moduli_ref[:, cut]
+            out_ref[chip, 8:11, lane + capacity : lane + 2 * capacity] = bend_ref[:, cut]
+
+
+def pack(positions, forces, rest_length, moduli, rest_bend, devices):
+    operands = (positions, forces, rest_length, moduli, rest_bend)
+    nodes = positions.shape[1]
     return pl.pallas_call(
         pack_kernel,
-        out_shape=jax.ShapeDtypeStruct((devices, ROWS, LANES), jnp.float32),
-        in_specs=[VMEM] * 3,
-        out_specs=VMEM,
-        compiler_params=GRANT,
-    )(rest_length, moduli, rest_bend)
-
-
-def pick_kernel(capacity, slots_ref, owner_ref, out_ref):
-    devices = slots_ref.shape[0]
+        out_shape=(
+            jax.ShapeDtypeStruct((devices // 2, 2 * ROWS, 2 * LANES), jnp.float32),
+            jax.ShapeDtypeStruct((ROWS, nodes), jnp.float32),
+        ),
+        in_specs=[pl.BlockSpec(memory_space=pl.ANY)] * 5,
+        out_specs=(VMEM,) * 2,
+        scratch_shapes=[pltpu.VMEM(x.shape, x.dtype) for x in operands] + [pltpu.SemaphoreType.DMA((5,))],
+        compiler_params=pltpu.CompilerParams(vmem_limit_bytes=60 * 1024 * 1024),
+    )(*operands)
+
+
+def pick_slots(capacity, near_ref, far_ref, owner_ref, params_ref):
+    chips = near_ref.shape[0]
     nodes = owner_ref.shape[1]
     owner = owner_ref[...]
     across = jnp.broadcast_to(owner, (nodes, nodes))
-    down = across.T
     earlier = lax.broadcasted_iota(jnp.int32, (nodes, nodes), 0) < lax.broadcasted_iota(
         jnp.int32, (nodes, nodes), 1
     )
-    rank = jnp.sum(jnp.where((across == down) & earlier, 1, 0), axis=0, keepdims=True)
-    for at in range(0, nodes, LANES):
-        place = jnp.broadcast_to(rank[:, at : at + LANES], (ROWS, LANES))
-        named = jnp.broadcast_to(owner[:, at : at + LANES], (ROWS, LANES))
-        for part in range(PARAMS // ROWS):
-
-            def choose(device, chosen):
-                taken = jnp.take_along_axis(
-                    slots_ref[device], place + part * capacity, axis=1, mode="promise_in_bounds"
-                )
-                return jnp.where(named == device, taken, chosen)
-
-            out_ref[part * ROWS : (part + 1) * ROWS, at : at + LANES] = lax.fori_loop(
-                0, devices, choose, jnp.zeros((ROWS, LANES), jnp.float32), unroll=4
-            )
-
-
-def pick_slots(slots, owner, capacity):
-    return pl.pallas_call(
-        functools.partial(pick_kernel, capacity),
-        out_shape=jax.ShapeDtypeStruct((PARAMS, owner.shape[1]), jnp.float32),
-        in_specs=[VMEM] * 2,
-        out_specs=VMEM,
-        compiler_params=GRANT,
-    )(slots, owner)
+    rank = jnp.sum(jnp.where((across == across.T) & earlier, 1, 0), axis=0, keepdims=True)
+    parity = lax.axis_index("src") & 1
+    lanes = pl.ds(pl.multiple_of(parity * LANES, LANES), LANES)
+    spots = range(0, nodes, LANES)
+    places = [jnp.broadcast_to(rank[:, at : at + LANES], (ROWS, LANES)) for at in spots]
+    owners = [jnp.broadcast_to(owner[:, at : at + LANES], (ROWS, LANES)) for at in spots]
+
+    def choose(chip, chosen):
+        chosen = list(chosen)
+        for ref, device in ((near_ref, 2 * chip + parity), (far_ref, 2 * chip + 1 - parity)):
+            block = ref[chip, ROWS : 2 * ROWS, lanes]
+            for i in range(len(spots)):
+                for part in range(2):
+                    taken = jnp.take_along_axis(
+                        block, places[i] + part * capacity, axis=1, mode="promise_in_bounds"
+                    )
+                    at = 2 * i + part
+                    chosen[at] = jnp.where(owners[i] == device, taken, chosen[at])
+        return tuple(chosen)
+
+    zero = jnp.zeros((ROWS, LANES), jnp.float32)
+    chosen = lax.fori_loop(0, chips, choose, (zero,) * (2 * len(spots)), unroll=4)
+    for i, at in enumerate(spots):
+        for part in range(2):
+            params_ref[part * ROWS : (part + 1) * ROWS, at : at + LANES] = chosen[2 * i + part]
 
 
 def spread_columns(own_ref, column_ref):
@@ -167,9 +187,7 @@
     pair_sums([source_ref], column_ref, None, sum_ref)
 
 
-def step_kernel(others, scale, *refs):
-    own_ref, column_ref, start_ref, neighbours_ref, params_ref, out_ref, sum_ref = refs[others:]
-    pair_sums(refs[:others], column_ref, start_ref, sum_ref)
+def advance(scale, own_ref, sum_ref, neighbours_ref, params_ref, out_ref):
     velocity = velocity_rows(sum_ref, scale)
     x = [own_ref[c : c + 1, :] + time_step * velocity[c] for c in range(3)]
     force = membrane(x, neighbours_ref, params_ref)
@@ -179,18 +197,30 @@
     out_ref[6:ROWS, :] = jnp.zeros((ROWS - 6, x[0].shape[1]), jnp.float32)
 
 
-def last_kernel(others, scale, *refs):
-    own_ref, column_ref, start_ref, position_ref, velocity_ref, sum_ref = refs[others:]
-    pair_sums(refs[:others], column_ref, start_ref, sum_ref)
+def first_kernel(scale, capacity, *refs):
+    far_ref, own_ref, column_ref, start_ref, neighbours_ref, near_ref, owner_ref, out_ref, params_ref, sum_ref = refs
+    pick_slots(capacity, near_ref, far_ref, owner_ref, params_ref)
+    pair_sums([far_ref], column_ref, start_ref, sum_ref)
+    advance(scale, own_ref, sum_ref, neighbours_ref, params_ref, out_ref)
+
+
+def step_kernel(scale, *refs):
+    far_ref, own_ref, column_ref, start_ref, neighbours_ref, params_ref, out_ref, sum_ref = refs
+    pair_sums([far_ref], column_ref, start_ref, sum_ref)
+    advance(scale, own_ref, sum_ref, neighbours_ref, params_ref, out_ref)
+
+
+def last_kernel(scale, *refs):
+    far_ref, own_ref, column_ref, start_ref, position_ref, velocity_ref, sum_ref = refs
+    pair_sums([far_ref], column_ref, start_ref, sum_ref)
     velocity = velocity_rows(sum_ref, scale)
     position_ref[...] = own_ref[0:3, :]
     for c in range(3):
         velocity_ref[c : c + 1, :] = velocity[c]
 
 
-def spread(state, devices):
+def spread(copies, devices):
     parities = [list(range(parity, devices, 2)) for parity in range(2)]
-    copies = jnp.broadcast_to(state[None], (devices // 2,) + state.shape)
     near = lax.all_to_all(copies, AXES, split_axis=0, concat_axis=0, axis_index_groups=parities, tiled=True)
     far = lax.ppermute(near, AXES, [(i, i ^ 1) for i in range(devices)])
     return near, far
@@ -210,37 +240,41 @@
     )(near, state)
 
 
+def call(kernel, out_shape, operands):
+    nodes = operands[1].shape[1]
+    return pl.pallas_call(
+        kernel,
+        out_shape=out_shape,
+        in_specs=[VMEM] * len(operands),
+        out_specs=jax.tree.map(lambda _: VMEM, out_shape),
+        scratch_shapes=[pltpu.VMEM((3, nodes, LANES), jnp.float32)],
+        compiler_params=GRANT,
+    )(*operands)
+
+
 def body(positions, forces, neighbours, patch_owner, rest_length, moduli, rest_bend):
     devices = lax.axis_size("tgt") * lax.axis_size("src")
     nodes = positions.shape[1]
     scale = 1.0 / math.sqrt(devices * nodes)
-    state = jnp.concatenate([positions, forces, jnp.zeros((ROWS - 6, nodes), jnp.float32)], axis=0)
-    sums = [pltpu.VMEM((3, nodes, LANES), jnp.float32)]
+    capacity = rest_length.shape[1] // devices
+    state_shape = jax.ShapeDtypeStruct((ROWS, nodes), jnp.float32)
+    params_shape = jax.ShapeDtypeStruct((PARAMS, nodes), jnp.float32)
+    row_shape = jax.ShapeDtypeStruct((3, nodes), jnp.float32)
+    copies, state = pack(positions, forces, rest_length, moduli, rest_bend, devices)
     for step in range(STEPS + 1):
-        near, far = spread(state, devices)
+        near, far = spread(copies, devices)
+        column, start = near_sums(near, state)
+        operands = (far, state, column, start)
         if step == 0:
-            packed = pack_slots(rest_length, moduli, rest_bend, devices)
-            near, far, packed = lax.optimization_barrier((near, far, packed))
-            slots = lax.all_to_all(packed, AXES, split_axis=0, concat_axis=0, tiled=True)
-            params = pick_slots(slots, patch_owner.reshape(1, nodes), rest_length.shape[1] // devices)
-        column, start = near_sums(near, state)
-        if step < STEPS:
-            state = pl.pallas_call(
-                functools.partial(step_kernel, 1, scale),
-                out_shape=jax.ShapeDtypeStruct((ROWS, nodes), jnp.float32),
-                in_specs=[VMEM] * (6),
-                out_specs=VMEM,
-                scratch_shapes=sums,
-                compiler_params=GRANT,
-            )(far, state, column, start, neighbours, params)
-    return pl.pallas_call(
-        functools.partial(last_kernel, 1, scale),
-        out_shape=(jax.ShapeDtypeStruct((3, nodes), jnp.float32),) * 2,
-        in_specs=[VMEM] * (4),
-        out_specs=(VMEM,) * 2,
-        scratch_shapes=sums,
-        compiler_params=GRANT,
-    )(far, state, column, start)
+            state, params = call(
+                functools.partial(first_kernel, scale, capacity),
+                (state_shape, params_shape),
+                operands + (neighbours, near, patch_owner.reshape(1, nodes)),
+            )
+        elif step < STEPS:
+            state = call(functools.partial(step_kernel, scale), state_shape, operands + (neighbours, params))
+        copies = jnp.broadcast_to(state[None], (devices // 2,) + state.shape)
+    return call(functools.partial(last_kernel, scale), (row_shape, row_shape), operands)
 
 
 def solution(mesh):

time: 103 us -> 97.5 us (0.947)
  waiting for transfers between devices: 3.51 us -> 0.01 us
  starting transfers between devices: 10.3 us -> 8.04 us
  blocking collectives: 43 us -> 44.2 us
    all_to_all x1 -> x0, waiting for transfers between devices: 3.37 us -> none  [body(): lax.all_to_all(packed, AXES, split_axis=0, concat_axis=0, tiled=True)]
    all_to_all x1 -> x0, starting transfers between devices: 2.53 us -> none  [body(): lax.all_to_all(packed, AXES, split_axis=0, concat_axis=0, tiled=True)]
    all_to_all x4, blocking collectives: 43 us -> 44.2 us  [spread(): lax.all_to_all(copies, AXES, split_axis=0, concat_axis=0, axis_index_grou...]
    pallas_call x6 -> x5, Pallas kernels: 24.2 us -> 23.4 us  [the longest x4 21.6 us: call(): pl.pallas_call(kernel, out_shape=out_shape, in_specs=[VMEM] * len(operand...]
  transfers between devices with their start and end apart: 5 -> 4, of which waited for: 2 -> 0; matrix products, arithmetic and copies ran while one was open for 0% -> 0% of each run, Pallas kernels for 20% -> 21%
where the time goes in v6:
time: 97.5 us; the launch traced here: 97.1 us
  blocking collectives  44.2 us (45%)
  Pallas kernels  43.4 us (45%)
  starting transfers between devices  8.04 us (8%)
    all_to_all x4, blocking collectives, spread(): lax.all_to_all(copies, AXES, split_axis=0, concat_axis=0, axis_index_grou...  44.2 us
    pallas_call x4, Pallas kernels, call(): pl.pallas_call(kernel, out_shape=out_shape, in_specs=[VMEM] * len(operand...  21.6 us
    pallas_call x4, Pallas kernels, near_sums(): pl.pallas_call(near_kernel, out_shape=(shape, shape), in_specs=[VMEM] * 2...  20 us
    ppermute x4, starting transfers between devices, spread(): far = lax.ppermute(near, AXES, [(i, i ^ 1) for i in range(devices)])  8.04 us
  transfers between devices with their start and end apart: 4, of which 0 were waited for; matrix products, arithmetic and copies ran while one was open for 0% of the time, Pallas kernels for 21%

profile of v6, /device:TPU:1, one launch (start us, length us, event | category | flops | bytes accessed | tf_op | source)
XLA Modules:
  0.0 97.1 jit_solution(15040982090140670957)
XLA Ops:
  0.6 1.8 %shard_map.86 = (f32[16,16,256]{2,1,0:T(8,128)}, f32[8,256]{1,0:T(8,128)}) custom-call(f32[3,256]{1,0:T(4,128)} %refs_0_.1, f32[3,256]{1,0:T(4,128)} %refs_1_.1, f32[6,1280]{1,0:T(8,128)} %refs_2_.1, f32[2,1280]{1,0:T(2,128)} %refs_3_.1, f32[3,1280]{1,0:T(4,128)} %refs_4_.4), custom_call_target="tpu_custom_call" | custom-call | tf_op jit(solution)/shard_map/pallas_call | solution.py:54
  2.4 0.0 copy-start.1
  2.4 16.6 %all_to_all.20.source_ref.refs_5_ = f32[16,16,256]{2,1,0:T(8,128)S(1)} all-to-all(f32[16,16,256]{2,1,0:T(8,128)} %get-tuple-element.14), channel_id=1, replica_groups={{0,2,4,6,8,10,12,14,16,18,20,22,24,26,28,30},{1,3,5,7,9,11,13,15,17,19,..., dimensions={0} | all-to-all | bytes 524288 | tf_op jit(solution)/shard_map/all_to_all | solution.py:224
  19.1 2.3 %collective-permute-start = (f32[16,16,256]{2,1,0:T(8,128)S(1)}, f32[16,16,256]{2,1,0:T(8,128)S(1)}, u32[]{:S(2)}, u32[]{:S(2)}) collective-permute-start(f32[16,16,256]{2,1,0:T(8,128)S(1)} %all_to_all.20.source_ref.refs_5_), channel_id=1, source_target_pairs={{0,1},{1,0},{2,3},{3,2},{4,5},{5,4},{6,7},{7,6},{8,9},{9,8},{10,11... | collective-permute-start | bytes 786440 | tf_op jit(solution)/shard_map/ppermute | solution.py:225
  21.4 0.0 copy-done.1
  21.4 0.0 copy-start
  21.4 5.0 %shard_map.87 = (f32[3,256,128]{2,1,0:T(8,128)S(1)}, f32[3,256,128]{2,1,0:T(8,128)S(1)}) custom-call(f32[16,16,256]{2,1,0:T(8,128)S(1)} %all_to_all.20.source_ref.refs_5_, f32[8,256]{1,0:T(8,128)S(1)} %copy-done.1), custom_call_target="tpu_custom_call" | custom-call | flops 32505856 | bytes 786432 | tf_op jit(solution)/shard_map/pallas_call | solution.py:233
  26.4 0.0 collective-permute-done.refs_0_
  26.4 0.0 copy-start.2
  26.4 0.0 copy-done
  26.4 0.7 copy-done.2
  27.0 5.8 %shard_map.88 = (f32[8,256]{1,0:T(8,128)S(1)}, f32[16,256]{1,0:T(8,128)S(1)}) custom-call(f32[16,16,256]{2,1,0:T(8,128)S(1)} %collective-permute-done.refs_0_, f32[8,256]{1,0:T(8,128)S(1)} %copy-done.1, f32[3,256,128]{2,1,0:T(8,128)S(1)} %get-tuple-element.16.refs_2_, f32[3,256,128]{2,1,0:T(8,128)S(1)} %get-tuple-element.17.refs_3_, s32[12,256]{1,0:T(8,128)S(1)} %copy-done, ...), custom_call_target="tpu_custom_call" | custom-call | tf_op jit(solution)/shard_map/pallas_call | solution.py:245
  32.9 9.2 %all_to_all.21.source_ref = f32[16,8,256]{2,1,0:T(8,128)S(1)} all-to-all(f32[16,8,256]{2,1,0:T(8,128)S(1)} %broadcast_in_dim.6), channel_id=1, replica_groups={{0,2,4,6,8,10,12,14,16,18,20,22,24,26,28,30},{1,3,5,7,9,11,13,15,17,19,..., dimensions={0} | all-to-all | bytes 262144 | tf_op jit(solution)/shard_map/all_to_all | solution.py:224
  42.1 1.8 %collective-permute-start.1 = (f32[16,8,256]{2,1,0:T(8,128)S(1)}, f32[16,8,256]{2,1,0:T(8,128)S(1)}, u32[]{:S(2)}, u32[]{:S(2)}) collective-permute-start(f32[16,8,256]{2,1,0:T(8,128)S(1)} %all_to_all.21.source_ref), channel_id=1, source_target_pairs={{0,1},{1,0},{2,3},{3,2},{4,5},{5,4},{6,7},{7,6},{8,9},{9,8},{10,11... | collective-permute-start | bytes 393224 | tf_op jit(solution)/shard_map/ppermute | solution.py:225
  43.9 5.0 %shard_map.89 = (f32[3,256,128]{2,1,0:T(8,128)S(1)}, f32[3,256,128]{2,1,0:T(8,128)S(1)}) custom-call(f32[16,8,256]{2,1,0:T(8,128)S(1)} %all_to_all.21.source_ref, f32[8,256]{1,0:T(8,128)S(1)} %get-tuple-element.18.own_ref.refs_1_), custom_call_target="tpu_custom_call" | custom-call | flops 32505856 | bytes 786432 | tf_op jit(solution)/shard_map/pallas_call | solution.py:233
  48.9 0.0 collective-permute-done.1.refs_0_
  48.9 5.1 %shard_map.90.own_ref.refs_1_ = f32[8,256]{1,0:T(8,128)S(1)} custom-call(f32[16,8,256]{2,1,0:T(8,128)S(1)} %collective-permute-done.1.refs_0_, f32[8,256]{1,0:T(8,128)S(1)} %get-tuple-element.18.own_ref.refs_1_, f32[3,256,128]{2,1,0:T(8,128)S(1)} %get-tuple-element.19.refs_2_, f32[3,256,128]{2,1,0:T(8,128)S(1)} %get-tuple-element.20.refs_3_, ...), custom_call_target="tpu_custom_call" | custom-call | tf_op jit(solution)/shard_map/pallas_call | solution.py:245
  54.1 9.2 %all_to_all.22.source_ref = f32[16,8,256]{2,1,0:T(8,128)S(1)} all-to-all(f32[16,8,256]{2,1,0:T(8,128)S(1)} %broadcast_in_dim.7), channel_id=1, replica_groups={{0,2,4,6,8,10,12,14,16,18,20,22,24,26,28,30},{1,3,5,7,9,11,13,15,17,19,..., dimensions={0} | all-to-all | bytes 262144 | tf_op jit(solution)/shard_map/all_to_all | solution.py:224
  63.3 2.0 %collective-permute-start.2 = (f32[16,8,256]{2,1,0:T(8,128)S(1)}, f32[16,8,256]{2,1,0:T(8,128)S(1)}, u32[]{:S(2)}, u32[]{:S(2)}) collective-permute-start(f32[16,8,256]{2,1,0:T(8,128)S(1)} %all_to_all.22.source_ref), channel_id=1, source_target_pairs={{0,1},{1,0},{2,3},{3,2},{4,5},{5,4},{6,7},{7,6},{8,9},{9,8},{10,11... | collective-permute-start | bytes 393224 | tf_op jit(solution)/shard_map/ppermute | solution.py:225
  65.3 5.0 %shard_map.91 = (f32[3,256,128]{2,1,0:T(8,128)S(1)}, f32[3,256,128]{2,1,0:T(8,128)S(1)}) custom-call(f32[16,8,256]{2,1,0:T(8,128)S(1)} %all_to_all.22.source_ref, f32[8,256]{1,0:T(8,128)S(1)} %shard_map.90.own_ref.refs_1_), custom_call_target="tpu_custom_call" | custom-call | flops 32505856 | bytes 786432 | tf_op jit(solution)/shard_map/pallas_call | solution.py:233
  70.3 0.0 collective-permute-done.2.refs_0_
  70.3 5.1 %shard_map.92.own_ref.refs_1_ = f32[8,256]{1,0:T(8,128)S(1)} custom-call(f32[16,8,256]{2,1,0:T(8,128)S(1)} %collective-permute-done.2.refs_0_, f32[8,256]{1,0:T(8,128)S(1)} %shard_map.90.own_ref.refs_1_, f32[3,256,128]{2,1,0:T(8,128)S(1)} %get-tuple-element.22.refs_2_, f32[3,256,128]{2,1,0:T(8,128)S(1)} %get-tuple-element.23.refs_3_, s32[12,256]{1,0:T(8,128)S(1)} %copy-done, ...), custom_call_target="tpu_custom_call" | custom-call | tf_op jit(solution)/shard_map/pallas_call | solution.py:245
  75.4 9.2 %all_to_all.23.source_ref = f32[16,8,256]{2,1,0:T(8,128)S(1)} all-to-all(f32[16,8,256]{2,1,0:T(8,128)S(1)} %broadcast_in_dim.8), channel_id=1, replica_groups={{0,2,4,6,8,10,12,14,16,18,20,22,24,26,28,30},{1,3,5,7,9,11,13,15,17,19,..., dimensions={0} | all-to-all | bytes 262144 | tf_op jit(solution)/shard_map/all_to_all | solution.py:224
  84.6 1.9 %collective-permute-start.3 = (f32[16,8,256]{2,1,0:T(8,128)S(1)}, f32[16,8,256]{2,1,0:T(8,128)S(1)}, u32[]{:S(2)}, u32[]{:S(2)}) collective-permute-start(f32[16,8,256]{2,1,0:T(8,128)S(1)} %all_to_all.23.source_ref), channel_id=1, source_target_pairs={{0,1},{1,0},{2,3},{3,2},{4,5},{5,4},{6,7},{7,6},{8,9},{9,8},{10,11... | collective-permute-start | bytes 393224 | tf_op jit(solution)/shard_map/ppermute | solution.py:225
  86.4 5.0 %shard_map.93 = (f32[3,256,128]{2,1,0:T(8,128)S(1)}, f32[3,256,128]{2,1,0:T(8,128)S(1)}) custom-call(f32[16,8,256]{2,1,0:T(8,128)S(1)} %all_to_all.23.source_ref, f32[8,256]{1,0:T(8,128)S(1)} %shard_map.92.own_ref.refs_1_), custom_call_target="tpu_custom_call" | custom-call | flops 32505856 | bytes 786432 | tf_op jit(solution)/shard_map/pallas_call | solution.py:233
  91.5 0.0 collective-permute-done.3.refs_0_
  91.5 5.6 %shard_map.94 = (f32[3,256]{1,0:T(4,128)}, f32[3,256]{1,0:T(4,128)}) custom-call(f32[16,8,256]{2,1,0:T(8,128)S(1)} %collective-permute-done.3.refs_0_, f32[8,256]{1,0:T(8,128)S(1)} %shard_map.92.own_ref.refs_1_, f32[3,256,128]{2,1,0:T(8,128)S(1)} %get-tuple-element.24.refs_2_, f32[3,256,128]{2,1,0:T(8,128)S(1)} %get-tuple-element.25.refs_3_), custom_call_target="tpu_custom_call" | custom-call | tf_op jit(solution)/shard_map/pallas_call | solution.py:245
  (3 shorter events, 0.0 us)
Async XLA Ops:
  2.4 19.0 %copy-start.1 = (f32[8,256]{1,0:T(8,128)S(1)}, f32[8,256]{1,0:T(8,128)}, u32[]{:S(2)}) copy-start(f32[8,256]{1,0:T(8,128)} %get-tuple-element.15.own_ref.refs_1_) | copy-start | bytes 24580
  19.1 7.3 %collective-permute-start = (f32[16,16,256]{2,1,0:T(8,128)S(1)}, f32[16,16,256]{2,1,0:T(8,128)S(1)}, u32[]{:S(2)}, u32[]{:S(2)}) collective-permute-start(f32[16,16,256]{2,1,0:T(8,128)S(1)} %all_to_all.20.source_ref.refs_5_), channel_id=1, source_target_pairs={{0,1},{1,0},{2,3},{3,2},{4,5},{5,4},{6,7},{7,6},{8,9},{9,8},{10,11... | collective-permute-start | bytes 786440 | tf_op jit(solution)/shard_map/ppermute | solution.py:225
  21.4 5.0 %copy-start = (s32[12,256]{1,0:T(8,128)S(1)}, s32[12,256]{1,0:T(8,128)}, u32[]{:S(2)}) copy-start(s32[12,256]{1,0:T(8,128)} %refs_4_.7) | copy-start | bytes 36868
  26.4 0.7 copy-start.2
  42.1 6.8 %collective-permute-start.1 = (f32[16,8,256]{2,1,0:T(8,128)S(1)}, f32[16,8,256]{2,1,0:T(8,128)S(1)}, u32[]{:S(2)}, u32[]{:S(2)}) collective-permute-start(f32[16,8,256]{2,1,0:T(8,128)S(1)} %all_to_all.21.source_ref), channel_id=1, source_target_pairs={{0,1},{1,0},{2,3},{3,2},{4,5},{5,4},{6,7},{7,6},{8,9},{9,8},{10,11... | collective-permute-start | bytes 393224 | tf_op jit(solution)/shard_map/ppermute | solution.py:225
  63.3 7.0 %collective-permute-start.2 = (f32[16,8,256]{2,1,0:T(8,128)S(1)}, f32[16,8,256]{2,1,0:T(8,128)S(1)}, u32[]{:S(2)}, u32[]{:S(2)}) collective-permute-start(f32[16,8,256]{2,1,0:T(8,128)S(1)} %all_to_all.22.source_ref), channel_id=1, source_target_pairs={{0,1},{1,0},{2,3},{3,2},{4,5},{5,4},{6,7},{7,6},{8,9},{9,8},{10,11... | collective-permute-start | bytes 393224 | tf_op jit(solution)/shard_map/ppermute | solution.py:225
  84.6 6.9 %collective-permute-start.3 = (f32[16,8,256]{2,1,0:T(8,128)S(1)}, f32[16,8,256]{2,1,0:T(8,128)S(1)}, u32[]{:S(2)}, u32[]{:S(2)}) collective-permute-start(f32[16,8,256]{2,1,0:T(8,128)S(1)} %all_to_all.23.source_ref), channel_id=1, source_target_pairs={{0,1},{1,0},{2,3},{3,2},{4,5},{5,4},{6,7},{7,6},{8,9},{9,8},{10,11... | collective-permute-start | bytes 393224 | tf_op jit(solution)/shard_map/ppermute | solution.py:225

commit v7 on v6

--- a/solution.py
+++ b/solution.py
@@ -12,7 +12,8 @@
 LANES = 128
 ROWS = 8
 TARGET_ROWS = 32
-PARAMS = 16
+PARAMS = 12
+FOLD = 4
 
 blob_square = 0.0025
 time_step = 0.5
@@ -23,7 +24,8 @@
 
 
 def pack_kernel(*refs):
-    inputs, (out_ref, state_ref), copies, semaphores = refs[:5], refs[5:7], refs[7:12], refs[12]
+    inputs, out_ref, copies = refs[:5], refs[5], refs[6:11]
+    slots_ref, semaphores = refs[11:]
     loads = [pltpu.make_async_copy(inputs[i], copies[i], semaphores.at[i]) for i in range(5)]
     for load in loads:
         load.start()
@@ -33,19 +35,21 @@
     chips = out_ref.shape[0]
     nodes = position_ref.shape[1]
     capacity = length_ref.shape[1] // (2 * chips)
-    state = jnp.concatenate(
-        [position_ref[...], force_ref[...], jnp.zeros((ROWS - 6, nodes), jnp.float32)], axis=0
-    )
-    state_ref[...] = state
+    state = [ref[c : c + 1, :] for ref in (position_ref, force_ref) for c in range(3)]
+    slots_ref[0:6, :] = length_ref[...]
+    slots_ref[6:8, :] = moduli_ref[...]
+    slots_ref[8:11, :] = bend_ref[...]
+    slots_ref[11:12, :] = bend_ref[0:1, :]
     for chip in range(chips):
-        out_ref[chip, 0:ROWS, :] = state
+        for c in range(6):
+            out_ref[chip, :, c * nodes : (c + 1) * nodes] = state[c]
         for core in range(2):
-            start = (2 * chip + core) * capacity
-            cut = slice(start, start + capacity)
-            lane = core * LANES
-            out_ref[chip, 8:14, lane : lane + capacity] = length_ref[:, cut]
-            out_ref[chip, 14:16, lane : lane + capacity] = moduli_ref[:, cut]
-            out_ref[chip, 8:11, lane + capacity : lane + 2 * capacity] = bend_ref[:, cut]
+            cut = slice((2 * chip + core) * capacity, (2 * chip + core + 1) * capacity)
+            for part in range(PARAMS // FOLD):
+                rows = slots_ref[part * FOLD : (part + 1) * FOLD, cut]
+                for t in range(FOLD):
+                    lane = 6 * nodes + (core * FOLD + t) * LANES + part * capacity
+                    out_ref[chip, :, lane : lane + capacity] = rows[t : t + 1, :]
 
 
 def pack(positions, forces, rest_length, moduli, rest_bend, devices):
@@ -53,13 +57,11 @@
     nodes = positions.shape[1]
     return pl.pallas_call(
         pack_kernel,
-        out_shape=(
-            jax.ShapeDtypeStruct((devices // 2, 2 * ROWS, 2 * LANES), jnp.float32),
-            jax.ShapeDtypeStruct((ROWS, nodes), jnp.float32),
-        ),
+        out_shape=jax.ShapeDtypeStruct((devices // 2, 1, 6 * nodes + 2 * FOLD * LANES), jnp.float32),
         in_specs=[pl.BlockSpec(memory_space=pl.ANY)] * 5,
-        out_specs=(VMEM,) * 2,
-        scratch_shapes=[pltpu.VMEM(x.shape, x.dtype) for x in operands] + [pltpu.SemaphoreType.DMA((5,))],
+        out_specs=VMEM,
+        scratch_shapes=[pltpu.VMEM(x.shape, x.dtype) for x in operands]
+        + [pltpu.VMEM((PARAMS, rest_length.shape[1]), jnp.float32), pltpu.SemaphoreType.DMA((5,))],
         compiler_params=pltpu.CompilerParams(vmem_limit_bytes=60 * 1024 * 1024),
     )(*operands)
 
@@ -67,6 +69,7 @@
 def pick_slots(capacity, near_ref, far_ref, owner_ref, params_ref):
     chips = near_ref.shape[0]
     nodes = owner_ref.shape[1]
+    parts = PARAMS // FOLD
     owner = owner_ref[...]
     across = jnp.broadcast_to(owner, (nodes, nodes))
     earlier = lax.broadcasted_iota(jnp.int32, (nodes, nodes), 0) < lax.broadcasted_iota(
@@ -74,35 +77,36 @@
     )
     rank = jnp.sum(jnp.where((across == across.T) & earlier, 1, 0), axis=0, keepdims=True)
     parity = lax.axis_index("src") & 1
-    lanes = pl.ds(pl.multiple_of(parity * LANES, LANES), LANES)
     spots = range(0, nodes, LANES)
-    places = [jnp.broadcast_to(rank[:, at : at + LANES], (ROWS, LANES)) for at in spots]
+    part = jnp.minimum(lax.broadcasted_iota(jnp.int32, (ROWS, LANES), 0), parts - 1)
+    places = [rank[:, at : at + LANES] + part * capacity for at in spots]
     owners = [jnp.broadcast_to(owner[:, at : at + LANES], (ROWS, LANES)) for at in spots]
 
     def choose(chip, chosen):
         chosen = list(chosen)
         for ref, device in ((near_ref, 2 * chip + parity), (far_ref, 2 * chip + 1 - parity)):
-            block = ref[chip, ROWS : 2 * ROWS, lanes]
-            for i in range(len(spots)):
-                for part in range(2):
-                    taken = jnp.take_along_axis(
-                        block, places[i] + part * capacity, axis=1, mode="promise_in_bounds"
-                    )
-                    at = 2 * i + part
+            for t in range(FOLD):
+                lane = pl.multiple_of(6 * nodes + (parity * FOLD + t) * LANES, LANES)
+                block = jnp.broadcast_to(ref[chip, :, pl.ds(lane, LANES)], (ROWS, LANES))
+                for i in range(len(spots)):
+                    taken = jnp.take_along_axis(block, places[i], axis=1, mode="promise_in_bounds")
+                    at = i * FOLD + t
                     chosen[at] = jnp.where(owners[i] == device, taken, chosen[at])
         return tuple(chosen)
 
     zero = jnp.zeros((ROWS, LANES), jnp.float32)
-    chosen = lax.fori_loop(0, chips, choose, (zero,) * (2 * len(spots)), unroll=4)
+    chosen = lax.fori_loop(0, chips, choose, (zero,) * (FOLD * len(spots)), unroll=4)
     for i, at in enumerate(spots):
-        for part in range(2):
-            params_ref[part * ROWS : (part + 1) * ROWS, at : at + LANES] = chosen[2 * i + part]
+        for t in range(FOLD):
+            for j in range(parts):
+                params_ref[j * FOLD + t : j * FOLD + t + 1, at : at + LANES] = chosen[i * FOLD + t][j : j + 1, :]
 
 
 def spread_columns(own_ref, column_ref):
+    nodes = column_ref.shape[1]
     for c in range(3):
-        for at in range(0, own_ref.shape[1], LANES):
-            row = own_ref[c : c + 1, at : at + LANES]
+        for at in range(0, nodes, LANES):
+            row = own_ref[0, :, c * nodes + at : c * nodes + at + LANES]
             column_ref[c, at : at + LANES, :] = jnp.broadcast_to(row, (LANES, LANES)).T
 
 
@@ -120,8 +124,8 @@
 
             def per_source(device, totals):
                 for at in range(0, nodes, LANES):
-                    x = [source_ref[device, c : c + 1, at : at + LANES] for c in range(3)]
-                    f = [source_ref[device, 3 + c : 4 + c, at : at + LANES] for c in range(3)]
+                    rows = [source_ref[device, :, c * nodes + at : c * nodes + at + LANES] for c in range(6)]
+                    x, f = rows[:3], rows[3:]
                     d = [target[c] - x[c] for c in range(3)]
                     shifted = d[0] * d[0] + (d[1] * d[1] + (d[2] * d[2] + blob_square))
                     r = lax.rsqrt(shifted)
@@ -189,12 +193,13 @@
 
 def advance(scale, own_ref, sum_ref, neighbours_ref, params_ref, out_ref):
     velocity = velocity_rows(sum_ref, scale)
-    x = [own_ref[c : c + 1, :] + time_step * velocity[c] for c in range(3)]
+    nodes = velocity[0].shape[1]
+    x = [own_ref[0, :, c * nodes : (c + 1) * nodes] + time_step * velocity[c] for c in range(3)]
     force = membrane(x, neighbours_ref, params_ref)
-    for c in range(3):
-        out_ref[c : c + 1, :] = x[c]
-        out_ref[3 + c : 4 + c, :] = force[c]
-    out_ref[6:ROWS, :] = jnp.zeros((ROWS - 6, x[0].shape[1]), jnp.float32)
+    for chip in range(out_ref.shape[0]):
+        for c in range(3):
+            out_ref[chip, :, c * nodes : (c + 1) * nodes] = x[c]
+            out_ref[chip, :, (3 + c) * nodes : (4 + c) * nodes] = force[c]
 
 
 def first_kernel(scale, capacity, *refs):
@@ -214,8 +219,9 @@
     far_ref, own_ref, column_ref, start_ref, position_ref, velocity_ref, sum_ref = refs
     pair_sums([far_ref], column_ref, start_ref, sum_ref)
     velocity = velocity_rows(sum_ref, scale)
-    position_ref[...] = own_ref[0:3, :]
+    nodes = velocity[0].shape[1]
     for c in range(3):
+        position_ref[c : c + 1, :] = own_ref[0, :, c * nodes : (c + 1) * nodes]
         velocity_ref[c : c + 1, :] = velocity[c]
 
 
@@ -226,8 +232,7 @@
     return near, far
 
 
-def near_sums(near, state):
-    nodes = state.shape[1]
+def near_sums(near, copies, nodes):
     shape = jax.ShapeDtypeStruct((3, nodes, LANES), jnp.float32)
     pairs = near.shape[0] * nodes * nodes
     return pl.pallas_call(
@@ -237,11 +242,10 @@
         out_specs=(VMEM,) * 2,
         compiler_params=GRANT,
         cost_estimate=pl.CostEstimate(flops=31 * pairs, bytes_accessed=8 * 3 * nodes * LANES, transcendentals=pairs),
-    )(near, state)
-
-
-def call(kernel, out_shape, operands):
-    nodes = operands[1].shape[1]
+    )(near, copies)
+
+
+def call(kernel, out_shape, operands, nodes):
     return pl.pallas_call(
         kernel,
         out_shape=out_shape,
@@ -257,24 +261,25 @@
     nodes = positions.shape[1]
     scale = 1.0 / math.sqrt(devices * nodes)
     capacity = rest_length.shape[1] // devices
-    state_shape = jax.ShapeDtypeStruct((ROWS, nodes), jnp.float32)
+    copies_shape = jax.ShapeDtypeStruct((devices // 2, 1, 6 * nodes), jnp.float32)
     params_shape = jax.ShapeDtypeStruct((PARAMS, nodes), jnp.float32)
     row_shape = jax.ShapeDtypeStruct((3, nodes), jnp.float32)
-    copies, state = pack(positions, forces, rest_length, moduli, rest_bend, devices)
+    copies = pack(positions, forces, rest_length, moduli, rest_bend, devices)
     for step in range(STEPS + 1):
         near, far = spread(copies, devices)
-        column, start = near_sums(near, state)
-        operands = (far, state, column, start)
+        column, start = near_sums(near, copies, nodes)
+        operands = (far, copies, column, start)
         if step == 0:
-            state, params = call(
+            copies, params = call(
                 functools.partial(first_kernel, scale, capacity),
-                (state_shape, params_shape),
+                (copies_shape, params_shape),
                 operands + (neighbours, near, patch_owner.reshape(1, nodes)),
+                nodes,
             )
         elif step < STEPS:
-            state = call(functools.partial(step_kernel, scale), state_shape, operands + (neighbours, params))
-        copies = jnp.broadcast_to(state[None], (devices // 2,) + state.shape)
-    return call(functools.partial(last_kernel, scale), (row_shape, row_shape), operands)
+            operands = operands + (neighbours, params)
+            copies = call(functools.partial(step_kernel, scale), copies_shape, operands, nodes)
+    return call(functools.partial(last_kernel, scale), (row_shape, row_shape), operands, nodes)
 
 
 def solution(mesh):

time: 97.5 us -> 93.7 us (0.961)
  blocking collectives: 44.2 us -> 41.3 us
  starting transfers between devices: 8.04 us -> 6.97 us
    all_to_all x4, blocking collectives: 44.2 us -> 41.3 us  [spread(): lax.all_to_all(copies, AXES, split_axis=0, concat_axis=0, axis_index_grou...]
    ppermute x4, starting transfers between devices: 8.04 us -> 6.97 us  [spread(): far = lax.ppermute(near, AXES, [(i, i ^ 1) for i in range(devices)])]
where the time goes in v7:
time: 93.7 us; the launch traced here: 93.3 us
  Pallas kernels  43.5 us (46%)
  blocking collectives  41.3 us (44%)
  starting transfers between devices  6.97 us (7%)
    all_to_all x4, blocking collectives, spread(): lax.all_to_all(copies, AXES, split_axis=0, concat_axis=0, axis_index_grou...  41.3 us
    pallas_call x4, Pallas kernels, call(): pl.pallas_call(kernel, out_shape=out_shape, in_specs=[VMEM] * len(operand...  21.6 us
    pallas_call x4, Pallas kernels, near_sums(): pl.pallas_call(near_kernel, out_shape=(shape, shape), in_specs=[VMEM] * 2...  20 us
    ppermute x4, starting transfers between devices, spread(): far = lax.ppermute(near, AXES, [(i, i ^ 1) for i in range(devices)])  6.97 us
    pallas_call x1, Pallas kernels, pack(): pl.pallas_call(pack_kernel, out_shape=jax.ShapeDtypeStruct((devices // 2,...  1.97 us
  transfers between devices with their start and end apart: 4, of which 0 were waited for; matrix products, arithmetic and copies ran while one was open for 0% of the time, Pallas kernels for 21%

profile of v7, /device:TPU:1, one launch (start us, length us, event | category | flops | bytes accessed | tf_op | source)
XLA Modules:
  0.0 93.3 jit_solution(8693359105395652667)
XLA Ops:
  0.6 2.0 %shard_map.86.own_ref.refs_1_ = f32[16,1,2560]{2,1,0:T(1,128)} custom-call(f32[3,256]{1,0:T(4,128)} %refs_0_.1, f32[3,256]{1,0:T(4,128)} %refs_1_.1, f32[6,1280]{1,0:T(8,128)} %refs_2_.1, f32[2,1280]{1,0:T(2,128)} %refs_3_.1, f32[3,1280]{1,0:T(4,128)} %refs_4_.4), custom_call_target="tpu_custom_call" | custom-call | tf_op jit(solution)/shard_map/pallas_call | solution.py:58
  2.6 0.0 copy-start
  2.6 14.1 %all_to_all.20.source_ref.refs_5_ = f32[16,1,2560]{2,1,0:T(1,128)S(1)} all-to-all(f32[16,1,2560]{2,1,0:T(1,128)} %shard_map.86.own_ref.refs_1_), channel_id=1, replica_groups={{0,2,4,6,8,10,12,14,16,18,20,22,24,26,28,30},{1,3,5,7,9,11,13,15,17,19,..., dimensions={0} | all-to-all | bytes 327680 | tf_op jit(solution)/shard_map/all_to_all | solution.py:230
  16.7 2.9 %collective-permute-start = (f32[16,1,2560]{2,1,0:T(1,128)S(1)}, f32[16,1,2560]{2,1,0:T(1,128)S(1)}, u32[]{:S(2)}, u32[]{:S(2)}) collective-permute-start(f32[16,1,2560]{2,1,0:T(1,128)S(1)} %all_to_all.20.source_ref.refs_5_), channel_id=1, source_target_pairs={{0,1},{1,0},{2,3},{3,2},{4,5},{5,4},{6,7},{7,6},{8,9},{9,8},{10,11... | collective-permute-start | bytes 491528 | tf_op jit(solution)/shard_map/ppermute | solution.py:231
  19.6 0.0 copy-done
  19.6 0.0 copy-start.1
  19.6 5.0 %shard_map.87 = (f32[3,256,128]{2,1,0:T(8,128)S(1)}, f32[3,256,128]{2,1,0:T(8,128)S(1)}) custom-call(f32[16,1,2560]{2,1,0:T(1,128)S(1)} %all_to_all.20.source_ref.refs_5_, f32[16,1,2560]{2,1,0:T(1,128)S(1)} %copy-done), custom_call_target="tpu_custom_call" | custom-call | flops 32505856 | bytes 786432 | tf_op jit(solution)/shard_map/pallas_call | solution.py:238
  24.6 0.0 collective-permute-done.refs_0_
  24.6 0.0 copy-start.2
  24.6 0.0 copy-done.1
  24.6 0.7 copy-done.2
  25.3 5.8 %shard_map.88 = (f32[16,1,1536]{2,1,0:T(1,128)S(1)}, f32[12,256]{1,0:T(8,128)S(1)}) custom-call(f32[16,1,2560]{2,1,0:T(1,128)S(1)} %collective-permute-done.refs_0_, f32[16,1,2560]{2,1,0:T(1,128)S(1)} %copy-done, f32[3,256,128]{2,1,0:T(8,128)S(1)} %get-tuple-element.12.refs_2_, f32[3,256,128]{2,1,0:T(8,128)S(1)} %get-tuple-element.13.refs_3_, ...), custom_call_target="tpu_custom_call" | custom-call | tf_op jit(solution)/shard_map/pallas_call | solution.py:249
  31.1 9.1 %all_to_all.21.source_ref = f32[16,1,1536]{2,1,0:T(1,128)S(1)} all-to-all(f32[16,1,1536]{2,1,0:T(1,128)S(1)} %get-tuple-element.14.own_ref.refs_1_), channel_id=1, replica_groups={{0,2,4,6,8,10,12,14,16,18,20,22,24,26,28,30},{1,3,5,7,9,11,13,15,17,19,..., dimensions={0} | all-to-all | bytes 196608 | tf_op jit(solution)/shard_map/all_to_all | solution.py:230
  40.2 1.3 %collective-permute-start.1 = (f32[16,1,1536]{2,1,0:T(1,128)S(1)}, f32[16,1,1536]{2,1,0:T(1,128)S(1)}, u32[]{:S(2)}, u32[]{:S(2)}) collective-permute-start(f32[16,1,1536]{2,1,0:T(1,128)S(1)} %all_to_all.21.source_ref), channel_id=1, source_target_pairs={{0,1},{1,0},{2,3},{3,2},{4,5},{5,4},{6,7},{7,6},{8,9},{9,8},{10,11... | collective-permute-start | bytes 294920 | tf_op jit(solution)/shard_map/ppermute | solution.py:231
  41.5 5.0 %shard_map.89 = (f32[3,256,128]{2,1,0:T(8,128)S(1)}, f32[3,256,128]{2,1,0:T(8,128)S(1)}) custom-call(f32[16,1,1536]{2,1,0:T(1,128)S(1)} %all_to_all.21.source_ref, f32[16,1,1536]{2,1,0:T(1,128)S(1)} %get-tuple-element.14.own_ref.refs_1_), custom_call_target="tpu_custom_call" | custom-call | flops 32505856 | bytes 786432 | tf_op jit(solution)/shard_map/pallas_call | solution.py:238
  46.5 0.0 collective-permute-done.1.refs_0_
  46.5 5.1 %shard_map.90.own_ref.refs_1_ = f32[16,1,1536]{2,1,0:T(1,128)S(1)} custom-call(f32[16,1,1536]{2,1,0:T(1,128)S(1)} %collective-permute-done.1.refs_0_, f32[16,1,1536]{2,1,0:T(1,128)S(1)} %get-tuple-element.14.own_ref.refs_1_, f32[3,256,128]{2,1,0:T(8,128)S(1)} %get-tuple-element.15.refs_2_, f32[3,256,128]{2,1,0:T(8,128)S(1)} %get-tuple-element.16.refs_3_, ...), custom_call_target="tpu_custom_call" | custom-call | tf_op jit(solution)/shard_map/pallas_call | solution.py:249
  51.6 9.1 %all_to_all.22.source_ref = f32[16,1,1536]{2,1,0:T(1,128)S(1)} all-to-all(f32[16,1,1536]{2,1,0:T(1,128)S(1)} %shard_map.90.own_ref.refs_1_), channel_id=1, replica_groups={{0,2,4,6,8,10,12,14,16,18,20,22,24,26,28,30},{1,3,5,7,9,11,13,15,17,19,..., dimensions={0} | all-to-all | bytes 196608 | tf_op jit(solution)/shard_map/all_to_all | solution.py:230
  60.7 1.5 %collective-permute-start.2 = (f32[16,1,1536]{2,1,0:T(1,128)S(1)}, f32[16,1,1536]{2,1,0:T(1,128)S(1)}, u32[]{:S(2)}, u32[]{:S(2)}) collective-permute-start(f32[16,1,1536]{2,1,0:T(1,128)S(1)} %all_to_all.22.source_ref), channel_id=1, source_target_pairs={{0,1},{1,0},{2,3},{3,2},{4,5},{5,4},{6,7},{7,6},{8,9},{9,8},{10,11... | collective-permute-start | bytes 294920 | tf_op jit(solution)/shard_map/ppermute | solution.py:231
  62.2 5.0 %shard_map.91 = (f32[3,256,128]{2,1,0:T(8,128)S(1)}, f32[3,256,128]{2,1,0:T(8,128)S(1)}) custom-call(f32[16,1,1536]{2,1,0:T(1,128)S(1)} %all_to_all.22.source_ref, f32[16,1,1536]{2,1,0:T(1,128)S(1)} %shard_map.90.own_ref.refs_1_), custom_call_target="tpu_custom_call" | custom-call | flops 32505856 | bytes 786432 | tf_op jit(solution)/shard_map/pallas_call | solution.py:238
  67.2 0.0 collective-permute-done.2.refs_0_
  67.2 5.1 %shard_map.92.own_ref.refs_1_ = f32[16,1,1536]{2,1,0:T(1,128)S(1)} custom-call(f32[16,1,1536]{2,1,0:T(1,128)S(1)} %collective-permute-done.2.refs_0_, f32[16,1,1536]{2,1,0:T(1,128)S(1)} %shard_map.90.own_ref.refs_1_, f32[3,256,128]{2,1,0:T(8,128)S(1)} %get-tuple-element.18.refs_2_, f32[3,256,128]{2,1,0:T(8,128)S(1)} %get-tuple-element.19.refs_3_, ...), custom_call_target="tpu_custom_call" | custom-call | tf_op jit(solution)/shard_map/pallas_call | solution.py:249
  72.3 9.1 %all_to_all.23.source_ref = f32[16,1,1536]{2,1,0:T(1,128)S(1)} all-to-all(f32[16,1,1536]{2,1,0:T(1,128)S(1)} %shard_map.92.own_ref.refs_1_), channel_id=1, replica_groups={{0,2,4,6,8,10,12,14,16,18,20,22,24,26,28,30},{1,3,5,7,9,11,13,15,17,19,..., dimensions={0} | all-to-all | bytes 196608 | tf_op jit(solution)/shard_map/all_to_all | solution.py:230
  81.4 1.3 %collective-permute-start.3 = (f32[16,1,1536]{2,1,0:T(1,128)S(1)}, f32[16,1,1536]{2,1,0:T(1,128)S(1)}, u32[]{:S(2)}, u32[]{:S(2)}) collective-permute-start(f32[16,1,1536]{2,1,0:T(1,128)S(1)} %all_to_all.23.source_ref), channel_id=1, source_target_pairs={{0,1},{1,0},{2,3},{3,2},{4,5},{5,4},{6,7},{7,6},{8,9},{9,8},{10,11... | collective-permute-start | bytes 294920 | tf_op jit(solution)/shard_map/ppermute | solution.py:231
  82.7 5.0 %shard_map.93 = (f32[3,256,128]{2,1,0:T(8,128)S(1)}, f32[3,256,128]{2,1,0:T(8,128)S(1)}) custom-call(f32[16,1,1536]{2,1,0:T(1,128)S(1)} %all_to_all.23.source_ref, f32[16,1,1536]{2,1,0:T(1,128)S(1)} %shard_map.92.own_ref.refs_1_), custom_call_target="tpu_custom_call" | custom-call | flops 32505856 | bytes 786432 | tf_op jit(solution)/shard_map/pallas_call | solution.py:238
  87.7 0.0 collective-permute-done.3.refs_0_
  87.7 5.6 %shard_map.94 = (f32[3,256]{1,0:T(4,128)}, f32[3,256]{1,0:T(4,128)}) custom-call(f32[16,1,1536]{2,1,0:T(1,128)S(1)} %collective-permute-done.3.refs_0_, f32[16,1,1536]{2,1,0:T(1,128)S(1)} %shard_map.92.own_ref.refs_1_, f32[3,256,128]{2,1,0:T(8,128)S(1)} %get-tuple-element.20.refs_2_, f32[3,256,128]{2,1,0:T(8,128)S(1)} %get-tuple-element.21.refs_3_), custom_call_target="tpu_custom_call" | custom-call | tf_op jit(solution)/shard_map/pallas_call | solution.py:249
Async XLA Ops:
  2.6 17.0 %copy-start = (f32[16,1,2560]{2,1,0:T(1,128)S(1)}, f32[16,1,2560]{2,1,0:T(1,128)}, u32[]{:S(2)}) copy-start(f32[16,1,2560]{2,1,0:T(1,128)} %shard_map.86.own_ref.refs_1_) | copy-start | bytes 491524
  16.7 7.9 %collective-permute-start = (f32[16,1,2560]{2,1,0:T(1,128)S(1)}, f32[16,1,2560]{2,1,0:T(1,128)S(1)}, u32[]{:S(2)}, u32[]{:S(2)}) collective-permute-start(f32[16,1,2560]{2,1,0:T(1,128)S(1)} %all_to_all.20.source_ref.refs_5_), channel_id=1, source_target_pairs={{0,1},{1,0},{2,3},{3,2},{4,5},{5,4},{6,7},{7,6},{8,9},{9,8},{10,11... | collective-permute-start | bytes 491528 | tf_op jit(solution)/shard_map/ppermute | solution.py:231
  19.6 5.0 %copy-start.1 = (s32[12,256]{1,0:T(8,128)S(1)}, s32[12,256]{1,0:T(8,128)}, u32[]{:S(2)}) copy-start(s32[12,256]{1,0:T(8,128)} %refs_4_.7) | copy-start | bytes 36868
  24.6 0.7 copy-start.2
  40.2 6.3 %collective-permute-start.1 = (f32[16,1,1536]{2,1,0:T(1,128)S(1)}, f32[16,1,1536]{2,1,0:T(1,128)S(1)}, u32[]{:S(2)}, u32[]{:S(2)}) collective-permute-start(f32[16,1,1536]{2,1,0:T(1,128)S(1)} %all_to_all.21.source_ref), channel_id=1, source_target_pairs={{0,1},{1,0},{2,3},{3,2},{4,5},{5,4},{6,7},{7,6},{8,9},{9,8},{10,11... | collective-permute-start | bytes 294920 | tf_op jit(solution)/shard_map/ppermute | solution.py:231
  60.7 6.5 %collective-permute-start.2 = (f32[16,1,1536]{2,1,0:T(1,128)S(1)}, f32[16,1,1536]{2,1,0:T(1,128)S(1)}, u32[]{:S(2)}, u32[]{:S(2)}) collective-permute-start(f32[16,1,1536]{2,1,0:T(1,128)S(1)} %all_to_all.22.source_ref), channel_id=1, source_target_pairs={{0,1},{1,0},{2,3},{3,2},{4,5},{5,4},{6,7},{7,6},{8,9},{9,8},{10,11... | collective-permute-start | bytes 294920 | tf_op jit(solution)/shard_map/ppermute | solution.py:231
  81.4 6.3 %collective-permute-start.3 = (f32[16,1,1536]{2,1,0:T(1,128)S(1)}, f32[16,1,1536]{2,1,0:T(1,128)S(1)}, u32[]{:S(2)}, u32[]{:S(2)}) collective-permute-start(f32[16,1,1536]{2,1,0:T(1,128)S(1)} %all_to_all.23.source_ref), channel_id=1, source_target_pairs={{0,1},{1,0},{2,3},{3,2},{4,5},{5,4},{6,7},{7,6},{8,9},{9,8},{10,11... | collective-permute-start | bytes 294920 | tf_op jit(solution)/shard_map/ppermute | solution.py:231

commit v8 on v7

--- a/solution.py
+++ b/solution.py
@@ -12,10 +12,12 @@
 LANES = 128
 ROWS = 8
 TARGET_ROWS = 32
+UNROLL = 8
 PARAMS = 12
 FOLD = 4
 
 blob_square = 0.0025
+inverse_blob = 20.0
 time_step = 0.5
 
 AXES = ("tgt", "src")
@@ -35,7 +37,8 @@
     chips = out_ref.shape[0]
     nodes = position_ref.shape[1]
     capacity = length_ref.shape[1] // (2 * chips)
-    state = [ref[c : c + 1, :] for ref in (position_ref, force_ref) for c in range(3)]
+    state = [inverse_blob * position_ref[c : c + 1, :] for c in range(3)]
+    state += [force_ref[c : c + 1, :] for c in range(3)]
     slots_ref[0:6, :] = length_ref[...]
     slots_ref[6:8, :] = moduli_ref[...]
     slots_ref[8:11, :] = bend_ref[...]
@@ -127,10 +130,10 @@
                     rows = [source_ref[device, :, c * nodes + at : c * nodes + at + LANES] for c in range(6)]
                     x, f = rows[:3], rows[3:]
                     d = [target[c] - x[c] for c in range(3)]
-                    shifted = d[0] * d[0] + (d[1] * d[1] + (d[2] * d[2] + blob_square))
+                    shifted = d[0] * d[0] + (d[1] * d[1] + (d[2] * d[2] + 1.0))
                     r = lax.rsqrt(shifted)
                     cube = r * (r * r)
-                    direct = r + blob_square * cube
+                    direct = r + cube
                     along = (d[0] * f[0] + d[1] * f[1] + d[2] * f[2]) * cube
                     totals = tuple(totals[c] + (direct * f[c] + along * d[c]) for c in range(3))
                 return totals
@@ -151,7 +154,7 @@
             jnp.sum(sum_ref[c, at : at + LANES, :].T, axis=0, keepdims=True)
             for at in range(0, nodes, LANES)
         ]
-        velocity.append(jnp.concatenate(parts, axis=1) * scale)
+        velocity.append(jnp.concatenate(parts, axis=1) * (inverse_blob * scale))
     return velocity
 
 
@@ -191,37 +194,38 @@
     pair_sums([source_ref], column_ref, None, sum_ref)
 
 
-def advance(scale, own_ref, sum_ref, neighbours_ref, params_ref, out_ref):
+def advance(scale, position_ref, sum_ref, neighbours_ref, params_ref, out_ref, moved_ref):
     velocity = velocity_rows(sum_ref, scale)
     nodes = velocity[0].shape[1]
-    x = [own_ref[0, :, c * nodes : (c + 1) * nodes] + time_step * velocity[c] for c in range(3)]
+    x = [position_ref[c : c + 1, :] + time_step * velocity[c] for c in range(3)]
+    for c in range(3):
+        moved_ref[c : c + 1, :] = x[c]
+    scaled = [inverse_blob * v for v in x]
     force = membrane(x, neighbours_ref, params_ref)
     for chip in range(out_ref.shape[0]):
         for c in range(3):
-            out_ref[chip, :, c * nodes : (c + 1) * nodes] = x[c]
+            out_ref[chip, :, c * nodes : (c + 1) * nodes] = scaled[c]
             out_ref[chip, :, (3 + c) * nodes : (4 + c) * nodes] = force[c]
 
 
 def first_kernel(scale, capacity, *refs):
-    far_ref, own_ref, column_ref, start_ref, neighbours_ref, near_ref, owner_ref, out_ref, params_ref, sum_ref = refs
+    far_ref, position_ref, column_ref, start_ref, neighbours_ref, near_ref, owner_ref = refs[:7]
+    out_ref, moved_ref, params_ref, sum_ref = refs[7:]
     pick_slots(capacity, near_ref, far_ref, owner_ref, params_ref)
     pair_sums([far_ref], column_ref, start_ref, sum_ref)
-    advance(scale, own_ref, sum_ref, neighbours_ref, params_ref, out_ref)
+    advance(scale, position_ref, sum_ref, neighbours_ref, params_ref, out_ref, moved_ref)
 
 
 def step_kernel(scale, *refs):
-    far_ref, own_ref, column_ref, start_ref, neighbours_ref, params_ref, out_ref, sum_ref = refs
+    far_ref, position_ref, column_ref, start_ref, neighbours_ref, params_ref, out_ref, moved_ref, sum_ref = refs
     pair_sums([far_ref], column_ref, start_ref, sum_ref)
-    advance(scale, own_ref, sum_ref, neighbours_ref, params_ref, out_ref)
-
-
-def last_kernel(scale, *refs):
-    far_ref, own_ref, column_ref, start_ref, position_ref, velocity_ref, sum_ref = refs
+    advance(scale, position_ref, sum_ref, neighbours_ref, params_ref, out_ref, moved_ref)
+
+
+def last_kernel(scale, far_ref, column_ref, start_ref, velocity_ref, sum_ref):
     pair_sums([far_ref], column_ref, start_ref, sum_ref)
     velocity = velocity_rows(sum_ref, scale)
-    nodes = velocity[0].shape[1]
     for c in range(3):
-        position_ref[c : c + 1, :] = own_ref[0, :, c * nodes : (c + 1) * nodes]
         velocity_ref[c : c + 1, :] = velocity[c]
 
 
@@ -264,22 +268,25 @@
     copies_shape = jax.ShapeDtypeStruct((devices // 2, 1, 6 * nodes), jnp.float32)
     params_shape = jax.ShapeDtypeStruct((PARAMS, nodes), jnp.float32)
     row_shape = jax.ShapeDtypeStruct((3, nodes), jnp.float32)
+    position = positions
     copies = pack(positions, forces, rest_length, moduli, rest_bend, devices)
     for step in range(STEPS + 1):
         near, far = spread(copies, devices)
         column, start = near_sums(near, copies, nodes)
-        operands = (far, copies, column, start)
+        operands = (far, position, column, start)
         if step == 0:
-            copies, params = call(
+            copies, position, params = call(
                 functools.partial(first_kernel, scale, capacity),
-                (copies_shape, params_shape),
+                (copies_shape, row_shape, params_shape),
                 operands + (neighbours, near, patch_owner.reshape(1, nodes)),
                 nodes,
             )
         elif step < STEPS:
             operands = operands + (neighbours, params)
-            copies = call(functools.partial(step_kernel, scale), copies_shape, operands, nodes)
-    return call(functools.partial(last_kernel, scale), (row_shape, row_shape), operands, nodes)
+            shapes = (copies_shape, row_shape)
+            copies, position = call(functools.partial(step_kernel, scale), shapes, operands, nodes)
+    velocity = call(functools.partial(last_kernel, scale), row_shape, (far, column, start), nodes)
+    return position, velocity
 
 
 def solution(mesh):

time: 93.7 us -> 93.1 us (level)
  no operation moved by 1% of the time
where the time goes in v8:
time: 93.1 us; the launch traced here: 92.6 us
  Pallas kernels  42.9 us (46%)
  blocking collectives  41.3 us (44%)
  starting transfers between devices  6.97 us (7%)
    all_to_all x4, blocking collectives, spread(): lax.all_to_all(copies, AXES, split_axis=0, concat_axis=0, axis_index_grou...  41.3 us
    pallas_call x4, Pallas kernels, call(): pl.pallas_call(kernel, out_shape=out_shape, in_specs=[VMEM] * len(operand...  21.5 us
    pallas_call x4, Pallas kernels, near_sums(): pl.pallas_call(near_kernel, out_shape=(shape, shape), in_specs=[VMEM] * 2...  19.4 us
    ppermute x4, starting transfers between devices, spread(): far = lax.ppermute(near, AXES, [(i, i ^ 1) for i in range(devices)])  6.97 us
    pallas_call x1, Pallas kernels, pack(): pl.pallas_call(pack_kernel, out_shape=jax.ShapeDtypeStruct((devices // 2,...  1.98 us
  transfers between devices with their start and end apart: 4, of which 0 were waited for; matrix products, arithmetic and copies ran while one was open for 0% of the time, Pallas kernels for 21%

profile of v8, /device:TPU:1, one launch (start us, length us, event | category | flops | bytes accessed | tf_op | source)
XLA Modules:
  0.0 92.6 jit_solution(14869468776969608955)
XLA Ops:
  0.6 2.0 %shard_map.86.own_ref = f32[16,1,2560]{2,1,0:T(1,128)} custom-call(f32[3,256]{1,0:T(4,128)} %refs_1_.3, f32[3,256]{1,0:T(4,128)} %refs_1_.2, f32[6,1280]{1,0:T(8,128)} %refs_2_.1, f32[2,1280]{1,0:T(2,128)} %refs_3_.1, f32[3,1280]{1,0:T(4,128)} %refs_4_.4), custom_call_target="tpu_custom_call" | custom-call | tf_op jit(solution)/shard_map/pallas_call | solution.py:61
  2.6 0.0 copy-start
  2.6 14.1 %all_to_all.20.source_ref.refs_5_ = f32[16,1,2560]{2,1,0:T(1,128)S(1)} all-to-all(f32[16,1,2560]{2,1,0:T(1,128)} %shard_map.86.own_ref), channel_id=1, replica_groups={{0,2,4,6,8,10,12,14,16,18,20,22,24,26,28,30},{1,3,5,7,9,11,13,15,17,19,..., dimensions={0} | all-to-all | bytes 327680 | tf_op jit(solution)/shard_map/all_to_all | solution.py:234
  16.7 2.9 %collective-permute-start = (f32[16,1,2560]{2,1,0:T(1,128)S(1)}, f32[16,1,2560]{2,1,0:T(1,128)S(1)}, u32[]{:S(2)}, u32[]{:S(2)}) collective-permute-start(f32[16,1,2560]{2,1,0:T(1,128)S(1)} %all_to_all.20.source_ref.refs_5_), channel_id=1, source_target_pairs={{0,1},{1,0},{2,3},{3,2},{4,5},{5,4},{6,7},{7,6},{8,9},{9,8},{10,11... | collective-permute-start | bytes 491528 | tf_op jit(solution)/shard_map/ppermute | solution.py:235
  19.6 0.0 copy-done
  19.6 0.0 copy-start.1
  19.6 4.9 %shard_map.87 = (f32[3,256,128]{2,1,0:T(8,128)S(1)}, f32[3,256,128]{2,1,0:T(8,128)S(1)}) custom-call(f32[16,1,2560]{2,1,0:T(1,128)S(1)} %all_to_all.20.source_ref.refs_5_, f32[16,1,2560]{2,1,0:T(1,128)S(1)} %copy-done), custom_call_target="tpu_custom_call" | custom-call | flops 32505856 | bytes 786432 | tf_op jit(solution)/shard_map/pallas_call | solution.py:242
  24.5 0.0 copy-start.2
  24.5 0.0 collective-permute-done.refs_0_
  24.5 0.0 copy-start.3
  24.5 0.0 copy-done.1
  24.5 0.6 copy-done.2
  25.2 0.0 copy-done.3
  25.2 5.6 %shard_map.88 = (f32[16,1,1536]{2,1,0:T(1,128)S(1)}, f32[3,256]{1,0:T(4,128)S(1)}, f32[12,256]{1,0:T(8,128)S(1)}) custom-call(f32[16,1,2560]{2,1,0:T(1,128)S(1)} %collective-permute-done.refs_0_, f32[3,256]{1,0:T(4,128)S(1)} %copy-done.2, f32[3,256,128]{2,1,0:T(8,128)S(1)} %get-tuple-element.17.refs_2_, f32[3,256,128]{2,1,0:T(8,128)S(1)} %get-tuple-element.18.refs_3_, ...), custom_call_target="tpu_custom_call" | custom-call | tf_op jit(solution)/shard_map/pallas_call | solution.py:253
  30.8 9.1 %all_to_all.21.source_ref = f32[16,1,1536]{2,1,0:T(1,128)S(1)} all-to-all(f32[16,1,1536]{2,1,0:T(1,128)S(1)} %get-tuple-element.19.own_ref), channel_id=1, replica_groups={{0,2,4,6,8,10,12,14,16,18,20,22,24,26,28,30},{1,3,5,7,9,11,13,15,17,19,..., dimensions={0} | all-to-all | bytes 196608 | tf_op jit(solution)/shard_map/all_to_all | solution.py:234
  39.9 1.3 %collective-permute-start.1 = (f32[16,1,1536]{2,1,0:T(1,128)S(1)}, f32[16,1,1536]{2,1,0:T(1,128)S(1)}, u32[]{:S(2)}, u32[]{:S(2)}) collective-permute-start(f32[16,1,1536]{2,1,0:T(1,128)S(1)} %all_to_all.21.source_ref), channel_id=1, source_target_pairs={{0,1},{1,0},{2,3},{3,2},{4,5},{5,4},{6,7},{7,6},{8,9},{9,8},{10,11... | collective-permute-start | bytes 294920 | tf_op jit(solution)/shard_map/ppermute | solution.py:235
  41.2 4.9 %shard_map.89 = (f32[3,256,128]{2,1,0:T(8,128)S(1)}, f32[3,256,128]{2,1,0:T(8,128)S(1)}) custom-call(f32[16,1,1536]{2,1,0:T(1,128)S(1)} %all_to_all.21.source_ref, f32[16,1,1536]{2,1,0:T(1,128)S(1)} %get-tuple-element.19.own_ref), custom_call_target="tpu_custom_call" | custom-call | flops 32505856 | bytes 786432 | tf_op jit(solution)/shard_map/pallas_call | solution.py:242
  46.1 0.0 collective-permute-done.1.refs_0_
  46.1 5.0 %shard_map.90 = (f32[16,1,1536]{2,1,0:T(1,128)S(1)}, f32[3,256]{1,0:T(4,128)S(1)}) custom-call(f32[16,1,1536]{2,1,0:T(1,128)S(1)} %collective-permute-done.1.refs_0_, f32[3,256]{1,0:T(4,128)S(1)} %get-tuple-element.20.refs_1_, f32[3,256,128]{2,1,0:T(8,128)S(1)} %get-tuple-element.21.refs_2_, f32[3,256,128]{2,1,0:T(8,128)S(1)} %get-tuple-element.22.refs_3_, ...), custom_call_target="tpu_custom_call" | custom-call | tf_op jit(solution)/shard_map/pallas_call | solution.py:253
  51.1 9.1 %all_to_all.22.source_ref = f32[16,1,1536]{2,1,0:T(1,128)S(1)} all-to-all(f32[16,1,1536]{2,1,0:T(1,128)S(1)} %get-tuple-element.24.own_ref), channel_id=1, replica_groups={{0,2,4,6,8,10,12,14,16,18,20,22,24,26,28,30},{1,3,5,7,9,11,13,15,17,19,..., dimensions={0} | all-to-all | bytes 196608 | tf_op jit(solution)/shard_map/all_to_all | solution.py:234
  60.1 1.5 %collective-permute-start.2 = (f32[16,1,1536]{2,1,0:T(1,128)S(1)}, f32[16,1,1536]{2,1,0:T(1,128)S(1)}, u32[]{:S(2)}, u32[]{:S(2)}) collective-permute-start(f32[16,1,1536]{2,1,0:T(1,128)S(1)} %all_to_all.22.source_ref), channel_id=1, source_target_pairs={{0,1},{1,0},{2,3},{3,2},{4,5},{5,4},{6,7},{7,6},{8,9},{9,8},{10,11... | collective-permute-start | bytes 294920 | tf_op jit(solution)/shard_map/ppermute | solution.py:235
  61.7 4.9 %shard_map.91 = (f32[3,256,128]{2,1,0:T(8,128)S(1)}, f32[3,256,128]{2,1,0:T(8,128)S(1)}) custom-call(f32[16,1,1536]{2,1,0:T(1,128)S(1)} %all_to_all.22.source_ref, f32[16,1,1536]{2,1,0:T(1,128)S(1)} %get-tuple-element.24.own_ref), custom_call_target="tpu_custom_call" | custom-call | flops 32505856 | bytes 786432 | tf_op jit(solution)/shard_map/pallas_call | solution.py:242
  66.5 0.0 collective-permute-done.2.refs_0_
  66.6 5.4 %shard_map.92 = (f32[16,1,1536]{2,1,0:T(1,128)S(1)}, f32[3,256]{1,0:T(4,128)}) custom-call(f32[16,1,1536]{2,1,0:T(1,128)S(1)} %collective-permute-done.2.refs_0_, f32[3,256]{1,0:T(4,128)S(1)} %get-tuple-element.25.refs_1_, f32[3,256,128]{2,1,0:T(8,128)S(1)} %get-tuple-element.26.refs_2_, f32[3,256,128]{2,1,0:T(8,128)S(1)} %get-tuple-element.27.refs_3_, ...), custom_call_target="tpu_custom_call" | custom-call | tf_op jit(solution)/shard_map/pallas_call | solution.py:253
  72.0 9.1 %all_to_all.23.source_ref = f32[16,1,1536]{2,1,0:T(1,128)S(1)} all-to-all(f32[16,1,1536]{2,1,0:T(1,128)S(1)} %get-tuple-element.29.own_ref), channel_id=1, replica_groups={{0,2,4,6,8,10,12,14,16,18,20,22,24,26,28,30},{1,3,5,7,9,11,13,15,17,19,..., dimensions={0} | all-to-all | bytes 196608 | tf_op jit(solution)/shard_map/all_to_all | solution.py:234
  81.1 1.3 %collective-permute-start.3 = (f32[16,1,1536]{2,1,0:T(1,128)S(1)}, f32[16,1,1536]{2,1,0:T(1,128)S(1)}, u32[]{:S(2)}, u32[]{:S(2)}) collective-permute-start(f32[16,1,1536]{2,1,0:T(1,128)S(1)} %all_to_all.23.source_ref), channel_id=1, source_target_pairs={{0,1},{1,0},{2,3},{3,2},{4,5},{5,4},{6,7},{7,6},{8,9},{9,8},{10,11... | collective-permute-start | bytes 294920 | tf_op jit(solution)/shard_map/ppermute | solution.py:235
  82.3 4.9 %shard_map.93 = (f32[3,256,128]{2,1,0:T(8,128)S(1)}, f32[3,256,128]{2,1,0:T(8,128)S(1)}) custom-call(f32[16,1,1536]{2,1,0:T(1,128)S(1)} %all_to_all.23.source_ref, f32[16,1,1536]{2,1,0:T(1,128)S(1)} %get-tuple-element.29.own_ref), custom_call_target="tpu_custom_call" | custom-call | flops 32505856 | bytes 786432 | tf_op jit(solution)/shard_map/pallas_call | solution.py:242
  87.2 0.0 collective-permute-done.3.far_ref
  87.2 5.4 %shard_map.94 = f32[3,256]{1,0:T(4,128)} custom-call(f32[16,1,1536]{2,1,0:T(1,128)S(1)} %collective-permute-done.3.far_ref, f32[3,256,128]{2,1,0:T(8,128)S(1)} %get-tuple-element.30.column_ref, f32[3,256,128]{2,1,0:T(8,128)S(1)} %get-tuple-element.31.start_ref), custom_call_target="tpu_custom_call" | custom-call | tf_op jit(solution)/shard_map/pallas_call | solution.py:253
Async XLA Ops:
  2.6 17.0 %copy-start = (f32[16,1,2560]{2,1,0:T(1,128)S(1)}, f32[16,1,2560]{2,1,0:T(1,128)}, u32[]{:S(2)}) copy-start(f32[16,1,2560]{2,1,0:T(1,128)} %shard_map.86.own_ref) | copy-start | bytes 491524
  16.7 7.7 %collective-permute-start = (f32[16,1,2560]{2,1,0:T(1,128)S(1)}, f32[16,1,2560]{2,1,0:T(1,128)S(1)}, u32[]{:S(2)}, u32[]{:S(2)}) collective-permute-start(f32[16,1,2560]{2,1,0:T(1,128)S(1)} %all_to_all.20.source_ref.refs_5_), channel_id=1, source_target_pairs={{0,1},{1,0},{2,3},{3,2},{4,5},{5,4},{6,7},{7,6},{8,9},{9,8},{10,11... | collective-permute-start | bytes 491528 | tf_op jit(solution)/shard_map/ppermute | solution.py:235
  19.6 4.9 %copy-start.1 = (s32[12,256]{1,0:T(8,128)S(1)}, s32[12,256]{1,0:T(8,128)}, u32[]{:S(2)}) copy-start(s32[12,256]{1,0:T(8,128)} %refs_4_.7) | copy-start | bytes 36868
  24.5 0.7 copy-start.2
  24.5 0.7 copy-start.3
  39.9 6.2 %collective-permute-start.1 = (f32[16,1,1536]{2,1,0:T(1,128)S(1)}, f32[16,1,1536]{2,1,0:T(1,128)S(1)}, u32[]{:S(2)}, u32[]{:S(2)}) collective-permute-start(f32[16,1,1536]{2,1,0:T(1,128)S(1)} %all_to_all.21.source_ref), channel_id=1, source_target_pairs={{0,1},{1,0},{2,3},{3,2},{4,5},{5,4},{6,7},{7,6},{8,9},{9,8},{10,11... | collective-permute-start | bytes 294920 | tf_op jit(solution)/shard_map/ppermute | solution.py:235
  60.1 6.4 %collective-permute-start.2 = (f32[16,1,1536]{2,1,0:T(1,128)S(1)}, f32[16,1,1536]{2,1,0:T(1,128)S(1)}, u32[]{:S(2)}, u32[]{:S(2)}) collective-permute-start(f32[16,1,1536]{2,1,0:T(1,128)S(1)} %all_to_all.22.source_ref), channel_id=1, source_target_pairs={{0,1},{1,0},{2,3},{3,2},{4,5},{5,4},{6,7},{7,6},{8,9},{9,8},{10,11... | collective-permute-start | bytes 294920 | tf_op jit(solution)/shard_map/ppermute | solution.py:235
  81.1 6.1 %collective-permute-start.3 = (f32[16,1,1536]{2,1,0:T(1,128)S(1)}, f32[16,1,1536]{2,1,0:T(1,128)S(1)}, u32[]{:S(2)}, u32[]{:S(2)}) collective-permute-start(f32[16,1,1536]{2,1,0:T(1,128)S(1)} %all_to_all.23.source_ref), channel_id=1, source_target_pairs={{0,1},{1,0},{2,3},{3,2},{4,5},{5,4},{6,7},{7,6},{8,9},{9,8},{10,11... | collective-permute-start | bytes 294920 | tf_op jit(solution)/shard_map/ppermute | solution.py:235

commit v9 on v8

--- a/solution.py
+++ b/solution.py
@@ -12,7 +12,8 @@
 LANES = 128
 ROWS = 8
 TARGET_ROWS = 32
-UNROLL = 8
+UNROLL = 16
+PICK_UNROLL = 4
 PARAMS = 12
 FOLD = 4
 
@@ -85,9 +86,12 @@
     places = [rank[:, at : at + LANES] + part * capacity for at in spots]
     owners = [jnp.broadcast_to(owner[:, at : at + LANES], (ROWS, LANES)) for at in spots]
 
-    def choose(chip, chosen):
+    def choose(step, chosen):
         chosen = list(chosen)
-        for ref, device in ((near_ref, 2 * chip + parity), (far_ref, 2 * chip + 1 - parity)):
+        chips_now = [step * PICK_UNROLL + i for i in range(PICK_UNROLL)]
+        pairs = [(near_ref, chip, 2 * chip + parity) for chip in chips_now]
+        pairs += [(far_ref, chip, 2 * chip + 1 - parity) for chip in chips_now]
+        for ref, chip, device in pairs:
             for t in range(FOLD):
                 lane = pl.multiple_of(6 * nodes + (parity * FOLD + t) * LANES, LANES)
                 block = jnp.broadcast_to(ref[chip, :, pl.ds(lane, LANES)], (ROWS, LANES))
@@ -98,7 +102,7 @@
         return tuple(chosen)
 
     zero = jnp.zeros((ROWS, LANES), jnp.float32)
-    chosen = lax.fori_loop(0, chips, choose, (zero,) * (FOLD * len(spots)), unroll=4)
+    chosen = lax.fori_loop(0, chips // PICK_UNROLL, choose, (zero,) * (FOLD * len(spots)))
     for i, at in enumerate(spots):
         for t in range(FOLD):
             for j in range(parts):
@@ -111,6 +115,18 @@
         for at in range(0, nodes, LANES):
             row = own_ref[0, :, c * nodes + at : c * nodes + at + LANES]
             column_ref[c, at : at + LANES, :] = jnp.broadcast_to(row, (LANES, LANES)).T
+
+
+def add_block(source_ref, nodes, device, at, target, totals):
+    rows = [source_ref[device, :, c * nodes + at : c * nodes + at + LANES] for c in range(6)]
+    x, f = rows[:3], rows[3:]
+    d = [target[c] - x[c] for c in range(3)]
+    shifted = d[0] * d[0] + (d[1] * d[1] + (d[2] * d[2] + 1.0))
+    r = lax.rsqrt(shifted)
+    cube = r * (r * r)
+    direct = r + cube
+    along = (d[0] * f[0] + d[1] * f[1] + d[2] * f[2]) * cube
+    return tuple(totals[c] + (direct * f[c] + along * d[c]) for c in range(3))
 
 
 def pair_sums(source_refs, column_ref, start_ref, sum_ref):
@@ -124,21 +140,15 @@
         else:
             totals = tuple(start_ref[c, rows, :] for c in range(3))
         for source_ref in source_refs:
-
-            def per_source(device, totals):
-                for at in range(0, nodes, LANES):
-                    rows = [source_ref[device, :, c * nodes + at : c * nodes + at + LANES] for c in range(6)]
-                    x, f = rows[:3], rows[3:]
-                    d = [target[c] - x[c] for c in range(3)]
-                    shifted = d[0] * d[0] + (d[1] * d[1] + (d[2] * d[2] + 1.0))
-                    r = lax.rsqrt(shifted)
-                    cube = r * (r * r)
-                    direct = r + cube
-                    along = (d[0] * f[0] + d[1] * f[1] + d[2] * f[2]) * cube
-                    totals = tuple(totals[c] + (direct * f[c] + along * d[c]) for c in range(3))
+            together = math.gcd(source_ref.shape[0], UNROLL)
+
+            def per_pass(step, totals):
+                for i in range(together):
+                    for at in range(0, nodes, LANES):
+                        totals = add_block(source_ref, nodes, step * together + i, at, target, totals)
                 return totals
 
-            totals = lax.fori_loop(0, source_ref.shape[0], per_source, totals, unroll=2)
+            totals = lax.fori_loop(0, source_ref.shape[0] // together, per_pass, totals)
         for c in range(3):
             sum_ref[c, rows, :] = totals[c]
         return 0

time: 93.1 us -> 92.4 us (level)
  no operation moved by 1% of the time
where the time goes in v9:
time: 92.4 us; the launch traced here: 92 us
  Pallas kernels  42.3 us (46%)
  blocking collectives  41.3 us (45%)
  starting transfers between devices  6.97 us (8%)
    all_to_all x4, blocking collectives, spread(): lax.all_to_all(copies, AXES, split_axis=0, concat_axis=0, axis_index_grou...  41.3 us
    pallas_call x4, Pallas kernels, call(): pl.pallas_call(kernel, out_shape=out_shape, in_specs=[VMEM] * len(operand...  21.3 us
    pallas_call x4, Pallas kernels, near_sums(): pl.pallas_call(near_kernel, out_shape=(shape, shape), in_specs=[VMEM] * 2...  18.9 us
    ppermute x4, starting transfers between devices, spread(): far = lax.ppermute(near, AXES, [(i, i ^ 1) for i in range(devices)])  6.97 us
    pallas_call x1, Pallas kernels, pack(): pl.pallas_call(pack_kernel, out_shape=jax.ShapeDtypeStruct((devices // 2,...  1.98 us
  transfers between devices with their start and end apart: 4, of which 0 were waited for; matrix products, arithmetic and copies ran while one was open for 0% of the time, Pallas kernels for 21%

profile of v9, /device:TPU:1, one launch (start us, length us, event | category | flops | bytes accessed | tf_op | source)
XLA Modules:
  0.0 92.0 jit_solution(7733381390113228500)
XLA Ops:
  0.6 2.0 %shard_map.86.own_ref = f32[16,1,2560]{2,1,0:T(1,128)} custom-call(f32[3,256]{1,0:T(4,128)} %refs_1_.3, f32[3,256]{1,0:T(4,128)} %refs_1_.2, f32[6,1280]{1,0:T(8,128)} %refs_2_.1, f32[2,1280]{1,0:T(2,128)} %refs_3_.1, f32[3,1280]{1,0:T(4,128)} %refs_4_.4), custom_call_target="tpu_custom_call" | custom-call | tf_op jit(solution)/shard_map/pallas_call | solution.py:62
  2.6 0.0 copy-start
  2.6 14.1 %all_to_all.20.source_ref.refs_5_ = f32[16,1,2560]{2,1,0:T(1,128)S(1)} all-to-all(f32[16,1,2560]{2,1,0:T(1,128)} %shard_map.86.own_ref), channel_id=1, replica_groups={{0,2,4,6,8,10,12,14,16,18,20,22,24,26,28,30},{1,3,5,7,9,11,13,15,17,19,..., dimensions={0} | all-to-all | bytes 327680 | tf_op jit(solution)/shard_map/all_to_all | solution.py:244
  16.7 2.9 %collective-permute-start = (f32[16,1,2560]{2,1,0:T(1,128)S(1)}, f32[16,1,2560]{2,1,0:T(1,128)S(1)}, u32[]{:S(2)}, u32[]{:S(2)}) collective-permute-start(f32[16,1,2560]{2,1,0:T(1,128)S(1)} %all_to_all.20.source_ref.refs_5_), channel_id=1, source_target_pairs={{0,1},{1,0},{2,3},{3,2},{4,5},{5,4},{6,7},{7,6},{8,9},{9,8},{10,11... | collective-permute-start | bytes 491528 | tf_op jit(solution)/shard_map/ppermute | solution.py:245
  19.6 0.0 copy-done
  19.6 0.0 copy-start.1
  19.6 4.8 %shard_map.87 = (f32[3,256,128]{2,1,0:T(8,128)S(1)}, f32[3,256,128]{2,1,0:T(8,128)S(1)}) custom-call(f32[16,1,2560]{2,1,0:T(1,128)S(1)} %all_to_all.20.source_ref.refs_5_, f32[16,1,2560]{2,1,0:T(1,128)S(1)} %copy-done), custom_call_target="tpu_custom_call" | custom-call | flops 32505856 | bytes 786432 | tf_op jit(solution)/shard_map/pallas_call | solution.py:252
  24.5 0.0 copy-start.2
  24.5 0.0 collective-permute-done.refs_0_
  24.5 0.0 copy-start.3
  24.5 0.0 copy-done.1
  24.5 0.6 copy-done.2
  25.1 0.0 copy-done.3
  25.2 5.5 %shard_map.88 = (f32[16,1,1536]{2,1,0:T(1,128)S(1)}, f32[3,256]{1,0:T(4,128)S(1)}, f32[12,256]{1,0:T(8,128)S(1)}) custom-call(f32[16,1,2560]{2,1,0:T(1,128)S(1)} %collective-permute-done.refs_0_, f32[3,256]{1,0:T(4,128)S(1)} %copy-done.2, f32[3,256,128]{2,1,0:T(8,128)S(1)} %get-tuple-element.17.refs_2_, f32[3,256,128]{2,1,0:T(8,128)S(1)} %get-tuple-element.18.refs_3_, ...), custom_call_target="tpu_custom_call" | custom-call | tf_op jit(solution)/shard_map/pallas_call | solution.py:263
  30.7 9.1 %all_to_all.21.source_ref = f32[16,1,1536]{2,1,0:T(1,128)S(1)} all-to-all(f32[16,1,1536]{2,1,0:T(1,128)S(1)} %get-tuple-element.19.own_ref), channel_id=1, replica_groups={{0,2,4,6,8,10,12,14,16,18,20,22,24,26,28,30},{1,3,5,7,9,11,13,15,17,19,..., dimensions={0} | all-to-all | bytes 196608 | tf_op jit(solution)/shard_map/all_to_all | solution.py:244
  39.8 1.3 %collective-permute-start.1 = (f32[16,1,1536]{2,1,0:T(1,128)S(1)}, f32[16,1,1536]{2,1,0:T(1,128)S(1)}, u32[]{:S(2)}, u32[]{:S(2)}) collective-permute-start(f32[16,1,1536]{2,1,0:T(1,128)S(1)} %all_to_all.21.source_ref), channel_id=1, source_target_pairs={{0,1},{1,0},{2,3},{3,2},{4,5},{5,4},{6,7},{7,6},{8,9},{9,8},{10,11... | collective-permute-start | bytes 294920 | tf_op jit(solution)/shard_map/ppermute | solution.py:245
  41.1 4.7 %shard_map.89 = (f32[3,256,128]{2,1,0:T(8,128)S(1)}, f32[3,256,128]{2,1,0:T(8,128)S(1)}) custom-call(f32[16,1,1536]{2,1,0:T(1,128)S(1)} %all_to_all.21.source_ref, f32[16,1,1536]{2,1,0:T(1,128)S(1)} %get-tuple-element.19.own_ref), custom_call_target="tpu_custom_call" | custom-call | flops 32505856 | bytes 786432 | tf_op jit(solution)/shard_map/pallas_call | solution.py:252
  45.8 0.0 collective-permute-done.1.refs_0_
  45.8 5.0 %shard_map.90 = (f32[16,1,1536]{2,1,0:T(1,128)S(1)}, f32[3,256]{1,0:T(4,128)S(1)}) custom-call(f32[16,1,1536]{2,1,0:T(1,128)S(1)} %collective-permute-done.1.refs_0_, f32[3,256]{1,0:T(4,128)S(1)} %get-tuple-element.20.refs_1_, f32[3,256,128]{2,1,0:T(8,128)S(1)} %get-tuple-element.21.refs_2_, f32[3,256,128]{2,1,0:T(8,128)S(1)} %get-tuple-element.22.refs_3_, ...), custom_call_target="tpu_custom_call" | custom-call | tf_op jit(solution)/shard_map/pallas_call | solution.py:263
  50.8 9.1 %all_to_all.22.source_ref = f32[16,1,1536]{2,1,0:T(1,128)S(1)} all-to-all(f32[16,1,1536]{2,1,0:T(1,128)S(1)} %get-tuple-element.24.own_ref), channel_id=1, replica_groups={{0,2,4,6,8,10,12,14,16,18,20,22,24,26,28,30},{1,3,5,7,9,11,13,15,17,19,..., dimensions={0} | all-to-all | bytes 196608 | tf_op jit(solution)/shard_map/all_to_all | solution.py:244
  59.9 1.5 %collective-permute-start.2 = (f32[16,1,1536]{2,1,0:T(1,128)S(1)}, f32[16,1,1536]{2,1,0:T(1,128)S(1)}, u32[]{:S(2)}, u32[]{:S(2)}) collective-permute-start(f32[16,1,1536]{2,1,0:T(1,128)S(1)} %all_to_all.22.source_ref), channel_id=1, source_target_pairs={{0,1},{1,0},{2,3},{3,2},{4,5},{5,4},{6,7},{7,6},{8,9},{9,8},{10,11... | collective-permute-start | bytes 294920 | tf_op jit(solution)/shard_map/ppermute | solution.py:245
  61.4 4.7 %shard_map.91 = (f32[3,256,128]{2,1,0:T(8,128)S(1)}, f32[3,256,128]{2,1,0:T(8,128)S(1)}) custom-call(f32[16,1,1536]{2,1,0:T(1,128)S(1)} %all_to_all.22.source_ref, f32[16,1,1536]{2,1,0:T(1,128)S(1)} %get-tuple-element.24.own_ref), custom_call_target="tpu_custom_call" | custom-call | flops 32505856 | bytes 786432 | tf_op jit(solution)/shard_map/pallas_call | solution.py:252
  66.1 0.0 collective-permute-done.2.refs_0_
  66.1 5.5 %shard_map.92 = (f32[16,1,1536]{2,1,0:T(1,128)S(1)}, f32[3,256]{1,0:T(4,128)}) custom-call(f32[16,1,1536]{2,1,0:T(1,128)S(1)} %collective-permute-done.2.refs_0_, f32[3,256]{1,0:T(4,128)S(1)} %get-tuple-element.25.refs_1_, f32[3,256,128]{2,1,0:T(8,128)S(1)} %get-tuple-element.26.refs_2_, f32[3,256,128]{2,1,0:T(8,128)S(1)} %get-tuple-element.27.refs_3_, ...), custom_call_target="tpu_custom_call" | custom-call | tf_op jit(solution)/shard_map/pallas_call | solution.py:263
  71.6 9.1 %all_to_all.23.source_ref = f32[16,1,1536]{2,1,0:T(1,128)S(1)} all-to-all(f32[16,1,1536]{2,1,0:T(1,128)S(1)} %get-tuple-element.29.own_ref), channel_id=1, replica_groups={{0,2,4,6,8,10,12,14,16,18,20,22,24,26,28,30},{1,3,5,7,9,11,13,15,17,19,..., dimensions={0} | all-to-all | bytes 196608 | tf_op jit(solution)/shard_map/all_to_all | solution.py:244
  80.7 1.3 %collective-permute-start.3 = (f32[16,1,1536]{2,1,0:T(1,128)S(1)}, f32[16,1,1536]{2,1,0:T(1,128)S(1)}, u32[]{:S(2)}, u32[]{:S(2)}) collective-permute-start(f32[16,1,1536]{2,1,0:T(1,128)S(1)} %all_to_all.23.source_ref), channel_id=1, source_target_pairs={{0,1},{1,0},{2,3},{3,2},{4,5},{5,4},{6,7},{7,6},{8,9},{9,8},{10,11... | collective-permute-start | bytes 294920 | tf_op jit(solution)/shard_map/ppermute | solution.py:245
  82.0 4.7 %shard_map.93 = (f32[3,256,128]{2,1,0:T(8,128)S(1)}, f32[3,256,128]{2,1,0:T(8,128)S(1)}) custom-call(f32[16,1,1536]{2,1,0:T(1,128)S(1)} %all_to_all.23.source_ref, f32[16,1,1536]{2,1,0:T(1,128)S(1)} %get-tuple-element.29.own_ref), custom_call_target="tpu_custom_call" | custom-call | flops 32505856 | bytes 786432 | tf_op jit(solution)/shard_map/pallas_call | solution.py:252
  86.7 0.0 collective-permute-done.3.far_ref
  86.7 5.3 %shard_map.94 = f32[3,256]{1,0:T(4,128)} custom-call(f32[16,1,1536]{2,1,0:T(1,128)S(1)} %collective-permute-done.3.far_ref, f32[3,256,128]{2,1,0:T(8,128)S(1)} %get-tuple-element.30.column_ref, f32[3,256,128]{2,1,0:T(8,128)S(1)} %get-tuple-element.31.start_ref), custom_call_target="tpu_custom_call" | custom-call | tf_op jit(solution)/shard_map/pallas_call | solution.py:263
Async XLA Ops:
  2.6 17.0 %copy-start = (f32[16,1,2560]{2,1,0:T(1,128)S(1)}, f32[16,1,2560]{2,1,0:T(1,128)}, u32[]{:S(2)}) copy-start(f32[16,1,2560]{2,1,0:T(1,128)} %shard_map.86.own_ref) | copy-start | bytes 491524
  16.7 7.7 %collective-permute-start = (f32[16,1,2560]{2,1,0:T(1,128)S(1)}, f32[16,1,2560]{2,1,0:T(1,128)S(1)}, u32[]{:S(2)}, u32[]{:S(2)}) collective-permute-start(f32[16,1,2560]{2,1,0:T(1,128)S(1)} %all_to_all.20.source_ref.refs_5_), channel_id=1, source_target_pairs={{0,1},{1,0},{2,3},{3,2},{4,5},{5,4},{6,7},{7,6},{8,9},{9,8},{10,11... | collective-permute-start | bytes 491528 | tf_op jit(solution)/shard_map/ppermute | solution.py:245
  19.6 4.9 %copy-start.1 = (s32[12,256]{1,0:T(8,128)S(1)}, s32[12,256]{1,0:T(8,128)}, u32[]{:S(2)}) copy-start(s32[12,256]{1,0:T(8,128)} %refs_4_.7) | copy-start | bytes 36868
  24.5 0.7 copy-start.2
  24.5 0.7 copy-start.3
  39.8 6.0 %collective-permute-start.1 = (f32[16,1,1536]{2,1,0:T(1,128)S(1)}, f32[16,1,1536]{2,1,0:T(1,128)S(1)}, u32[]{:S(2)}, u32[]{:S(2)}) collective-permute-start(f32[16,1,1536]{2,1,0:T(1,128)S(1)} %all_to_all.21.source_ref), channel_id=1, source_target_pairs={{0,1},{1,0},{2,3},{3,2},{4,5},{5,4},{6,7},{7,6},{8,9},{9,8},{10,11... | collective-permute-start | bytes 294920 | tf_op jit(solution)/shard_map/ppermute | solution.py:245
  59.9 6.2 %collective-permute-start.2 = (f32[16,1,1536]{2,1,0:T(1,128)S(1)}, f32[16,1,1536]{2,1,0:T(1,128)S(1)}, u32[]{:S(2)}, u32[]{:S(2)}) collective-permute-start(f32[16,1,1536]{2,1,0:T(1,128)S(1)} %all_to_all.22.source_ref), channel_id=1, source_target_pairs={{0,1},{1,0},{2,3},{3,2},{4,5},{5,4},{6,7},{7,6},{8,9},{9,8},{10,11... | collective-permute-start | bytes 294920 | tf_op jit(solution)/shard_map/ppermute | solution.py:245
  80.7 6.0 %collective-permute-start.3 = (f32[16,1,1536]{2,1,0:T(1,128)S(1)}, f32[16,1,1536]{2,1,0:T(1,128)S(1)}, u32[]{:S(2)}, u32[]{:S(2)}) collective-permute-start(f32[16,1,1536]{2,1,0:T(1,128)S(1)} %all_to_all.23.source_ref), channel_id=1, source_target_pairs={{0,1},{1,0},{2,3},{3,2},{4,5},{5,4},{6,7},{7,6},{8,9},{9,8},{10,11... | collective-permute-start | bytes 294920 | tf_op jit(solution)/shard_map/ppermute | solution.py:245

commit v10 on v9

v10 whole, which is shorter than its diff:
```python
import functools
import math

import jax
import jax.numpy as jnp
import numpy as np
from jax import lax
from jax.experimental import pallas as pl
from jax.experimental.pallas import tpu as pltpu
from jax.sharding import Mesh
from jax.sharding import PartitionSpec as P

STEPS = 3
LANES = 128
ROWS = 8
PIECES = 32
DEPTH = 128
FAR_OFF = 2048.0
CUT_UNROLL = 4
CHUNK = 16
LOADS = 7
SIDE = 32
PICK_UNROLL = 4
PARAMS = 12
FOLD = 4

inverse_blob = 20.0
time_step = 0.5

CHIPS = ("tgt", "z")
AXES = CHIPS + ("core",)
VMEM = pl.BlockSpec(memory_space=pltpu.VMEM)
GRANT = pltpu.CompilerParams(vmem_limit_bytes=32 * 1024 * 1024)


def pack_kernel(*refs):
    inputs, (out_ref, side_ref), copies = refs[:LOADS], refs[LOADS : LOADS + 2], refs[LOADS + 2 : -3]
    slots_ref, target_ref, semaphores = refs[-3:]
    loads = [pltpu.make_async_copy(inputs[i], copies[i], semaphores.at[i]) for i in range(LOADS)]
    for load in loads:
        load.start()
    for load in loads:
        load.wait()
    position_ref, force_ref, length_ref, moduli_ref, bend_ref, owner_ref, select_ref = copies
    chips = out_ref.shape[0]
    nodes = position_ref.shape[1]
    capacity = length_ref.shape[1] // (2 * chips)
    state = [inverse_blob * position_ref[c : c + 1, :] for c in range(3)]
    make_left(state, select_ref, side_ref, target_ref)
    rank_nodes(owner_ref, side_ref)
    state += [force_ref[c : c + 1, :] for c in range(3)]
    slots_ref[0:6, :] = length_ref[...]
    slots_ref[6:8, :] = moduli_ref[...]
    slots_ref[8:11, :] = bend_ref[...]
    slots_ref[11:12, :] = bend_ref[0:1, :]
    for chip in range(chips):
        for c in range(6):
            out_ref[chip, :, c * nodes : (c + 1) * nodes] = state[c]
        for core in range(2):
            cut = slice((2 * chip + core) * capacity, (2 * chip + core + 1) * capacity)
            for part in range(PARAMS // FOLD):
                rows = slots_ref[part * FOLD : (part + 1) * FOLD, cut]
                for t in range(FOLD):
                    lane = 6 * nodes + (core * FOLD + t) * LANES + part * capacity
                    out_ref[chip, :, lane : lane + capacity] = rows[t : t + 1, :]


def side_shape(nodes):
    return jax.ShapeDtypeStruct((2 * nodes + SIDE, DEPTH), jnp.float32)


def pack(positions, forces, rest_length, moduli, rest_bend, owner, select, devices):
    operands = (positions, forces, rest_length, moduli, rest_bend, owner, select)
    nodes = positions.shape[1]
    return pl.pallas_call(
        pack_kernel,
        out_shape=(
            jax.ShapeDtypeStruct((devices // 2, 1, 6 * nodes + 2 * FOLD * LANES), jnp.float32),
            side_shape(nodes),
        ),
        in_specs=[pl.BlockSpec(memory_space=pl.ANY)] * LOADS,
        out_specs=(VMEM,) * 2,
        scratch_shapes=[pltpu.VMEM(x.shape, x.dtype) for x in operands]
        + [
            pltpu.VMEM((PARAMS, rest_length.shape[1]), jnp.float32),
            pltpu.VMEM((PIECES, nodes), jnp.float32),
            pltpu.SemaphoreType.DMA((LOADS,)),
        ],
        compiler_params=pltpu.CompilerParams(vmem_limit_bytes=60 * 1024 * 1024),
    )(*operands)


def rank_nodes(owner_ref, side_ref):
    nodes = owner_ref.shape[1]
    owner = owner_ref[...]
    across = jnp.broadcast_to(owner, (nodes, nodes))
    earlier = lax.broadcasted_iota(jnp.int32, (nodes, nodes), 0) < lax.broadcasted_iota(
        jnp.int32, (nodes, nodes), 1
    )
    rank = jnp.sum(jnp.where((across == across.T) & earlier, 1, 0), axis=0, keepdims=True)
    first = side_ref.shape[0] - ROWS
    for v in (rank, owner):
        for at in range(0, nodes, LANES):
            side_ref[first : first + 1, :] = v[:, at : at + LANES].astype(jnp.float32)
            first += 1


def pick_slots(capacity, near_ref, far_ref, side_ref, params_ref):
    chips = near_ref.shape[0]
    nodes = params_ref.shape[1]
    parts = PARAMS // FOLD
    named = side_ref[side_ref.shape[0] - ROWS :, :].astype(jnp.int32)
    parity = lax.axis_index("core")
    spots = range(0, nodes, LANES)
    part = jnp.minimum(lax.broadcasted_iota(jnp.int32, (ROWS, LANES), 0), parts - 1)
    places = [named[i : i + 1, :] + part * capacity for i in range(len(spots))]
    owners = [jnp.broadcast_to(named[len(spots) + i : len(spots) + i + 1, :], (ROWS, LANES)) for i in range(len(spots))]

    def choose(step, chosen):
        chosen = list(chosen)
        chips_now = [step * PICK_UNROLL + i for i in range(PICK_UNROLL)]
        pairs = [(near_ref, chip, 2 * chip + parity) for chip in chips_now]
        pairs += [(far_ref, chip, 2 * chip + 1 - parity) for chip in chips_now]
        for ref, chip, device in pairs:
            for t in range(FOLD):
                lane = pl.multiple_of(6 * nodes + (parity * FOLD + t) * LANES, LANES)
                block = jnp.broadcast_to(ref[chip, :, pl.ds(lane, LANES)], (ROWS, LANES))
                for i in range(len(spots)):
                    taken = jnp.take_along_axis(block, places[i], axis=1, mode="promise_in_bounds")
                    at = i * FOLD + t
                    chosen[at] = jnp.where(owners[i] == device, taken, chosen[at])
        return tuple(chosen)

    zero = jnp.zeros((ROWS, LANES), jnp.float32)
    chosen = lax.fori_loop(0, chips // PICK_UNROLL, choose, (zero,) * (FOLD * len(spots)))
    for i, at in enumerate(spots):
        for t in range(FOLD):
            for j in range(parts):
                params_ref[j * FOLD + t : j * FOLD + t + 1, at : at + LANES] = chosen[i * FOLD + t][j : j + 1, :]


def high(v):
    return v.astype(jnp.bfloat16).astype(jnp.float32)


def three(v):
    first = high(v)
    second = high(v - first)
    return first, second, (v - first) - second


def on_grid(v, grid, per_grid):
    return jnp.floor(v * per_grid + 0.5) * grid


def norm_and_cross(x, coarse):
    rest = [v - w for v, w in zip(x, coarse)]
    norm = coarse[0] * coarse[0] + coarse[1] * coarse[1] + coarse[2] * coarse[2]
    cross = [(2.0 * w + r) * r for w, r in zip(coarse, rest)]
    return norm, cross[0] + cross[1] + cross[2]


def selectors():
    c1, c2, r1, r2, n, g, one = 0, 3, 6, 9, 12, 15, 18
    A,B,C,D,E,F,G,H = range(0,128,16)
    s = np.zeros((PIECES, DEPTH), np.float32); t = np.zeros((PIECES, DEPTH), np.float32)
    for at, first in ((A,c1),(B,c2),(C,c1),(D,c2),(E,r1),(F,r2),(G,r1),(H,r2)):
        for c in range(3):
            s[first+c, at+c] = -2.0
            s[first+c, at+8+c] = -2.0
    s[one, A+6] = s[one, A+14] = s[one, A+15] = 1.0
    s[n, A+7] = s[n+1, B+7] = s[n+2, E+7] = 1.0
    s[one, C+6] = s[one, C+14] = s[one, C+15] = 1.0
    s[g, C+7] = s[g+1, D+7] = s[g+2, G+7] = 1.0
    for at, first, second in ((A,c1,c1),(B,c2,c2),(C,c1,None),(D,c2,None),(E,r1,r1),(F,r2,None)):
        for c in range(3):
            t[first+c, at+3+c] = 1.0
            if second is not None: t[second+c, at+11+c] = 1.0
    for c in range(3): t[one, C+11+c] = 1.0
    return np.concatenate([s, t], axis=1)


def own_rows(own_ref, nodes):
    return [own_ref[0, :, c * nodes : (c + 1) * nodes] for c in range(3)]


def pick_grid(size):
    grid = jnp.full(size.shape, 2.0**-3, jnp.float32)
    per_grid = jnp.full(size.shape, 2.0**3, jnp.float32)
    for step in range(1, 25):
        beyond = size > 2.0 ** (6 + step)
        grid = jnp.where(beyond, 2.0 ** (step - 3), grid)
        per_grid = jnp.where(beyond, 2.0 ** (3 - step), per_grid)
    return grid, per_grid


def set_grid(size, info_ref):
    grid, per_grid = pick_grid(size)
    info_ref[0:ROWS, :] = jnp.broadcast_to(grid, (ROWS, LANES))
    info_ref[ROWS : 2 * ROWS, :] = jnp.broadcast_to(per_grid, (ROWS, LANES))


def build_left(x, select_ref, info_ref, target_ref, left_ref):
    grid, per_grid = info_ref[0:1, 0:1], info_ref[ROWS : ROWS + 1, 0:1]
    shift = [info_ref[2 * ROWS + c : 2 * ROWS + c + 1, 0:1] for c in range(3)]
    x = [v - o for v, o in zip(x, shift)]
    coarse = [on_grid(v, grid, per_grid) for v in x]
    norm, cross = norm_and_cross(x, coarse)
    c1 = [high(v) for v in coarse]
    r1 = [high(v - w) for v, w in zip(x, coarse)]
    pieces = c1 + [v - w for v, w in zip(coarse, c1)]
    pieces += r1 + [(v - w) - r for v, w, r in zip(x, coarse, r1)]
    pieces += list(three(norm)) + list(three(cross + 1.0)) + [jnp.ones_like(norm)]
    target_ref[...] = jnp.zeros(target_ref.shape, jnp.float32)
    for r, piece in enumerate(pieces):
        target_ref[r : r + 1, :] = piece
    left = lax.dot_general(
        target_ref[...].astype(jnp.bfloat16),
        select_ref[...].astype(jnp.bfloat16),
        (((0,), (0,)), ((), ())),
        preferred_element_type=jnp.float32,
    ).astype(jnp.bfloat16)
    nodes = left.shape[0]
    left_ref[0:nodes, :] = left[:, 0:DEPTH].astype(left_ref.dtype)
    left_ref[nodes : 2 * nodes, :] = left[:, DEPTH : 2 * DEPTH].astype(left_ref.dtype)


def info_of(side_ref):
    rows = side_ref.shape[0] - SIDE
    return side_ref.at[rows : rows + 3 * ROWS, :]


def make_left(x, select_ref, side_ref, target_ref):
    info_ref = info_of(side_ref)
    size = jnp.max(functools.reduce(jnp.maximum, [jnp.abs(v) for v in x]), axis=1, keepdims=True)
    shift = [jnp.where(size > FAR_OFF, v[:, 0:1], 0.0) for v in x]
    info_ref[2 * ROWS : 3 * ROWS, :] = jnp.zeros((ROWS, LANES), jnp.float32)
    for c in range(3):
        info_ref[2 * ROWS + c : 2 * ROWS + c + 1, :] = jnp.broadcast_to(shift[c], (1, LANES))
    apart = functools.reduce(jnp.maximum, [jnp.abs(v - o) for v, o in zip(x, shift)])
    set_grid(2.0 * jnp.max(apart, axis=1, keepdims=True), info_ref)
    build_left(x, select_ref, info_ref, target_ref, side_ref)


def cut_sources(source_ref, own_ref, select_ref, side_ref, work):
    pieces_ref, row_ref, target_ref, my_left_ref, my_info_ref = work[:5]
    halves = pieces_ref.shape[0]
    blocks = pieces_ref.shape[1] // PIECES
    stride = source_ref.shape[0] // blocks
    info_ref = info_of(side_ref)
    my_left_ref[...] = side_ref[0 : my_left_ref.shape[0], :].astype(jnp.bfloat16)
    my_info_ref[...] = info_ref[...]
    shift = [info_ref[2 * ROWS + c : 2 * ROWS + c + 1, :] for c in range(3)]
    x, f = [], []
    for h in range(halves):
        rows = [source_ref[pl.ds(c * halves + h, blocks, stride=stride), :] for c in range(6)]
        x.append([rows[c] - shift[c] for c in range(3)])
        f.append(rows[3:])
    size = functools.reduce(jnp.maximum, [jnp.abs(v) for part in x for v in part])
    size = jnp.max(jnp.max(size, axis=0, keepdims=True), axis=1, keepdims=True)
    beyond = jnp.max(size - 1024.0 * info_ref[0:1, 0:1]) > 0.0

    @pl.when(beyond)
    def _():
        set_grid(size, my_info_ref)
        build_left(own_rows(own_ref, target_ref.shape[1]), select_ref, my_info_ref, target_ref, my_left_ref)

    grid, per_grid = my_info_ref[0:1, :], my_info_ref[ROWS : ROWS + 1, :]
    for h in range(halves):
        norm, cross = norm_and_cross(x[h], [on_grid(v, grid, per_grid) for v in x[h]])
        n, g = three(norm), three(cross)
        c = three(-(x[h][0] * f[h][0] + x[h][1] * f[h][1] + x[h][2] * f[h][2]))
        one = jnp.ones_like(norm)
        sums = ((6, n[0]), (7, one), (14, n[1]), (15, n[2]), (22, g[0]), (23, one))
        sums += ((27, c[0]), (28, c[1]), (29, c[2]), (30, g[1]), (31, g[2]))
        for r, v in sums:
            pieces_ref[h, pl.ds(r, blocks, stride=PIECES), :] = v
    grid, per_grid = my_info_ref[0:6, :], my_info_ref[ROWS : ROWS + 6, :]
    shifts = my_info_ref[2 * ROWS : 2 * ROWS + 6, :]
    is_x = lax.broadcasted_iota(jnp.int32, (6, LANES), 0) < 3

    def cut(step, _):
        for i in range(CUT_UNROLL):
            block = step * CUT_UNROLL + i
            at = pl.multiple_of(block * PIECES, PIECES)
            for h in range(halves):
                tile = source_ref[pl.ds(block * stride + h, 6, stride=halves), :] - shifts
                coarse = on_grid(tile, grid, per_grid)
                rest = tile - coarse
                c1, r1, f1 = high(coarse), high(rest), high(tile)
                left_over = tile - f1
                f2 = high(left_over)
                pieces_ref[h, pl.ds(at, 6), :] = jnp.where(is_x, c1, f1)
                pieces_ref[h, pl.ds(at + 8, 6), :] = jnp.where(is_x, coarse - c1, f2)
                pieces_ref[h, pl.ds(at + 16, 6), :] = jnp.where(is_x, r1, left_over - f2)
                pieces_ref[h, pl.ds(at + 24, 3), :] = (rest - r1)[0:3]
                row_ref[h, pl.ds(pl.multiple_of(block * ROWS, ROWS), 6), :] = tile
        return 0

    lax.fori_loop(0, blocks // CUT_UNROLL, cut, 0)


def pair_sums(source_ref, own_ref, select_ref, side_ref, start_ref, sum_ref, work):
    pieces_ref, row_ref, _, my_left_ref, _, *product_refs = work
    nodes = sum_ref.shape[1]
    halves = pieces_ref.shape[0]
    blocks = pieces_ref.shape[1] // PIECES
    cut_sources(source_ref, own_ref, select_ref, side_ref, work)
    looped = blocks > CHUNK
    if looped:
        sum_ref[...] = jnp.zeros(sum_ref.shape, jnp.float32) if start_ref is None else start_ref[...]

    def multiply(first, into):
        for i, product_ref in enumerate(into):
            here = pl.ds(pl.multiple_of((first + i) * PIECES, PIECES), PIECES)
            rows = jnp.concatenate([pieces_ref[h, here, :] for h in range(halves)], axis=1).astype(jnp.bfloat16)
            p, q = rows[0:16], rows[16:32]
            right = jnp.concatenate([p, p, q, q, p, p, q, q], axis=0)
            for kind in range(2):
                product_ref[kind] = jnp.dot(
                    my_left_ref[kind * nodes : (kind + 1) * nodes, :], right, preferred_element_type=jnp.float32
                )

    def add(first, ready, fresh=False):
        tiles = []
        for i, product_ref in enumerate(ready):
            here = pl.ds(pl.multiple_of((first + i) * ROWS, ROWS), ROWS)
            for h in range(halves):
                lanes = slice(h * LANES, (h + 1) * LANES)
                rows = row_ref[h, here, :]
                spread = [jnp.broadcast_to(rows[r : r + 1, :], (ROWS, LANES)) for r in range(6)]
                tiles.append((product_ref, lanes, spread))
        for at in range(0, nodes, ROWS):
            here = slice(at, at + ROWS)
            if fresh and start_ref is None:
                totals = [jnp.zeros((ROWS, LANES), jnp.float32)] * 4
            else:
                totals = [(start_ref if fresh else sum_ref)[c, here, :] for c in range(4)]
            for product_ref, lanes, spread in tiles:
                r = lax.rsqrt(jnp.maximum(product_ref[0, here, lanes], 1.0))
                cube = r * (r * r)
                direct = r + cube
                along = product_ref[1, here, lanes] * cube
                for c in range(3):
                    totals[c] = totals[c] + (direct * spread[3 + c] - along * spread[c])
                totals[3] = totals[3] + along
            for c in range(4):
                sum_ref[c, here, :] = totals[c]

    def chunk(first, count):
        multiply(first, product_refs[0:2])
        for i in range(0, count, 4):
            multiply(first + i + 2, product_refs[2:4])
            add(first + i, product_refs[0:2], fresh=i == 0 and not looped)
            if i + 4 < count:
                multiply(first + i + 4, product_refs[0:2])
            add(first + i + 2, product_refs[2:4])

    if not looped:
        chunk(0, blocks)
    else:

        def step(i, _):
            chunk(i * CHUNK, CHUNK)
            return 0

        lax.fori_loop(0, blocks // CHUNK, step, 0)


def velocity_rows(own_ref, info_ref, sum_ref, scale):
    nodes = sum_ref.shape[1]
    sums = []
    for c in range(4):
        parts = [
            jnp.sum(sum_ref[c, at : at + LANES, :].T, axis=0, keepdims=True)
            for at in range(0, nodes, LANES)
        ]
        sums.append(jnp.concatenate(parts, axis=1))
    shift = [info_ref[2 * ROWS + c : 2 * ROWS + c + 1, 0:1] for c in range(3)]
    x = [v - o for v, o in zip(own_rows(own_ref, nodes), shift)]
    return [(sums[c] + x[c] * sums[3]) * (inverse_blob * scale) for c in range(3)]


def membrane(x, neighbours_ref, params_ref):
    nodes = x[0].shape[1]
    force = [[], [], []]
    for at in range(0, nodes, LANES):
        here = slice(at, at + LANES)
        points = [neighbours_ref[0:6, here], neighbours_ref[6:12, here]]
        edges = []
        for index in points:
            local = index & (LANES - 1)
            group = index // LANES
            component = []
            for c in range(3):
                found = jnp.zeros(index.shape, jnp.float32)
                for part in range(nodes // LANES):
                    source = jnp.broadcast_to(x[c][:, part * LANES : (part + 1) * LANES], index.shape)
                    taken = jnp.take_along_axis(source, local, axis=1, mode="promise_in_bounds")
                    found = jnp.where(group == part, taken, found)
                component.append(found - x[c][:, here])
            edges.append(component)
        near, far = edges
        length = params_ref[0:6, here]
        stretch = (near[0] * near[0] + near[1] * near[1] + near[2] * near[2]) / (length * length)
        tension = (stretch - 1.0) / (stretch + 1.0) / length
        for c in range(3):
            surface = jnp.sum(tension * near[c], axis=0, keepdims=True)
            bending = jnp.sum((2.0 / 9.0) * near[c] - (1.0 / 18.0) * far[c], axis=0, keepdims=True)
            bending = bending - params_ref[8 + c : 9 + c, here]
            force[c].append(params_ref[6:7, here] * surface + params_ref[7:8, here] * bending)
    return [jnp.concatenate(parts, axis=1) for parts in force]


def near_kernel(source_ref, own_ref, select_ref, side_ref, sum_ref, *work):
    pair_sums(source_ref, own_ref, select_ref, side_ref, None, sum_ref, work)


def advance(scale, sources, work, position_ref, sum_ref, neighbours_ref, params_ref, outs):
    out_ref, moved_ref, next_side_ref = outs
    own_ref, select_ref, side_ref = sources[1:4]
    velocity = velocity_rows(own_ref, info_of(side_ref), sum_ref, scale)
    nodes = velocity[0].shape[1]
    x = [position_ref[c : c + 1, :] + time_step * velocity[c] for c in range(3)]
    for c in range(3):
        moved_ref[c : c + 1, :] = x[c]
    scaled = [inverse_blob * v for v in x]
    force = membrane(x, neighbours_ref, params_ref)
    make_left(scaled, select_ref, next_side_ref, work[2])
    for chip in range(out_ref.shape[0]):
        for c in range(3):
            out_ref[chip, :, c * nodes : (c + 1) * nodes] = scaled[c]
            out_ref[chip, :, (3 + c) * nodes : (4 + c) * nodes] = force[c]


def first_kernel(scale, capacity, *refs):
    *sources, start_ref, position_ref, neighbours_ref, near_ref, far_ref = refs[:9]
    outs, (params_ref, sum_ref, *work) = refs[9:12], refs[12:]
    pick_slots(capacity, near_ref, far_ref, sources[3], params_ref)
    pair_sums(*sources, start_ref, sum_ref, work)
    advance(scale, sources, work, position_ref, sum_ref, neighbours_ref, params_ref, outs)


def step_kernel(scale, *refs):
    *sources, start_ref, position_ref, neighbours_ref, params_ref = refs[:8]
    outs, (sum_ref, *work) = refs[8:11], refs[11:]
    pair_sums(*sources, start_ref, sum_ref, work)
    advance(scale, sources, work, position_ref, sum_ref, neighbours_ref, params_ref, outs)


def last_kernel(scale, *refs):
    *sources, start_ref, velocity_ref, sum_ref = refs[:7]
    pair_sums(*sources, start_ref, sum_ref, refs[7:])
    velocity = velocity_rows(sources[1], info_of(sources[3]), sum_ref, scale)
    for c in range(3):
        velocity_ref[c : c + 1, :] = velocity[c]


def spread(copies):
    near = lax.all_to_all(copies, CHIPS, split_axis=0, concat_axis=0, tiled=True)
    far = lax.ppermute(near, "core", [(0, 1), (1, 0)])
    return near, far


def call(kernel, out_shape, operands, blocks, nodes, keeps_sums):
    pairs = blocks * nodes * nodes
    sums = [] if keeps_sums else [pltpu.VMEM((4, nodes, LANES), jnp.float32)]
    return pl.pallas_call(
        kernel,
        out_shape=out_shape,
        in_specs=[VMEM] * len(operands),
        out_specs=jax.tree.map(lambda _: VMEM, out_shape),
        scratch_shapes=sums
        + [
            pltpu.VMEM((nodes // LANES, blocks * PIECES, LANES), jnp.float32),
            pltpu.VMEM((nodes // LANES, blocks * ROWS, LANES), jnp.float32),
            pltpu.VMEM((PIECES, nodes), jnp.float32),
            pltpu.VMEM((2 * nodes, DEPTH), jnp.bfloat16),
            pltpu.VMEM((3 * ROWS, LANES), jnp.float32),
        ]
        + [pltpu.VMEM((2, nodes, nodes), jnp.float32)] * 4,
        compiler_params=GRANT,
        cost_estimate=pl.CostEstimate(flops=31 * pairs, bytes_accessed=8 * 3 * nodes * LANES, transcendentals=pairs),
    )(*operands)


def body(positions, forces, neighbours, patch_owner, rest_length, moduli, rest_bend):
    devices = lax.axis_size(AXES)
    nodes = positions.shape[1]
    chips = devices // 2
    scale = 1.0 / math.sqrt(devices * nodes)
    capacity = rest_length.shape[1] // devices
    copies_shape = jax.ShapeDtypeStruct((chips, 1, 6 * nodes), jnp.float32)
    params_shape = jax.ShapeDtypeStruct((PARAMS, nodes), jnp.float32)
    row_shape = jax.ShapeDtypeStruct((3, nodes), jnp.float32)
    step_shapes = (copies_shape, row_shape, side_shape(nodes))
    sums_shape = jax.ShapeDtypeStruct((4, nodes, LANES), jnp.float32)
    select = jnp.asarray(selectors())
    position = positions
    owner = patch_owner.reshape(1, nodes)
    copies, side = pack(
        positions, forces, rest_length, moduli, rest_bend, owner, select, devices
    )
    for step in range(STEPS + 1):
        near, far = spread(copies)
        shared = (copies, select, side)
        start = call(near_kernel, sums_shape, (near.reshape(-1, LANES),) + shared, chips, nodes, True)
        operands = (far.reshape(-1, LANES),) + shared + (start,)
        if step == 0:
            operands += (position, neighbours, near, far)
            kernel = functools.partial(first_kernel, scale, capacity)
            shapes = (*step_shapes, params_shape)
            copies, position, side, params = call(kernel, shapes, operands, chips, nodes, False)
        elif step < STEPS:
            operands += (position, neighbours, params)
            kernel = functools.partial(step_kernel, scale)
            copies, position, side = call(kernel, step_shapes, operands, chips, nodes, False)
    velocity = call(functools.partial(last_kernel, scale), row_shape, operands, chips, nodes, False)
    return position, velocity


def solution(mesh):
    tgt, src = mesh.devices.shape
    by_core = Mesh(mesh.devices.reshape(tgt, src // 2, 2), AXES)
    placed = (
        P(None, AXES),
        P(None, AXES),
        P(None, AXES),
        P(AXES, None),
        P(None, AXES),
        P(None, AXES),
        P(None, AXES),
    )
    return jax.shard_map(
        body,
        mesh=by_core,
        in_specs=placed,
        out_specs=(P(None, AXES), P(None, AXES)),
        check_vma=False,
    )
```

time: 92.4 us -> 83.1 us (0.90)
  Pallas kernels: 42.3 us -> 32.3 us
    pallas_call x5 -> x1, Pallas kernels: 20.9 us -> 2.34 us  [pack(): pl.pallas_call(pack_kernel, out_shape=(jax.ShapeDtypeStruct((devices // 2...]
    pallas_call x4 -> x8, Pallas kernels: 21.3 us -> 30 us  [call(): pl.pallas_call(kernel, out_shape=out_shape, in_specs=[VMEM] * len(operand...]
  transfers between devices with their start and end apart: 4 -> 4, of which waited for: 0 -> 0; matrix products, arithmetic and copies ran while one was open for 0% -> 0% of each run, Pallas kernels for 21% -> 16%
where the time goes in v10:
time: 83.1 us; the launch traced here: 82.6 us
  blocking collectives  41.5 us (50%)
  Pallas kernels  32.3 us (39%)
  starting transfers between devices  7.08 us (9%)
  local copies, waits for them, and re-layouts  0.98 us (1%)
    all_to_all x4, blocking collectives, spread(): lax.all_to_all(copies, CHIPS, split_axis=0, concat_axis=0, tiled=True)  41.5 us
    pallas_call x8, Pallas kernels, call(): pl.pallas_call(kernel, out_shape=out_shape, in_specs=[VMEM] * len(operand...  30 us
    ppermute x4, starting transfers between devices, spread(): far = lax.ppermute(near, 'core', [(0, 1), (1, 0)])  7.08 us
    pallas_call x1, Pallas kernels, pack(): pl.pallas_call(pack_kernel, out_shape=(jax.ShapeDtypeStruct((devices // 2...  2.34 us
  transfers between devices with their start and end apart: 4, of which 0 were waited for; matrix products, arithmetic and copies ran while one was open for 0% of the time, Pallas kernels for 16%

profile of v10, /device:TPU:1, one launch (start us, length us, event | category | flops | bytes accessed | tf_op | source)
XLA Modules:
  0.0 82.6 jit_solution(11799281403800424507)
XLA Ops:
  0.6 2.3 %shard_map.95 = (f32[16,1,2560]{2,1,0:T(1,128)}, f32[544,128]{1,0:T(8,128)}) custom-call(f32[3,256]{1,0:T(4,128)} %refs_5_.1, f32[3,256]{1,0:T(4,128)} %refs_1_.1, f32[6,1280]{1,0:T(8,128)} %refs_2_.5, f32[2,1280]{1,0:T(2,128)} %refs_3_.1, f32[3,1280]{1,0:T(4,128)} %refs_4_.1, s32[1,256]{1,0:T(1,128)} %bitcast.17, ...), custom_call_target="tpu_custom_call" | custom-call | tf_op jit(solution)/shard_map/pallas_call | solution.py:75
  3.0 0.0 copy-start
  3.0 0.0 copy-start.1
  3.0 14.1 %all_to_all.20.refs_7_ = f32[16,1,2560]{2,1,0:T(1,128)S(1)} all-to-all(f32[16,1,2560]{2,1,0:T(1,128)} %get-tuple-element.14.own_ref.refs_1_), channel_id=1, replica_groups=mesh['tgt'=4,'z'=4,'core'=2] {'tgt','z'}, dimensions={0} | all-to-all | bytes 327680 | tf_op jit(solution)/shard_map/all_to_all | solution.py:460
  17.1 2.9 %collective-permute-start = (f32[16,1,2560]{2,1,0:T(1,128)S(1)}, f32[16,1,2560]{2,1,0:T(1,128)S(1)}, u32[]{:S(2)}, u32[]{:S(2)}) collective-permute-start(f32[16,1,2560]{2,1,0:T(1,128)S(1)} %all_to_all.20.refs_7_), channel_id=1, source_target_pairs={{0,1},{1,0},{2,3},{3,2},{4,5},{5,4},{6,7},{7,6},{8,9},{9,8},{10,11... | collective-permute-start | bytes 491528 | tf_op jit(solution)/shard_map/ppermute | solution.py:461
  20.0 0.0 copy-done
  20.0 0.0 copy-done.1
  20.0 0.0 copy-start.3
  20.0 1.0 %copy-done.3 = f32[544,128]{1,0:T(8,128)S(1)} copy-done((f32[544,128]{1,0:T(8,128)S(1)}, f32[544,128]{1,0:T(8,128)}, u32[]{:S(2)}) %copy-start.3) | copy-done | bytes 278552
  20.9 0.0 copy-start.2
  20.9 0.0 copy-start.4
  20.9 0.0 copy-start.5
  20.9 3.2 %shard_map.96.refs_4_ = f32[4,256,128]{2,1,0:T(8,128)S(1)} custom-call(f32[320,128]{1,0:T(8,128)S(1)} %bitcast.9, f32[16,1,2560]{2,1,0:T(1,128)S(1)} %copy-done, f32[32,256]{1,0:T(8,128)S(1)} %copy-done.1, f32[544,128]{1,0:T(8,128)S(1)} %copy-done.3), custom_call_target="tpu_custom_call" | custom-call | flops 32505856 | bytes 786432 | tf_op jit(solution)/shard_map/pallas_call | solution.py:468
  24.1 0.0 collective-permute-done.refs_8_
  24.1 0.0 copy-done.2
  24.1 0.0 copy-done.4
  24.1 0.0 copy-done.5
  24.1 4.6 %shard_map.97 = (f32[16,1,1536]{2,1,0:T(1,128)S(1)}, f32[3,256]{1,0:T(4,128)S(1)}, f32[544,128]{1,0:T(8,128)S(1)}, f32[12,256]{1,0:T(8,128)S(1)}) custom-call(f32[320,128]{1,0:T(8,128)S(1)} %bitcast.13, f32[16,1,2560]{2,1,0:T(1,128)S(1)} %copy-done, f32[32,256]{1,0:T(8,128)S(1)} %copy-done.1, f32[544,128]{1,0:T(8,128)S(1)} %copy-done.4, ...), custom_call_target="tpu_custom_call" | custom-call | flops 32505856 | bytes 786432 | tf_op jit(solution)/shard_map/pallas_call | solution.py:468
  28.8 9.1 %all_to_all.21 = f32[16,1,1536]{2,1,0:T(1,128)S(1)} all-to-all(f32[16,1,1536]{2,1,0:T(1,128)S(1)} %get-tuple-element.16.own_ref.refs_1_), channel_id=1, replica_groups=mesh['tgt'=4,'z'=4,'core'=2] {'tgt','z'}, dimensions={0} | all-to-all | bytes 196608 | tf_op jit(solution)/shard_map/all_to_all | solution.py:460
  37.8 1.3 %collective-permute-start.1 = (f32[16,1,1536]{2,1,0:T(1,128)S(1)}, f32[16,1,1536]{2,1,0:T(1,128)S(1)}, u32[]{:S(2)}, u32[]{:S(2)}) collective-permute-start(f32[16,1,1536]{2,1,0:T(1,128)S(1)} %all_to_all.21), channel_id=1, source_target_pairs={{0,1},{1,0},{2,3},{3,2},{4,5},{5,4},{6,7},{7,6},{8,9},{9,8},{10,11... | collective-permute-start | bytes 294920 | tf_op jit(solution)/shard_map/ppermute | solution.py:461
  39.1 3.3 %shard_map.98.refs_4_ = f32[4,256,128]{2,1,0:T(8,128)S(1)} custom-call(f32[192,128]{1,0:T(8,128)S(1)} %bitcast.10, f32[16,1,1536]{2,1,0:T(1,128)S(1)} %get-tuple-element.16.own_ref.refs_1_, f32[32,256]{1,0:T(8,128)S(1)} %copy-done.1, f32[544,128]{1,0:T(8,128)S(1)} %get-tuple-element.17.side_ref.refs_3_), custom_call_target="tpu_custom_call" | custom-call | flops 32505856 | bytes 786432 | tf_op jit(solution)/shard_map/pallas_call | solution.py:468
  42.4 0.0 collective-permute-done.1
  42.4 4.2 %shard_map.99 = (f32[16,1,1536]{2,1,0:T(1,128)S(1)}, f32[3,256]{1,0:T(4,128)S(1)}, f32[544,128]{1,0:T(8,128)S(1)}) custom-call(f32[192,128]{1,0:T(8,128)S(1)} %bitcast.15, f32[16,1,1536]{2,1,0:T(1,128)S(1)} %get-tuple-element.16.own_ref.refs_1_, f32[32,256]{1,0:T(8,128)S(1)} %copy-done.1, f32[544,128]{1,0:T(8,128)S(1)} %get-tuple-element.17.side_ref.refs_3_, ...), custom_call_target="tpu_custom_call" | custom-call | flops 32505856 | bytes 786432 | tf_op jit(solution)/shard_map/pallas_call | solution.py:468
  46.7 9.2 %all_to_all.22 = f32[16,1,1536]{2,1,0:T(1,128)S(1)} all-to-all(f32[16,1,1536]{2,1,0:T(1,128)S(1)} %get-tuple-element.20.own_ref.refs_1_), channel_id=1, replica_groups=mesh['tgt'=4,'z'=4,'core'=2] {'tgt','z'}, dimensions={0} | all-to-all | bytes 196608 | tf_op jit(solution)/shard_map/all_to_all | solution.py:460
  55.9 1.7 %collective-permute-start.2 = (f32[16,1,1536]{2,1,0:T(1,128)S(1)}, f32[16,1,1536]{2,1,0:T(1,128)S(1)}, u32[]{:S(2)}, u32[]{:S(2)}) collective-permute-start(f32[16,1,1536]{2,1,0:T(1,128)S(1)} %all_to_all.22), channel_id=1, source_target_pairs={{0,1},{1,0},{2,3},{3,2},{4,5},{5,4},{6,7},{7,6},{8,9},{9,8},{10,11... | collective-permute-start | bytes 294920 | tf_op jit(solution)/shard_map/ppermute | solution.py:461
  57.5 3.3 %shard_map.100.refs_4_ = f32[4,256,128]{2,1,0:T(8,128)S(1)} custom-call(f32[192,128]{1,0:T(8,128)S(1)} %bitcast.11, f32[16,1,1536]{2,1,0:T(1,128)S(1)} %get-tuple-element.20.own_ref.refs_1_, f32[32,256]{1,0:T(8,128)S(1)} %copy-done.1, f32[544,128]{1,0:T(8,128)S(1)} %get-tuple-element.21.side_ref.refs_3_), custom_call_target="tpu_custom_call" | custom-call | flops 32505856 | bytes 786432 | tf_op jit(solution)/shard_map/pallas_call | solution.py:468
  60.8 0.0 collective-permute-done.2
  60.8 4.1 %shard_map.101 = (f32[16,1,1536]{2,1,0:T(1,128)S(1)}, f32[3,256]{1,0:T(4,128)}, f32[544,128]{1,0:T(8,128)S(1)}) custom-call(f32[192,128]{1,0:T(8,128)S(1)} %bitcast.14, f32[16,1,1536]{2,1,0:T(1,128)S(1)} %get-tuple-element.20.own_ref.refs_1_, f32[32,256]{1,0:T(8,128)S(1)} %copy-done.1, f32[544,128]{1,0:T(8,128)S(1)} %get-tuple-element.21.side_ref.refs_3_, ...), custom_call_target="tpu_custom_call" | custom-call | flops 32505856 | bytes 786432 | tf_op jit(solution)/shard_map/pallas_call | solution.py:468
  64.9 9.1 %all_to_all.23 = f32[16,1,1536]{2,1,0:T(1,128)S(1)} all-to-all(f32[16,1,1536]{2,1,0:T(1,128)S(1)} %get-tuple-element.24.own_ref.refs_1_), channel_id=1, replica_groups=mesh['tgt'=4,'z'=4,'core'=2] {'tgt','z'}, dimensions={0} | all-to-all | bytes 196608 | tf_op jit(solution)/shard_map/all_to_all | solution.py:460
  74.0 1.2 %collective-permute-start.3 = (f32[16,1,1536]{2,1,0:T(1,128)S(1)}, f32[16,1,1536]{2,1,0:T(1,128)S(1)}, u32[]{:S(2)}, u32[]{:S(2)}) collective-permute-start(f32[16,1,1536]{2,1,0:T(1,128)S(1)} %all_to_all.23), channel_id=1, source_target_pairs={{0,1},{1,0},{2,3},{3,2},{4,5},{5,4},{6,7},{7,6},{8,9},{9,8},{10,11... | collective-permute-start | bytes 294920 | tf_op jit(solution)/shard_map/ppermute | solution.py:461
  75.2 3.4 %shard_map.102.refs_4_ = f32[4,256,128]{2,1,0:T(8,128)S(1)} custom-call(f32[192,128]{1,0:T(8,128)S(1)} %bitcast.12, f32[16,1,1536]{2,1,0:T(1,128)S(1)} %get-tuple-element.24.own_ref.refs_1_, f32[32,256]{1,0:T(8,128)S(1)} %copy-done.1, f32[544,128]{1,0:T(8,128)S(1)} %get-tuple-element.25.side_ref.refs_3_), custom_call_target="tpu_custom_call" | custom-call | flops 32505856 | bytes 786432 | tf_op jit(solution)/shard_map/pallas_call | solution.py:468
  78.6 0.0 collective-permute-done.3
  78.6 4.0 %shard_map.103 = f32[3,256]{1,0:T(4,128)} custom-call(f32[192,128]{1,0:T(8,128)S(1)} %bitcast.16, f32[16,1,1536]{2,1,0:T(1,128)S(1)} %get-tuple-element.24.own_ref.refs_1_, f32[32,256]{1,0:T(8,128)S(1)} %copy-done.1, f32[544,128]{1,0:T(8,128)S(1)} %get-tuple-element.25.side_ref.refs_3_, f32[4,256,128]{2,1,0:T(8,128)S(1)} %shard_map.102.refs_4_), custom_call_target="tpu_custom_call" | custom-call | flops 32505856 | bytes 786432 | tf_op jit(solution)/shard_map/pallas_call | solution.py:468
Async XLA Ops:
  3.0 17.0 %copy-start = (f32[16,1,2560]{2,1,0:T(1,128)S(1)}, f32[16,1,2560]{2,1,0:T(1,128)}, u32[]{:S(2)}) copy-start(f32[16,1,2560]{2,1,0:T(1,128)} %get-tuple-element.14.own_ref.refs_1_) | copy-start | bytes 491524
  3.0 17.0 %copy-start.1 = (f32[32,256]{1,0:T(8,128)S(1)}, f32[32,256]{1,0:T(8,128)}, u32[]{:S(2)}) copy-start(f32[32,256]{1,0:T(8,128)} %constant.2.clone.refs_6_.select_ref.refs_2_) | copy-start | bytes 98308
  17.1 7.0 %collective-permute-start = (f32[16,1,2560]{2,1,0:T(1,128)S(1)}, f32[16,1,2560]{2,1,0:T(1,128)S(1)}, u32[]{:S(2)}, u32[]{:S(2)}) collective-permute-start(f32[16,1,2560]{2,1,0:T(1,128)S(1)} %all_to_all.20.refs_7_), channel_id=1, source_target_pairs={{0,1},{1,0},{2,3},{3,2},{4,5},{5,4},{6,7},{7,6},{8,9},{9,8},{10,11... | collective-permute-start | bytes 491528 | tf_op jit(solution)/shard_map/ppermute | solution.py:461
  20.0 1.0 %copy-start.3 = (f32[544,128]{1,0:T(8,128)S(1)}, f32[544,128]{1,0:T(8,128)}, u32[]{:S(2)}) copy-start(f32[544,128]{1,0:T(8,128)} %get-tuple-element.15.side_ref.refs_3_) | copy-start | bytes 835588
  20.9 3.2 %copy-start.2 = (f32[3,256]{1,0:T(4,128)S(1)}, f32[3,256]{1,0:T(4,128)}, u32[]{:S(2)}) copy-start(f32[3,256]{1,0:T(4,128)} %refs_5_.1) | copy-start | bytes 9220
  20.9 3.2 %copy-start.4 = (f32[544,128]{1,0:T(8,128)S(1)}, f32[544,128]{1,0:T(8,128)}, u32[]{:S(2)}) copy-start(f32[544,128]{1,0:T(8,128)} %get-tuple-element.15.side_ref.refs_3_) | copy-start | bytes 835588
  20.9 3.2 %copy-start.5 = (s32[12,256]{1,0:T(8,128)S(1)}, s32[12,256]{1,0:T(8,128)}, u32[]{:S(2)}) copy-start(s32[12,256]{1,0:T(8,128)} %refs_6_.6) | copy-start | bytes 36868
  37.8 4.6 %collective-permute-start.1 = (f32[16,1,1536]{2,1,0:T(1,128)S(1)}, f32[16,1,1536]{2,1,0:T(1,128)S(1)}, u32[]{:S(2)}, u32[]{:S(2)}) collective-permute-start(f32[16,1,1536]{2,1,0:T(1,128)S(1)} %all_to_all.21), channel_id=1, source_target_pairs={{0,1},{1,0},{2,3},{3,2},{4,5},{5,4},{6,7},{7,6},{8,9},{9,8},{10,11... | collective-permute-start | bytes 294920 | tf_op jit(solution)/shard_map/ppermute | solution.py:461
  55.9 4.9 %collective-permute-start.2 = (f32[16,1,1536]{2,1,0:T(1,128)S(1)}, f32[16,1,1536]{2,1,0:T(1,128)S(1)}, u32[]{:S(2)}, u32[]{:S(2)}) collective-permute-start(f32[16,1,1536]{2,1,0:T(1,128)S(1)} %all_to_all.22), channel_id=1, source_target_pairs={{0,1},{1,0},{2,3},{3,2},{4,5},{5,4},{6,7},{7,6},{8,9},{9,8},{10,11... | collective-permute-start | bytes 294920 | tf_op jit(solution)/shard_map/ppermute | solution.py:461
  74.0 4.6 %collective-permute-start.3 = (f32[16,1,1536]{2,1,0:T(1,128)S(1)}, f32[16,1,1536]{2,1,0:T(1,128)S(1)}, u32[]{:S(2)}, u32[]{:S(2)}) collective-permute-start(f32[16,1,1536]{2,1,0:T(1,128)S(1)} %all_to_all.23), channel_id=1, source_target_pairs={{0,1},{1,0},{2,3},{3,2},{4,5},{5,4},{6,7},{7,6},{8,9},{9,8},{10,11... | collective-permute-start | bytes 294920 | tf_op jit(solution)/shard_map/ppermute | solution.py:461

commit v11 on v10

--- a/solution.py
+++ b/solution.py
@@ -19,7 +19,7 @@
 CUT_UNROLL = 4
 CHUNK = 16
 LOADS = 7
-SIDE = 32
+SIDE = 128
 PICK_UNROLL = 4
 PARAMS = 12
 FOLD = 4
@@ -34,8 +34,8 @@
 
 
 def pack_kernel(*refs):
-    inputs, (out_ref, side_ref), copies = refs[:LOADS], refs[LOADS : LOADS + 2], refs[LOADS + 2 : -3]
-    slots_ref, target_ref, semaphores = refs[-3:]
+    inputs, (out_ref, side_ref), copies = refs[:LOADS], refs[LOADS : LOADS + 2], refs[LOADS + 2 : -4]
+    slots_ref, target_ref, info_ref, semaphores = refs[-4:]
     loads = [pltpu.make_async_copy(inputs[i], copies[i], semaphores.at[i]) for i in range(LOADS)]
     for load in loads:
         load.start()
@@ -46,7 +46,7 @@
     nodes = position_ref.shape[1]
     capacity = length_ref.shape[1] // (2 * chips)
     state = [inverse_blob * position_ref[c : c + 1, :] for c in range(3)]
-    make_left(state, select_ref, side_ref, target_ref)
+    make_left(state, select_ref[...].astype(jnp.bfloat16), side_ref, info_ref, target_ref)
     rank_nodes(owner_ref, side_ref)
     state += [force_ref[c : c + 1, :] for c in range(3)]
     slots_ref[0:6, :] = length_ref[...]
@@ -66,7 +66,7 @@
 
 
 def side_shape(nodes):
-    return jax.ShapeDtypeStruct((2 * nodes + SIDE, DEPTH), jnp.float32)
+    return jax.ShapeDtypeStruct((2 * nodes + SIDE, DEPTH), jnp.bfloat16)
 
 
 def pack(positions, forces, rest_length, moduli, rest_bend, owner, select, devices):
@@ -84,6 +84,7 @@
         + [
             pltpu.VMEM((PARAMS, rest_length.shape[1]), jnp.float32),
             pltpu.VMEM((PIECES, nodes), jnp.float32),
+            pltpu.VMEM((3 * ROWS, LANES), jnp.float32),
             pltpu.SemaphoreType.DMA((LOADS,)),
         ],
         compiler_params=pltpu.CompilerParams(vmem_limit_bytes=60 * 1024 * 1024),
@@ -98,18 +99,18 @@
         jnp.int32, (nodes, nodes), 1
     )
     rank = jnp.sum(jnp.where((across == across.T) & earlier, 1, 0), axis=0, keepdims=True)
-    first = side_ref.shape[0] - ROWS
-    for v in (rank, owner):
-        for at in range(0, nodes, LANES):
-            side_ref[first : first + 1, :] = v[:, at : at + LANES].astype(jnp.float32)
-            first += 1
+    rows = [v[:, at : at + LANES].astype(jnp.float32) for v in (rank, owner) for at in range(0, nodes, LANES)]
+    rows.append(jnp.zeros((16 - len(rows), LANES), jnp.float32))
+    first = side_ref.shape[0] - SIDE + 48
+    side_ref[first : first + 16, :] = jnp.concatenate(rows, axis=0).astype(jnp.bfloat16)
 
 
 def pick_slots(capacity, near_ref, far_ref, side_ref, params_ref):
     chips = near_ref.shape[0]
     nodes = params_ref.shape[1]
     parts = PARAMS // FOLD
-    named = side_ref[side_ref.shape[0] - ROWS :, :].astype(jnp.int32)
+    first = side_ref.shape[0] - SIDE + 48
+    named = side_ref[first : first + 16, :].astype(jnp.float32).astype(jnp.int32)
     parity = lax.axis_index("core")
     spots = range(0, nodes, LANES)
     part = jnp.minimum(lax.broadcasted_iota(jnp.int32, (ROWS, LANES), 0), parts - 1)
@@ -200,7 +201,7 @@
     info_ref[ROWS : 2 * ROWS, :] = jnp.broadcast_to(per_grid, (ROWS, LANES))
 
 
-def build_left(x, select_ref, info_ref, target_ref, left_ref):
+def build_left(x, select, info_ref, target_ref, left_ref):
     grid, per_grid = info_ref[0:1, 0:1], info_ref[ROWS : ROWS + 1, 0:1]
     shift = [info_ref[2 * ROWS + c : 2 * ROWS + c + 1, 0:1] for c in range(3)]
     x = [v - o for v, o in zip(x, shift)]
@@ -216,7 +217,7 @@
         target_ref[r : r + 1, :] = piece
     left = lax.dot_general(
         target_ref[...].astype(jnp.bfloat16),
-        select_ref[...].astype(jnp.bfloat16),
+        select,
         (((0,), (0,)), ((), ())),
         preferred_element_type=jnp.float32,
     ).astype(jnp.bfloat16)
@@ -225,13 +226,14 @@
     left_ref[nodes : 2 * nodes, :] = left[:, DEPTH : 2 * DEPTH].astype(left_ref.dtype)
 
 
-def info_of(side_ref):
-    rows = side_ref.shape[0] - SIDE
-    return side_ref.at[rows : rows + 3 * ROWS, :]
-
-
-def make_left(x, select_ref, side_ref, target_ref):
-    info_ref = info_of(side_ref)
+def select_of(side_ref):
+    first = side_ref.shape[0] - 2 * PIECES
+    return jnp.concatenate(
+        [side_ref[first : first + PIECES, :], side_ref[first + PIECES : first + 2 * PIECES, :]], axis=1
+    )
+
+
+def make_left(x, select, side_ref, info_ref, target_ref):
     size = jnp.max(functools.reduce(jnp.maximum, [jnp.abs(v) for v in x]), axis=1, keepdims=True)
     shift = [jnp.where(size > FAR_OFF, v[:, 0:1], 0.0) for v in x]
     info_ref[2 * ROWS : 3 * ROWS, :] = jnp.zeros((ROWS, LANES), jnp.float32)
@@ -239,18 +241,26 @@
         info_ref[2 * ROWS + c : 2 * ROWS + c + 1, :] = jnp.broadcast_to(shift[c], (1, LANES))
     apart = functools.reduce(jnp.maximum, [jnp.abs(v - o) for v, o in zip(x, shift)])
     set_grid(2.0 * jnp.max(apart, axis=1, keepdims=True), info_ref)
-    build_left(x, select_ref, info_ref, target_ref, side_ref)
-
-
-def cut_sources(source_ref, own_ref, select_ref, side_ref, work):
+    build_left(x, select, info_ref, target_ref, side_ref)
+    first = side_ref.shape[0] - SIDE
+    side_ref[first : first + 16, :] = info_ref[0 : 2 * ROWS, :].astype(jnp.bfloat16)
+    rows = [*three(info_ref[2 * ROWS : 3 * ROWS, :]), jnp.zeros((ROWS, LANES), jnp.float32)]
+    side_ref[first + 16 : first + 48, :] = jnp.concatenate(rows, axis=0).astype(jnp.bfloat16)
+    side_ref[first + 64 : first + 64 + PIECES, :] = select[:, 0:DEPTH]
+    side_ref[first + 64 + PIECES : first + SIDE, :] = select[:, DEPTH : 2 * DEPTH]
+
+
+def cut_sources(source_ref, own_ref, side_ref, work):
     pieces_ref, row_ref, target_ref, my_left_ref, my_info_ref = work[:5]
     halves = pieces_ref.shape[0]
     blocks = pieces_ref.shape[1] // PIECES
     stride = source_ref.shape[0] // blocks
-    info_ref = info_of(side_ref)
-    my_left_ref[...] = side_ref[0 : my_left_ref.shape[0], :].astype(jnp.bfloat16)
-    my_info_ref[...] = info_ref[...]
-    shift = [info_ref[2 * ROWS + c : 2 * ROWS + c + 1, :] for c in range(3)]
+    first = my_left_ref.shape[0]
+    my_left_ref[...] = side_ref[0:first, :]
+    my_info_ref[0 : 2 * ROWS, :] = side_ref[first : first + 16, :].astype(jnp.float32)
+    rows = side_ref[first + 16 : first + 48, :].astype(jnp.float32)
+    my_info_ref[2 * ROWS : 3 * ROWS, :] = (rows[0:8] + rows[8:16]) + rows[16:24]
+    shift = [my_info_ref[2 * ROWS + c : 2 * ROWS + c + 1, :] for c in range(3)]
     x, f = [], []
     for h in range(halves):
         rows = [source_ref[pl.ds(c * halves + h, blocks, stride=stride), :] for c in range(6)]
@@ -258,12 +268,12 @@
         f.append(rows[3:])
     size = functools.reduce(jnp.maximum, [jnp.abs(v) for part in x for v in part])
     size = jnp.max(jnp.max(size, axis=0, keepdims=True), axis=1, keepdims=True)
-    beyond = jnp.max(size - 1024.0 * info_ref[0:1, 0:1]) > 0.0
+    beyond = jnp.max(size - 1024.0 * my_info_ref[0:1, 0:1]) > 0.0
 
     @pl.when(beyond)
     def _():
         set_grid(size, my_info_ref)
-        build_left(own_rows(own_ref, target_ref.shape[1]), select_ref, my_info_ref, target_ref, my_left_ref)
+        build_left(own_rows(own_ref, target_ref.shape[1]), select_of(side_ref), my_info_ref, target_ref, my_left_ref)
 
     grid, per_grid = my_info_ref[0:1, :], my_info_ref[ROWS : ROWS + 1, :]
     for h in range(halves):
@@ -300,12 +310,12 @@
     lax.fori_loop(0, blocks // CUT_UNROLL, cut, 0)
 
 
-def pair_sums(source_ref, own_ref, select_ref, side_ref, start_ref, sum_ref, work):
+def pair_sums(source_ref, own_ref, side_ref, start_ref, sum_ref, work):
     pieces_ref, row_ref, _, my_left_ref, _, *product_refs = work
     nodes = sum_ref.shape[1]
     halves = pieces_ref.shape[0]
     blocks = pieces_ref.shape[1] // PIECES
-    cut_sources(source_ref, own_ref, select_ref, side_ref, work)
+    cut_sources(source_ref, own_ref, side_ref, work)
     looped = blocks > CHUNK
     if looped:
         sum_ref[...] = jnp.zeros(sum_ref.shape, jnp.float32) if start_ref is None else start_ref[...]
@@ -412,21 +422,21 @@
     return [jnp.concatenate(parts, axis=1) for parts in force]
 
 
-def near_kernel(source_ref, own_ref, select_ref, side_ref, sum_ref, *work):
-    pair_sums(source_ref, own_ref, select_ref, side_ref, None, sum_ref, work)
+def near_kernel(source_ref, own_ref, side_ref, sum_ref, *work):
+    pair_sums(source_ref, own_ref, side_ref, None, sum_ref, work)
 
 
 def advance(scale, sources, work, position_ref, sum_ref, neighbours_ref, params_ref, outs):
     out_ref, moved_ref, next_side_ref = outs
-    own_ref, select_ref, side_ref = sources[1:4]
-    velocity = velocity_rows(own_ref, info_of(side_ref), sum_ref, scale)
+    own_ref, side_ref = sources[1:3]
+    velocity = velocity_rows(own_ref, work[4], sum_ref, scale)
     nodes = velocity[0].shape[1]
     x = [position_ref[c : c + 1, :] + time_step * velocity[c] for c in range(3)]
     for c in range(3):
         moved_ref[c : c + 1, :] = x[c]
     scaled = [inverse_blob * v for v in x]
     force = membrane(x, neighbours_ref, params_ref)
-    make_left(scaled, select_ref, next_side_ref, work[2])
+    make_left(scaled, select_of(side_ref), next_side_ref, work[4], work[2])
     for chip in range(out_ref.shape[0]):
         for c in range(3):
             out_ref[chip, :, c * nodes : (c + 1) * nodes] = scaled[c]
@@ -434,24 +444,25 @@
 
 
 def first_kernel(scale, capacity, *refs):
-    *sources, start_ref, position_ref, neighbours_ref, near_ref, far_ref = refs[:9]
-    outs, (params_ref, sum_ref, *work) = refs[9:12], refs[12:]
-    pick_slots(capacity, near_ref, far_ref, sources[3], params_ref)
+    *sources, start_ref, position_ref, neighbours_ref, near_ref, far_ref = refs[:8]
+    outs, (params_ref, sum_ref, *work) = refs[8:11], refs[11:]
+    pick_slots(capacity, near_ref, far_ref, sources[2], params_ref)
     pair_sums(*sources, start_ref, sum_ref, work)
     advance(scale, sources, work, position_ref, sum_ref, neighbours_ref, params_ref, outs)
 
 
 def step_kernel(scale, *refs):
-    *sources, start_ref, position_ref, neighbours_ref, params_ref = refs[:8]
-    outs, (sum_ref, *work) = refs[8:11], refs[11:]
+    *sources, start_ref, position_ref, neighbours_ref, params_ref = refs[:7]
+    outs, (sum_ref, *work) = refs[7:10], refs[10:]
     pair_sums(*sources, start_ref, sum_ref, work)
     advance(scale, sources, work, position_ref, sum_ref, neighbours_ref, params_ref, outs)
 
 
 def last_kernel(scale, *refs):
-    *sources, start_ref, velocity_ref, sum_ref = refs[:7]
-    pair_sums(*sources, start_ref, sum_ref, refs[7:])
-    velocity = velocity_rows(sources[1], info_of(sources[3]), sum_ref, scale)
+    *sources, start_ref, velocity_ref, sum_ref = refs[:6]
+    work = refs[6:]
+    pair_sums(*sources, start_ref, sum_ref, work)
+    velocity = velocity_rows(sources[1], work[4], sum_ref, scale)
     for c in range(3):
         velocity_ref[c : c + 1, :] = velocity[c]
 
@@ -503,7 +514,7 @@
     )
     for step in range(STEPS + 1):
         near, far = spread(copies)
-        shared = (copies, select, side)
+        shared = (copies, side)
         start = call(near_kernel, sums_shape, (near.reshape(-1, LANES),) + shared, chips, nodes, True)
         operands = (far.reshape(-1, LANES),) + shared + (start,)
         if step == 0:

time: 83.1 us -> 82.2 us (0.989)
  local copies, waits for them, and re-layouts: 0.98 us -> 0.02 us
    unnamed x12 -> x8, local copies, waits for them, and re-layouts: 0.98 us -> 0.02 us
where the time goes in v11:
time: 82.2 us; the launch traced here: 81.5 us
  blocking collectives  41.4 us (50%)
  Pallas kernels  32.4 us (39%)
  starting transfers between devices  6.97 us (8%)
    all_to_all x4, blocking collectives, spread(): lax.all_to_all(copies, CHIPS, split_axis=0, concat_axis=0, tiled=True)  41.4 us
    pallas_call x8, Pallas kernels, call(): pl.pallas_call(kernel, out_shape=out_shape, in_specs=[VMEM] * len(operand...  30.1 us
    ppermute x4, starting transfers between devices, spread(): far = lax.ppermute(near, 'core', [(0, 1), (1, 0)])  6.97 us
    pallas_call x1, Pallas kernels, pack(): pl.pallas_call(pack_kernel, out_shape=(jax.ShapeDtypeStruct((devices // 2...  2.3 us
  transfers between devices with their start and end apart: 4, of which 0 were waited for; matrix products, arithmetic and copies ran while one was open for 0% of the time, Pallas kernels for 16%

profile of v11, /device:TPU:1, one launch (start us, length us, event | category | flops | bytes accessed | tf_op | source)
XLA Modules:
  0.0 81.5 jit_solution(5036440191794977915)
XLA Ops:
  0.6 2.3 %shard_map.95 = (f32[16,1,2560]{2,1,0:T(1,128)}, bf16[640,128]{1,0:T(8,128)(2,1)}) custom-call(f32[3,256]{1,0:T(4,128)} %refs_4_.3, f32[3,256]{1,0:T(4,128)} %refs_1_.1, f32[6,1280]{1,0:T(8,128)} %refs_2_.1, f32[2,1280]{1,0:T(2,128)} %refs_3_.1, f32[3,1280]{1,0:T(4,128)} %refs_4_.2, s32[1,256]{1,0:T(1,128)} %bitcast.17, f32[32,256]{1,0:T(8,128)} %constant.2.clone.refs_6_), custom_call_target="tpu_custom_call" | custom-call | tf_op jit(solution)/shard_map/pallas_call | solution.py:75
  2.9 0.0 copy-start
  2.9 0.0 copy-start.2
  3.0 14.1 %all_to_all.20.refs_6_ = f32[16,1,2560]{2,1,0:T(1,128)S(1)} all-to-all(f32[16,1,2560]{2,1,0:T(1,128)} %get-tuple-element.14.own_ref.refs_1_), channel_id=1, replica_groups=mesh['tgt'=4,'z'=4,'core'=2] {'tgt','z'}, dimensions={0} | all-to-all | bytes 327680 | tf_op jit(solution)/shard_map/all_to_all | solution.py:471
  17.1 2.9 %collective-permute-start = (f32[16,1,2560]{2,1,0:T(1,128)S(1)}, f32[16,1,2560]{2,1,0:T(1,128)S(1)}, u32[]{:S(2)}, u32[]{:S(2)}) collective-permute-start(f32[16,1,2560]{2,1,0:T(1,128)S(1)} %all_to_all.20.refs_6_), channel_id=1, source_target_pairs={{0,1},{1,0},{2,3},{3,2},{4,5},{5,4},{6,7},{7,6},{8,9},{9,8},{10,11... | collective-permute-start | bytes 491528 | tf_op jit(solution)/shard_map/ppermute | solution.py:472
  19.9 0.0 copy-done
  19.9 0.0 copy-done.2
  19.9 0.0 copy-start.1
  19.9 0.0 copy-start.3
  19.9 3.3 %shard_map.96.refs_3_ = f32[4,256,128]{2,1,0:T(8,128)S(1)} custom-call(f32[320,128]{1,0:T(8,128)S(1)} %bitcast.9, f32[16,1,2560]{2,1,0:T(1,128)S(1)} %copy-done, bf16[640,128]{1,0:T(8,128)(2,1)S(1)} %copy-done.2), custom_call_target="tpu_custom_call" | custom-call | flops 32505856 | bytes 786432 | tf_op jit(solution)/shard_map/pallas_call | solution.py:479
  23.2 0.0 collective-permute-done.refs_7_
  23.2 0.0 copy-done.1
  23.2 0.0 copy-done.3
  23.2 4.6 %shard_map.97 = (f32[16,1,1536]{2,1,0:T(1,128)S(1)}, f32[3,256]{1,0:T(4,128)S(1)}, bf16[640,128]{1,0:T(8,128)(2,1)S(1)}, f32[12,256]{1,0:T(8,128)S(1)}) custom-call(f32[320,128]{1,0:T(8,128)S(1)} %bitcast.13, f32[16,1,2560]{2,1,0:T(1,128)S(1)} %copy-done, bf16[640,128]{1,0:T(8,128)(2,1)S(1)} %copy-done.2, f32[4,256,128]{2,1,0:T(8,128)S(1)} %shard_map.96.refs_3_, ...), custom_call_target="tpu_custom_call" | custom-call | flops 32505856 | bytes 786432 | tf_op jit(solution)/shard_map/pallas_call | solution.py:479
  27.9 9.1 %all_to_all.21 = f32[16,1,1536]{2,1,0:T(1,128)S(1)} all-to-all(f32[16,1,1536]{2,1,0:T(1,128)S(1)} %get-tuple-element.16.own_ref.refs_1_), channel_id=1, replica_groups=mesh['tgt'=4,'z'=4,'core'=2] {'tgt','z'}, dimensions={0} | all-to-all | bytes 196608 | tf_op jit(solution)/shard_map/all_to_all | solution.py:471
  37.0 1.3 %collective-permute-start.1 = (f32[16,1,1536]{2,1,0:T(1,128)S(1)}, f32[16,1,1536]{2,1,0:T(1,128)S(1)}, u32[]{:S(2)}, u32[]{:S(2)}) collective-permute-start(f32[16,1,1536]{2,1,0:T(1,128)S(1)} %all_to_all.21), channel_id=1, source_target_pairs={{0,1},{1,0},{2,3},{3,2},{4,5},{5,4},{6,7},{7,6},{8,9},{9,8},{10,11... | collective-permute-start | bytes 294920 | tf_op jit(solution)/shard_map/ppermute | solution.py:472
  38.3 3.3 %shard_map.98.refs_3_ = f32[4,256,128]{2,1,0:T(8,128)S(1)} custom-call(f32[192,128]{1,0:T(8,128)S(1)} %bitcast.10, f32[16,1,1536]{2,1,0:T(1,128)S(1)} %get-tuple-element.16.own_ref.refs_1_, bf16[640,128]{1,0:T(8,128)(2,1)S(1)} %get-tuple-element.17.side_ref.refs_2_), custom_call_target="tpu_custom_call" | custom-call | flops 32505856 | bytes 786432 | tf_op jit(solution)/shard_map/pallas_call | solution.py:479
  41.5 0.0 collective-permute-done.1
  41.6 4.2 %shard_map.99 = (f32[16,1,1536]{2,1,0:T(1,128)S(1)}, f32[3,256]{1,0:T(4,128)S(1)}, bf16[640,128]{1,0:T(8,128)(2,1)S(1)}) custom-call(f32[192,128]{1,0:T(8,128)S(1)} %bitcast.15, f32[16,1,1536]{2,1,0:T(1,128)S(1)} %get-tuple-element.16.own_ref.refs_1_, bf16[640,128]{1,0:T(8,128)(2,1)S(1)} %get-tuple-element.17.side_ref.refs_2_, ...), custom_call_target="tpu_custom_call" | custom-call | flops 32505856 | bytes 786432 | tf_op jit(solution)/shard_map/pallas_call | solution.py:479
  45.8 9.1 %all_to_all.22 = f32[16,1,1536]{2,1,0:T(1,128)S(1)} all-to-all(f32[16,1,1536]{2,1,0:T(1,128)S(1)} %get-tuple-element.20.own_ref.refs_1_), channel_id=1, replica_groups=mesh['tgt'=4,'z'=4,'core'=2] {'tgt','z'}, dimensions={0} | all-to-all | bytes 196608 | tf_op jit(solution)/shard_map/all_to_all | solution.py:471
  54.9 1.5 %collective-permute-start.2 = (f32[16,1,1536]{2,1,0:T(1,128)S(1)}, f32[16,1,1536]{2,1,0:T(1,128)S(1)}, u32[]{:S(2)}, u32[]{:S(2)}) collective-permute-start(f32[16,1,1536]{2,1,0:T(1,128)S(1)} %all_to_all.22), channel_id=1, source_target_pairs={{0,1},{1,0},{2,3},{3,2},{4,5},{5,4},{6,7},{7,6},{8,9},{9,8},{10,11... | collective-permute-start | bytes 294920 | tf_op jit(solution)/shard_map/ppermute | solution.py:472
  56.4 3.3 %shard_map.100.refs_3_ = f32[4,256,128]{2,1,0:T(8,128)S(1)} custom-call(f32[192,128]{1,0:T(8,128)S(1)} %bitcast.11, f32[16,1,1536]{2,1,0:T(1,128)S(1)} %get-tuple-element.20.own_ref.refs_1_, bf16[640,128]{1,0:T(8,128)(2,1)S(1)} %get-tuple-element.21.side_ref.refs_2_), custom_call_target="tpu_custom_call" | custom-call | flops 32505856 | bytes 786432 | tf_op jit(solution)/shard_map/pallas_call | solution.py:479
  59.7 0.0 collective-permute-done.2
  59.7 4.1 %shard_map.101 = (f32[16,1,1536]{2,1,0:T(1,128)S(1)}, f32[3,256]{1,0:T(4,128)}, bf16[640,128]{1,0:T(8,128)(2,1)S(1)}) custom-call(f32[192,128]{1,0:T(8,128)S(1)} %bitcast.14, f32[16,1,1536]{2,1,0:T(1,128)S(1)} %get-tuple-element.20.own_ref.refs_1_, bf16[640,128]{1,0:T(8,128)(2,1)S(1)} %get-tuple-element.21.side_ref.refs_2_, ...), custom_call_target="tpu_custom_call" | custom-call | flops 32505856 | bytes 786432 | tf_op jit(solution)/shard_map/pallas_call | solution.py:479
  63.8 9.1 %all_to_all.23 = f32[16,1,1536]{2,1,0:T(1,128)S(1)} all-to-all(f32[16,1,1536]{2,1,0:T(1,128)S(1)} %get-tuple-element.24.own_ref.refs_1_), channel_id=1, replica_groups=mesh['tgt'=4,'z'=4,'core'=2] {'tgt','z'}, dimensions={0} | all-to-all | bytes 196608 | tf_op jit(solution)/shard_map/all_to_all | solution.py:471
  72.9 1.3 %collective-permute-start.3 = (f32[16,1,1536]{2,1,0:T(1,128)S(1)}, f32[16,1,1536]{2,1,0:T(1,128)S(1)}, u32[]{:S(2)}, u32[]{:S(2)}) collective-permute-start(f32[16,1,1536]{2,1,0:T(1,128)S(1)} %all_to_all.23), channel_id=1, source_target_pairs={{0,1},{1,0},{2,3},{3,2},{4,5},{5,4},{6,7},{7,6},{8,9},{9,8},{10,11... | collective-permute-start | bytes 294920 | tf_op jit(solution)/shard_map/ppermute | solution.py:472
  74.1 3.4 %shard_map.102.refs_3_ = f32[4,256,128]{2,1,0:T(8,128)S(1)} custom-call(f32[192,128]{1,0:T(8,128)S(1)} %bitcast.12, f32[16,1,1536]{2,1,0:T(1,128)S(1)} %get-tuple-element.24.own_ref.refs_1_, bf16[640,128]{1,0:T(8,128)(2,1)S(1)} %get-tuple-element.25.side_ref.refs_2_), custom_call_target="tpu_custom_call" | custom-call | flops 32505856 | bytes 786432 | tf_op jit(solution)/shard_map/pallas_call | solution.py:479
  77.5 0.0 collective-permute-done.3
  77.5 4.0 %shard_map.103 = f32[3,256]{1,0:T(4,128)} custom-call(f32[192,128]{1,0:T(8,128)S(1)} %bitcast.16, f32[16,1,1536]{2,1,0:T(1,128)S(1)} %get-tuple-element.24.own_ref.refs_1_, bf16[640,128]{1,0:T(8,128)(2,1)S(1)} %get-tuple-element.25.side_ref.refs_2_, f32[4,256,128]{2,1,0:T(8,128)S(1)} %shard_map.102.refs_3_), custom_call_target="tpu_custom_call" | custom-call | flops 32505856 | bytes 786432 | tf_op jit(solution)/shard_map/pallas_call | solution.py:479
Async XLA Ops:
  2.9 17.0 %copy-start = (f32[16,1,2560]{2,1,0:T(1,128)S(1)}, f32[16,1,2560]{2,1,0:T(1,128)}, u32[]{:S(2)}) copy-start(f32[16,1,2560]{2,1,0:T(1,128)} %get-tuple-element.14.own_ref.refs_1_) | copy-start | bytes 491524
  2.9 17.0 %copy-start.2 = (bf16[640,128]{1,0:T(8,128)(2,1)S(1)}, bf16[640,128]{1,0:T(8,128)(2,1)}, u32[]{:S(2)}) copy-start(bf16[640,128]{1,0:T(8,128)(2,1)} %get-tuple-element.15.side_ref.refs_2_) | copy-start | bytes 491524
  17.1 6.1 %collective-permute-start = (f32[16,1,2560]{2,1,0:T(1,128)S(1)}, f32[16,1,2560]{2,1,0:T(1,128)S(1)}, u32[]{:S(2)}, u32[]{:S(2)}) collective-permute-start(f32[16,1,2560]{2,1,0:T(1,128)S(1)} %all_to_all.20.refs_6_), channel_id=1, source_target_pairs={{0,1},{1,0},{2,3},{3,2},{4,5},{5,4},{6,7},{7,6},{8,9},{9,8},{10,11... | collective-permute-start | bytes 491528 | tf_op jit(solution)/shard_map/ppermute | solution.py:472
  19.9 3.3 %copy-start.1 = (f32[3,256]{1,0:T(4,128)S(1)}, f32[3,256]{1,0:T(4,128)}, u32[]{:S(2)}) copy-start(f32[3,256]{1,0:T(4,128)} %refs_4_.3) | copy-start | bytes 9220
  19.9 3.3 %copy-start.3 = (s32[12,256]{1,0:T(8,128)S(1)}, s32[12,256]{1,0:T(8,128)}, u32[]{:S(2)}) copy-start(s32[12,256]{1,0:T(8,128)} %refs_5_.5) | copy-start | bytes 36868
  37.0 4.6 %collective-permute-start.1 = (f32[16,1,1536]{2,1,0:T(1,128)S(1)}, f32[16,1,1536]{2,1,0:T(1,128)S(1)}, u32[]{:S(2)}, u32[]{:S(2)}) collective-permute-start(f32[16,1,1536]{2,1,0:T(1,128)S(1)} %all_to_all.21), channel_id=1, source_target_pairs={{0,1},{1,0},{2,3},{3,2},{4,5},{5,4},{6,7},{7,6},{8,9},{9,8},{10,11... | collective-permute-start | bytes 294920 | tf_op jit(solution)/shard_map/ppermute | solution.py:472
  54.9 4.8 %collective-permute-start.2 = (f32[16,1,1536]{2,1,0:T(1,128)S(1)}, f32[16,1,1536]{2,1,0:T(1,128)S(1)}, u32[]{:S(2)}, u32[]{:S(2)}) collective-permute-start(f32[16,1,1536]{2,1,0:T(1,128)S(1)} %all_to_all.22), channel_id=1, source_target_pairs={{0,1},{1,0},{2,3},{3,2},{4,5},{5,4},{6,7},{7,6},{8,9},{9,8},{10,11... | collective-permute-start | bytes 294920 | tf_op jit(solution)/shard_map/ppermute | solution.py:472
  72.9 4.7 %collective-permute-start.3 = (f32[16,1,1536]{2,1,0:T(1,128)S(1)}, f32[16,1,1536]{2,1,0:T(1,128)S(1)}, u32[]{:S(2)}, u32[]{:S(2)}) collective-permute-start(f32[16,1,1536]{2,1,0:T(1,128)S(1)} %all_to_all.23), channel_id=1, source_target_pairs={{0,1},{1,0},{2,3},{3,2},{4,5},{5,4},{6,7},{7,6},{8,9},{9,8},{10,11... | collective-permute-start | bytes 294920 | tf_op jit(solution)/shard_map/ppermute | solution.py:472
